TPU v7x, 32 devices: a whole 2x2x4 slice. The times are simulated.
32 devices in a mesh: dp: 16 (over z, y, core), mod: 2 (over x).
Axes of the slice: x: 2, y: 2, z: 4, core: 2. Of those that a mesh axis runs over, the one named last changes fastest.
Arguments:
- tokens: bfloat16 [32, 256, 1152], P(('dp', 'mod')), may hold values from -6 to 6
- cond: bfloat16 [256, 1152], P('dp'), may hold values from -6 to 6
- segment_ids: int32 [32, 256], P(('dp', 'mod')), may hold values from 0 to 7, never falling along the last dimension, each value on 1 to 64 neighbouring positions
- crop_slot: int32 [16, 16], P('dp'), may hold values from 0 to 15, each once within a row
- ada_weight: bfloat16 [1152, 6912], P(None, 'mod'), may hold values from -0.1875 to 0.1875
- ada_bias: bfloat16 [6, 1152], P('mod'), may hold values from -3 to 3
- attn_weight: bfloat16 [4608, 1152], P(('dp', 'mod'))
- fc_in: bfloat16 [4608, 1152], P(('dp', 'mod')), may hold values from -0.1875 to 0.1875
- fc_out: bfloat16 [4608, 1152], P(('dp', 'mod')), may hold values from -0.09375 to 0.09375
- biases: bfloat16 [9216], P(('dp', 'mod')), may hold values from -2 to 2
- out_grad: bfloat16 [32, 256, 1152], P(('dp', 'mod')), may hold values from -6 to 6
Outputs:
- out: bfloat16 [32, 256, 1152], P(('dp', 'mod'))
- tokens_grad: float32 [32, 256, 1152], P(('dp', 'mod'))
- cond_grad: float32 [256, 1152], P(('dp', 'mod'))
- ada_weight_grad: float32 [1152, 6912], P('dp', 'mod')
- ada_bias_grad: float32 [6, 1152], P('mod', 'dp')
- attn_weight_grad: float32 [4608, 1152], P(('dp', 'mod'))
- fc_in_grad: float32 [4608, 1152], P(('dp', 'mod'))
- fc_out_grad: float32 [4608, 1152], P(('dp', 'mod'))
- biases_grad: float32 [9216], P(('dp', 'mod'))
Inputs may be any that keep to these rules, and one draw needn't show every extreme that they name: `segment_ids`: within each sequence the crop numbers never fall, every crop has 1 to 64 tokens, and some crop has exactly 64. Each row holds every number once; crop c of sequence p * 2 + m uses conditioning row p * 2 * 8 + crop_slot[p, m * 8 + c].
All inputs are finite; a program needn't handle non-finite values.
Results may differ from a plain program's by a relative error of at most 0.015.
The roundings to bfloat16 on the way count: a program that leaves them out, or rounds other values in their place, can miss the bound.
Values may be sent and summed in bfloat16 or wider, within the bound.
No kernel may reach another device: no remote copies, remote signals or barrier semaphores. Data moves between devices by JAX's collectives and lax.ppermute only.
A program may use at most 384 MiB of HBM per device.

v0:
```python
import jax
import jax.numpy as jnp
from jax import lax
from jax.sharding import PartitionSpec as P

HEADS = 16


highest = lax.Precision.HIGHEST
norm_eps = 1e-06


def layer_norm(values):
    center = values - jnp.mean(values, axis=-1, keepdims=True)
    inverse = lax.rsqrt(jnp.mean(center * center, axis=-1, keepdims=True) + norm_eps)
    return (center * inverse, inverse)


def norm_back(grad_in, normed, inverse):
    centered = grad_in - jnp.mean(grad_in, axis=-1, keepdims=True)
    return (centered - normed * jnp.mean(grad_in * normed, axis=-1, keepdims=True)) * inverse


def times_rows(left, right):
    return lax.dot_general(
        left, right, (((1,), (1,)), ((), ())), preferred_element_type=jnp.float32
    )


def contract_rows(left, right):
    return lax.dot_general(
        left, right, (((0,), (0,)), ((), ())), preferred_element_type=jnp.float32
    )


def gelu_tanh(values):
    return jax.nn.gelu(values, approximate=True)


def owner_blocks(grad, dp_count, mod_count):
    return grad.reshape(
        (dp_count, mod_count, grad.shape[0] // (dp_count * mod_count)) + grad.shape[1:]
    )


def on_device(
    tokens,
    cond,
    segment_ids,
    crop_slot,
    ada_weight,
    ada_bias,
    attn_weight,
    fc_in,
    fc_out,
    biases,
    out_grad,
):
    model_width = tokens.shape[2]
    tok_len = tokens.shape[1]
    head_count = HEADS
    head_dim = model_width // head_count
    score_scale = head_dim ** (-0.5)
    dp_count = lax.axis_size("dp")
    mod_count = lax.axis_size("mod")
    crop_count = crop_slot.shape[1] // mod_count
    mod_rank = lax.axis_index("mod")
    silu_cond = jax.nn.silu(cond.astype(jnp.float32)).astype(jnp.bfloat16)
    mod_part = jnp.dot(
        silu_cond, ada_weight, preferred_element_type=jnp.float32
    ) + ada_bias.reshape(-1).astype(jnp.float32)
    modulation = lax.all_gather(mod_part.astype(jnp.bfloat16), "mod", axis=1, tiled=True)
    seg_ids = segment_ids[0]
    slots = lax.dynamic_slice_in_dim(crop_slot[0], mod_rank * crop_count, crop_count)
    crop_onehot = seg_ids[:, None] == jnp.arange(crop_count, dtype=jnp.int32)[None, :]
    token_slot = jnp.sum(jnp.where(crop_onehot, slots[None, :], 0), axis=1)
    slot_pick = token_slot[:, None] == jnp.arange(cond.shape[0], dtype=jnp.int32)[None, :]
    token_mod = jnp.dot(
        slot_pick.astype(jnp.bfloat16), modulation, preferred_element_type=jnp.float32
    )
    shift_a, scale_a, gate_a, shift_m, scale_m, gate_m = jnp.split(token_mod, 6, axis=1)
    attn_w, fcin_w, fcout_w, bias_all = (
        lax.all_gather(attn_weight, ("dp", "mod"), axis=0, tiled=True),
        lax.all_gather(fc_in, ("dp", "mod"), axis=0, tiled=True),
        lax.all_gather(fc_out, ("dp", "mod"), axis=0, tiled=True),
        lax.all_gather(biases, ("dp", "mod"), axis=0, tiled=True),
    )
    bias_all = bias_all.astype(jnp.float32)
    bias_query = bias_all[:model_width]
    bias_value = bias_all[model_width : 2 * model_width]
    bias_proj = bias_all[2 * model_width : 3 * model_width]
    bias_out = bias_all[3 * model_width : 4 * model_width]
    bias_in = bias_all[4 * model_width :]
    qkv_weight = attn_w[: 3 * model_width]
    proj_weight = attn_w[3 * model_width :]
    resid = tokens[0].astype(jnp.float32)
    normed_a, inverse_a = layer_norm(resid)
    attn_in = (normed_a * (1.0 + scale_a) + shift_a).astype(jnp.bfloat16)
    qkv_bias = jnp.concatenate([bias_query, jnp.zeros_like(bias_query), bias_value])
    qkv = (times_rows(attn_in, qkv_weight) + qkv_bias).astype(jnp.bfloat16)
    query = qkv[:, :model_width].reshape(tok_len, head_count, head_dim)
    key_part = qkv[:, model_width : 2 * model_width].reshape(tok_len, head_count, head_dim)
    value = qkv[:, 2 * model_width :].reshape(tok_len, head_count, head_dim)
    same_crop = seg_ids[:, None] == seg_ids[None, :]

    def scores_of(left, right):
        raw = (
            jnp.einsum("qhd,khd->hqk", left, right, preferred_element_type=jnp.float32)
            * score_scale
        )
        return jnp.where(same_crop[None], raw, -1e30)

    scores = scores_of(query, key_part)
    row_max = jnp.max(scores, axis=-1, keepdims=True)
    log_total = row_max + jnp.log(jnp.sum(jnp.exp(scores - row_max), axis=-1, keepdims=True))
    probs = jnp.exp(scores - log_total).astype(jnp.bfloat16)
    context = jnp.einsum("hqk,khd->qhd", probs, value, preferred_element_type=jnp.float32)
    context = context.reshape(tok_len, model_width).astype(jnp.bfloat16)
    attn_out = times_rows(context, proj_weight) + bias_proj
    mid = resid + gate_a * attn_out
    normed_m, inverse_m = layer_norm(mid)
    mlp_in = (normed_m * (1.0 + scale_m) + shift_m).astype(jnp.bfloat16)
    hidden = times_rows(mlp_in, fcin_w) + bias_in
    act_full, gelu_back = jax.vjp(gelu_tanh, hidden)
    act = act_full.astype(jnp.bfloat16)
    mlp_out = jnp.dot(act, fcout_w, preferred_element_type=jnp.float32) + bias_out
    result = (mid + gate_m * mlp_out).astype(jnp.bfloat16)
    grad_out = out_grad[0].astype(jnp.float32)
    grad_gate_m = grad_out * mlp_out
    grad_mlp = (gate_m * grad_out).astype(jnp.bfloat16)
    grad_act = times_rows(grad_mlp, fcout_w)
    grad_fcout = contract_rows(act, grad_mlp)
    grad_hidden = gelu_back(grad_act)[0].astype(jnp.bfloat16)
    grad_fcin = contract_rows(grad_hidden, mlp_in)
    grad_mlp_in = jnp.dot(grad_hidden, fcin_w, preferred_element_type=jnp.float32)
    grad_scale_m = grad_mlp_in * normed_m
    grad_mid = grad_out + norm_back(grad_mlp_in * (1.0 + scale_m), normed_m, inverse_m)
    grad_gate_a = grad_mid * attn_out
    grad_attn = (gate_a * grad_mid).astype(jnp.bfloat16)
    grad_proj = contract_rows(grad_attn, context)
    grad_context = jnp.dot(grad_attn, proj_weight, preferred_element_type=jnp.float32)
    grad_context = grad_context.astype(jnp.bfloat16).reshape(tok_len, head_count, head_dim)
    scores_again = scores_of(query, key_part)
    probs_full = jnp.exp(scores_again - log_total)
    probs_low = probs_full.astype(jnp.bfloat16)
    grad_probs = jnp.einsum("qhd,khd->hqk", grad_context, value, preferred_element_type=jnp.float32)
    grad_scores = probs_full * (
        grad_probs - jnp.sum(grad_probs * probs_full, axis=-1, keepdims=True)
    )
    grad_scores = grad_scores.astype(jnp.bfloat16)
    grad_query = (
        jnp.einsum("hqk,khd->qhd", grad_scores, key_part, preferred_element_type=jnp.float32)
        * score_scale
    )
    grad_keys = (
        jnp.einsum("hqk,qhd->khd", grad_scores, query, preferred_element_type=jnp.float32)
        * score_scale
    )
    grad_value = jnp.einsum(
        "hqk,qhd->khd", probs_low, grad_context, preferred_element_type=jnp.float32
    )
    grad_qkv = jnp.concatenate(
        [
            grad_query.reshape(tok_len, model_width),
            grad_keys.reshape(tok_len, model_width),
            grad_value.reshape(tok_len, model_width),
        ],
        axis=1,
    ).astype(jnp.bfloat16)
    grad_qkv_w = contract_rows(grad_qkv, attn_in)
    grad_attn_in = jnp.dot(grad_qkv, qkv_weight, preferred_element_type=jnp.float32)
    grad_scale_a = grad_attn_in * normed_a
    grad_tokens = grad_mid + norm_back(grad_attn_in * (1.0 + scale_a), normed_a, inverse_a)
    grad_qkv_wide = grad_qkv.astype(jnp.float32)
    grad_bias = jnp.concatenate(
        [
            jnp.sum(grad_qkv_wide[:, :model_width], axis=0),
            jnp.sum(grad_qkv_wide[:, 2 * model_width :], axis=0),
            jnp.sum(grad_attn.astype(jnp.float32), axis=0),
            jnp.sum(grad_mlp.astype(jnp.float32), axis=0),
            jnp.sum(grad_hidden.astype(jnp.float32), axis=0),
        ]
    )
    grad_attn_w = jnp.concatenate([grad_qkv_w, grad_proj], axis=0)
    grad_token_mod = jnp.concatenate(
        [grad_attn_in, grad_scale_a, grad_gate_a, grad_mlp_in, grad_scale_m, grad_gate_m], axis=1
    )
    grad_pair = jnp.dot(slot_pick.astype(jnp.float32).T, grad_token_mod, precision=highest)
    grad_mod = lax.psum_scatter(
        grad_pair.astype(jnp.bfloat16), "mod", scatter_dimension=1, tiled=True
    )
    grad_ada_w = contract_rows(silu_cond, grad_mod)
    grad_ada_b = jnp.sum(grad_mod.astype(jnp.float32), axis=0).reshape(
        ada_bias.shape[0], model_width
    )
    ada_w_sum, ada_b_sum = (
        lax.psum_scatter(grad_ada_w, "dp", scatter_dimension=0, tiled=True),
        lax.psum_scatter(grad_ada_b, "dp", scatter_dimension=1, tiled=True),
    )
    grad_silu = times_rows(grad_mod, ada_weight)
    grad_silu = lax.psum_scatter(
        grad_silu.astype(jnp.bfloat16), "mod", scatter_dimension=0, tiled=True
    ).astype(jnp.float32)
    own_cond = lax.dynamic_slice_in_dim(cond, mod_rank * crop_count, crop_count, 0).astype(
        jnp.float32
    )
    silu_out, silu_back = jax.vjp(jax.nn.silu, own_cond)
    grad_cond = silu_back(grad_silu)[0]
    attn_pair, fcin_pair, fcout_pair, bias_pair = (
        lax.all_to_all(
            owner_blocks(grad_attn_w, dp_count, mod_count).astype(jnp.bfloat16),
            "mod",
            split_axis=1,
            concat_axis=1,
            tiled=True,
        ).astype(jnp.float32),
        lax.all_to_all(
            owner_blocks(grad_fcin, dp_count, mod_count).astype(jnp.bfloat16),
            "mod",
            split_axis=1,
            concat_axis=1,
            tiled=True,
        ).astype(jnp.float32),
        lax.all_to_all(
            owner_blocks(grad_fcout, dp_count, mod_count).astype(jnp.bfloat16),
            "mod",
            split_axis=1,
            concat_axis=1,
            tiled=True,
        ).astype(jnp.float32),
        lax.all_to_all(
            owner_blocks(grad_bias, dp_count, mod_count).astype(jnp.bfloat16),
            "mod",
            split_axis=1,
            concat_axis=1,
            tiled=True,
        ).astype(jnp.float32),
    )
    attn_own, fcin_own, fcout_own, bias_own = (
        lax.all_to_all(
            jnp.sum(attn_pair, axis=1).astype(jnp.bfloat16),
            "dp",
            split_axis=0,
            concat_axis=0,
            tiled=True,
        ).astype(jnp.float32),
        lax.all_to_all(
            jnp.sum(fcin_pair, axis=1).astype(jnp.bfloat16),
            "dp",
            split_axis=0,
            concat_axis=0,
            tiled=True,
        ).astype(jnp.float32),
        lax.all_to_all(
            jnp.sum(fcout_pair, axis=1).astype(jnp.bfloat16),
            "dp",
            split_axis=0,
            concat_axis=0,
            tiled=True,
        ).astype(jnp.float32),
        lax.all_to_all(
            jnp.sum(bias_pair, axis=1).astype(jnp.bfloat16),
            "dp",
            split_axis=0,
            concat_axis=0,
            tiled=True,
        ).astype(jnp.float32),
    )
    attn_sum = jnp.sum(attn_own, axis=0)
    fcin_sum = jnp.sum(fcin_own, axis=0)
    fcout_sum = jnp.sum(fcout_own, axis=0)
    bias_sum = jnp.sum(bias_own, axis=0)
    return (
        result[None],
        grad_tokens[None],
        grad_cond,
        ada_w_sum,
        ada_b_sum,
        attn_sum,
        fcin_sum,
        fcout_sum,
        bias_sum,
    )


def solution(mesh):
    placed = (
        P(("dp", "mod"), None, None),
        P("dp", None),
        P(("dp", "mod"), None),
        P("dp", None),
        P(None, "mod"),
        P("mod", None),
        P(("dp", "mod"), None),
        P(("dp", "mod"), None),
        P(("dp", "mod"), None),
        P(("dp", "mod")),
        P(("dp", "mod"), None, None),
    )
    return jax.shard_map(
        on_device,
        mesh=mesh,
        in_specs=placed,
        out_specs=(
            P(("dp", "mod"), None, None),
            P(("dp", "mod"), None, None),
            P(("dp", "mod"), None),
            P("dp", "mod"),
            P("mod", "dp"),
            P(("dp", "mod"), None),
            P(("dp", "mod"), None),
            P(("dp", "mod"), None),
            P(("dp", "mod")),
        ),
        check_vma=False,
    )
```

profile of v0, /device:TPU:0, one launch (start us, length us, event | category | flops | bytes accessed | tf_op | source)
XLA Modules:
  0.0 1265.4 jit_solution(9717465726274575383)
XLA Ops:
  11.0 43.4 %all-reduce = bf16[9216]{0:T(1024)(128)(2,1)S(1)} all-reduce(bf16[9216]{0:T(1024)(128)(2,1)S(1)} %dynamic-update-slice), channel_id=1, replica_groups=mesh['dp'=16,'mod'=2] {'dp','mod'}, use_global_device_ids=true, to_apply=%add | all-reduce | flops 9216 | bytes 36864
  55.1 4.5 fusion.17
  59.6 5.6 all_gather.15
  69.0 1.9 copy-done.4
  71.3 30.6 %all-gather.4.cloned.1.call-done = bf16[4608,1152]{1,0:T(8,128)(2,1)} async-done(((bf16[144,1152]{1,0:T(8,128)(2,1)}), bf16[4608,1152]{1,0:T(8,128)(2,1)}) %all-gather.4.cloned.1.call-update) | async-done | bytes 10616848 | tf_op jit(solution)/shard_map/all_gather | solution.py:83
  101.8 5.9 fusion.7
  110.5 1.1 convolution_convert_fusion.8
  112.6 1.2 slice-done.1
  113.8 3.9 fusion.78
  118.3 72.2 %all-gather.8.cloned.1.call-done = bf16[4608,1152]{1,0:T(8,128)(2,1)} async-done(((bf16[144,1152]{1,0:T(8,128)(2,1)}), bf16[4608,1152]{1,0:T(8,128)(2,1)}) %all-gather.8.cloned.1.call-update) | async-done | bytes 10616848 | tf_op jit(solution)/shard_map/all_gather | solution.py:85
  190.6 12.5 fusion.82
  203.1 76.3 %all-gather.6.cloned.1.call-done = bf16[4608,1152]{1,0:T(8,128)(2,1)} async-done(((bf16[144,1152]{1,0:T(8,128)(2,1)}), bf16[4608,1152]{1,0:T(8,128)(2,1)}) %all-gather.6.cloned.1.call-update) | async-done | bytes 10616848 | tf_op jit(solution)/shard_map/all_gather | solution.py:84
  279.3 9.8 fusion.73
  289.2 8.6 fusion.83
  297.9 3.5 convolution_add_fusion.3
  301.4 1.3 fusion.71
  302.9 1.6 fusion.77
  305.4 3.6 convolution_convert_fusion.5
  309.0 2.1 copy.68
  311.1 4.2 multiply_reduce_fusion
  315.3 1.2 multiply_convert_fusion.1
  320.2 5.9 convolution_convert_fusion.2
  327.1 1.5 dynamic-update-slice.1
  328.6 1.4 dynamic-update-slice.2
  330.0 1.4 dynamic-update-slice.3
  331.4 1.4 dynamic-update-slice.4
  332.8 1.4 dynamic-update-slice.5
  334.2 1.4 convert_element_type.189
  335.6 1.4 copy.75
  337.0 3.8 all-to-all-start.6
  340.8 3.6 convolution_convert_fusion.4
  347.4 4.1 all-to-all-start.7
  351.6 10.6 pad_maximum_fusion
  362.2 4.7 copy.72
  366.9 7.9 all-to-all-start
  374.8 5.0 convolution_convert_fusion.1
  379.8 4.7 copy.73
  384.5 107.3 %all-to-all-done = bf16[16,2,144,1152]{3,2,0,1:T(8,128)(2,1)} async-done(((bf16[16,2,144,1152]{3,2,0,1:T(8,128)(2,1)}), bf16[16,2,144,1152]{3,2,0,1:T(8,128)(2,1)}, u32[]{:S(2)}, u32[]{:S(2)}) %all-to-all-start) | async-done | bytes 10616864 | tf_op jit(solution)/shard_map/all_to_all | solution.py:210
  491.8 8.1 all-to-all-start.2
  499.8 6.5 convolution_convert_fusion
  506.4 4.7 copy.74
  511.1 104.9 %all-to-all-done.2 = bf16[16,2,144,1152]{3,2,0,1:T(8,128)(2,1)} async-done(((bf16[16,2,144,1152]{3,2,0,1:T(8,128)(2,1)}), bf16[16,2,144,1152]{3,2,0,1:T(8,128)(2,1)}, u32[]{:S(2)}, u32[]{:S(2)}) %all-to-all-start.2) | async-done | bytes 10616864 | tf_op jit(solution)/shard_map/all_to_all | solution.py:217
  616.0 7.8 all-to-all-start.4
  623.8 9.8 reduce_sum.249
  633.6 105.5 %all-to-all-done.4 = bf16[16,2,144,1152]{3,2,0,1:T(8,128)(2,1)} async-done(((bf16[16,2,144,1152]{3,2,0,1:T(8,128)(2,1)}), bf16[16,2,144,1152]{3,2,0,1:T(8,128)(2,1)}, u32[]{:S(2)}, u32[]{:S(2)}) %all-to-all-start.4) | async-done | bytes 10616864 | tf_op jit(solution)/shard_map/all_to_all | solution.py:224
  739.0 5.4 all-to-all-start.1
  744.7 6.9 fusion.72
  751.6 2.9 fusion.39
  756.2 2.4 convolution_convert_fusion.3
  758.6 1.6 copy.81
  760.3 28.7 %reduce-scatter.8.cloned.1.call-done = bf16[3456,16]{1,0:T(8,128)(2,1)} async-done(((bf16[6912,16]{1,0:T(8,128)(2,1)}), bf16[3456,16]{1,0:T(8,128)(2,1)}) %reduce-scatter.8.cloned.1.call-update) | async-done | bytes 110608
  789.0 9.0 fusion.61
  798.0 10.3 reduce_sum.251
  808.4 41.2 %all-to-all-done.1 = bf16[16,144,1152]{2,1,0:T(8,128)(2,1)} async-done(((bf16[16,144,1152]{2,1,0:T(8,128)(2,1)}), bf16[16,144,1152]{2,1,0:T(8,128)(2,1)}, u32[]{:S(2)}, u32[]{:S(2)}) %all-to-all-start.1) | async-done | bytes 5308448 | tf_op jit(solution)/shard_map/all_to_all | solution.py:240
  849.5 68.9 %all-to-all-start.3 = ((bf16[16,144,1152]{2,1,0:T(8,128)(2,1)}), bf16[16,144,1152]{2,1,0:T(8,128)(2,1)}, u32[]{:S(2)}, u32[]{:S(2)}) async-start(bf16[16,144,1152]{2,1,0:T(8,128)(2,1)} %reduce_sum.251), calls=%async_computation.3 | async-start | bytes 10616832 | tf_op jit(solution)/shard_map/all_to_all | solution.py:247
  918.5 9.9 reduce_sum.253
  928.4 111.7 %all-to-all-done.3 = bf16[16,144,1152]{2,1,0:T(8,128)(2,1)} async-done(((bf16[16,144,1152]{2,1,0:T(8,128)(2,1)}), bf16[16,144,1152]{2,1,0:T(8,128)(2,1)}, u32[]{:S(2)}, u32[]{:S(2)}) %all-to-all-start.3) | async-done | bytes 5308448 | tf_op jit(solution)/shard_map/all_to_all | solution.py:247
  1040.1 36.1 %all-to-all-start.5 = ((bf16[16,144,1152]{2,1,0:T(8,128)(2,1)}), bf16[16,144,1152]{2,1,0:T(8,128)(2,1)}, u32[]{:S(2)}, u32[]{:S(2)}) async-start(bf16[16,144,1152]{2,1,0:T(8,128)(2,1)} %reduce_sum.253), calls=%async_computation.5 | async-start | bytes 10616832 | tf_op jit(solution)/shard_map/all_to_all | solution.py:254
  1080.5 151.1 %all-reduce.3 = f32[3,1152]{1,0:T(4,128)S(1)} all-reduce(f32[3,1152]{1,0:T(4,128)S(1)} %reshape.163), channel_id=5, replica_groups=mesh['dp'=16,'mod'=2] {'dp'}, use_global_device_ids=true, to_apply=%region_16.17.clone | all-reduce | flops 3456 | bytes 27648
  1231.6 5.5 convolution_convert_fusion.6
  1237.1 7.6 all-reduce.1
  1246.0 4.2 convert_reduce_fusion.2
  1250.2 4.2 convert_reduce_fusion.1
  1254.4 4.2 convert_reduce_fusion
  (179 shorter events, 27.4 us)
Async XLA Ops:
  7.2 58.1 %copy-start = (s32[1,16]{1,0:T(1,128)S(1)}, s32[1,16]{1,0:T(1,128)}, u32[]{:S(2)}) copy-start(s32[1,16]{1,0:T(1,128)} %param.14) | copy-start | bytes 196
  7.2 94.6 %all-gather.4.cloned.1.call-start = ((), (), s32[]{:S(2)}) async-start(), calls=%async_computation.10 | async-start | bytes 10948608 | tf_op jit(solution)/shard_map/all_gather | solution.py:83
  7.9 182.7 %all-gather.8.cloned.1.call-start = ((), (), s32[]{:S(2)}) async-start(), calls=%async_computation.12 | async-start | bytes 10948608 | tf_op jit(solution)/shard_map/all_gather | solution.py:85
  8.7 270.7 %all-gather.6.cloned.1.call-start = ((), (), s32[]{:S(2)}) async-start(), calls=%async_computation.11 | async-start | bytes 10948608 | tf_op jit(solution)/shard_map/all_gather | solution.py:84
  55.1 10.8 copy-start.41
  55.1 10.9 copy-start.5
  66.0 1.8 copy-start.37
  66.0 1.8 copy-start.10
  66.2 2.8 copy-start.39
  66.5 2.4 copy-start.42
  66.7 43.8 %copy-start.27 = (pred[256,256]{0,1:T(8,128)(4,1)}, pred[256,256]{0,1:T(8,128)(4,1)S(1)}, u32[]{:S(2)}) copy-start(pred[256,256]{0,1:T(8,128)(4,1)S(1)} %broadcast_compare_fusion) | copy-start | bytes 196612
  67.8 3.1 copy-start.4
  71.3 30.6 %copy-start.32 = (bf16[256,1152]{1,0:T(8,128)(2,1)}, bf16[256,1152]{1,0:T(8,128)(2,1)S(1)}, u32[]{:S(2)}) copy-start(bf16[256,1152]{1,0:T(8,128)(2,1)S(1)} %fusion.33) | copy-start | bytes 1769476
  108.3 2.1 copy-start.8
  108.6 1.9 copy-start.19
  108.6 3.9 slice-start
  109.5 2.2 copy-start.2
  109.5 4.3 slice-start.1
  111.7 6.3 copy-start.24
  117.7 72.9 %copy-start.29 = (bf16[256,1152]{1,0:T(8,128)(2,1)S(1)}, bf16[256,1152]{1,0:T(8,128)(2,1)}, u32[]{:S(2)}) copy-start(bf16[256,1152]{1,0:T(8,128)(2,1)} %get-tuple-element.18) | copy-start | bytes 1769476
  118.3 161.0 %copy-start.17 = (bf16[256,1152]{1,0:T(8,128)(2,1)}, bf16[256,1152]{1,0:T(8,128)(2,1)S(1)}, u32[]{:S(2)}) copy-start(bf16[256,1152]{1,0:T(8,128)(2,1)S(1)} %fusion.43) | copy-start | bytes 1769476
  279.3 18.5 %slice-start.4 = ((s8[10616832]{0:T(1024)(128)(4,1)}), s8[4194304]{0:T(1024)(128)(4,1)S(1)}, s32[]{:S(2)}) async-start(s8[10616832]{0:T(1024)(128)(4,1)} %bitcast.142), calls=%async_computation.19 | async-start | bytes 8388608
  279.3 18.5 %slice-start.5 = ((s8[10616832]{0:T(1024)(128)(4,1)}), s8[4194304]{0:T(1024)(128)(4,1)S(1)}, s32[]{:S(2)}) async-start(s8[10616832]{0:T(1024)(128)(4,1)} %bitcast.142), calls=%async_computation.20 | async-start | bytes 8388608
  289.2 8.6 copy-start.16
  289.2 8.7 copy-start.47
  289.2 8.7 copy-start.44
  289.2 8.7 slice-start.6
  289.2 12.2 slice-start.2
  297.9 3.5 slice-start.3
  301.4 3.2 copy-start.14
  301.4 1.5 copy-start.11
  311.1 4.2 copy-start.3
  311.1 4.2 copy-start.28
  311.1 4.2 copy-start.36
  316.6 1.3 copy-start.20
  317.1 2.2 copy-start.21
  317.9 1.4 copy-start.23
  319.0 7.2 copy-start.31
  319.0 1.3 copy-start.33
  320.2 20.6 %copy-start.25 = (bf16[16,72,256]{2,1,0:T(8,128)(2,1)S(1)}, bf16[16,72,256]{2,1,0:T(8,128)(2,1)}, u32[]{:S(2)}) copy-start(bf16[16,72,256]{2,1,0:T(8,128)(2,1)} %copy-done.24) | copy-start | bytes 1769476
  337.0 7.8 all-to-all-start.6
  347.4 19.5 %all-to-all-start.7 = ((bf16[16,2,144]{2,1,0:T(2,128)(2,1)}), bf16[16,2,144]{2,1,0:T(2,128)(2,1)}, u32[]{:S(2)}, u32[]{:S(2)}) async-start(bf16[16,2,144]{2,1,0:T(2,128)(2,1)} %reshape.175), calls=%async_computation.7 | async-start | bytes 32768 | tf_op jit(solution)/shard_map/all_to_all | solution.py:261
  366.9 7.9 copy-start.18
  366.9 124.8 %all-to-all-start = ((bf16[16,2,144,1152]{3,2,0,1:T(8,128)(2,1)}), bf16[16,2,144,1152]{3,2,0,1:T(8,128)(2,1)}, u32[]{:S(2)}, u32[]{:S(2)}) async-start(bf16[16,2,144,1152]{3,2,0,1:T(8,128)(2,1)} %copy.72), calls=%async_computation | async-start | bytes 21233664 | tf_op jit(solution)/shard_map/all_to_all | solution.py:210
  384.5 115.3 %copy-start.30 = (bf16[256,1152]{1,0:T(8,128)(2,1)S(1)}, bf16[256,1152]{1,0:T(8,128)(2,1)}, u32[]{:S(2)}) copy-start(bf16[256,1152]{1,0:T(8,128)(2,1)} %get-tuple-element.18) | copy-start | bytes 1769476
  491.8 124.2 %all-to-all-start.2 = ((bf16[16,2,144,1152]{3,2,0,1:T(8,128)(2,1)}), bf16[16,2,144,1152]{3,2,0,1:T(8,128)(2,1)}, u32[]{:S(2)}, u32[]{:S(2)}) async-start(bf16[16,2,144,1152]{3,2,0,1:T(8,128)(2,1)} %copy.73), calls=%async_computation.2 | async-start | bytes 21233664 | tf_op jit(solution)/shard_map/all_to_all | solution.py:217
  616.0 123.0 %all-to-all-start.4 = ((bf16[16,2,144,1152]{3,2,0,1:T(8,128)(2,1)}), bf16[16,2,144,1152]{3,2,0,1:T(8,128)(2,1)}, u32[]{:S(2)}, u32[]{:S(2)}) async-start(bf16[16,2,144,1152]{3,2,0,1:T(8,128)(2,1)} %copy.74), calls=%async_computation.4 | async-start | bytes 21233664 | tf_op jit(solution)/shard_map/all_to_all | solution.py:224
  633.6 111.1 %copy-start.22 = (bf16[16,72,256]{2,1,0:T(8,128)(2,1)S(1)}, bf16[16,72,256]{2,1,0:T(8,128)(2,1)}, u32[]{:S(2)}) copy-start(bf16[16,72,256]{2,1,0:T(8,128)(2,1)} %copy-done.21) | copy-start | bytes 1769476
  633.6 111.1 %copy-start.40 = (f32[256]{0:T(256)S(1)}, f32[256]{0:T(256)}, u32[]{:S(2)}) copy-start(f32[256]{0:T(256)} %copy-done.39) | copy-start | bytes 3076
  633.6 111.1 %copy-start.43 = (f32[256]{0:T(256)S(1)}, f32[256]{0:T(256)}, u32[]{:S(2)}) copy-start(f32[256]{0:T(256)} %copy-done.42) | copy-start | bytes 3076
  739.0 110.5 %all-to-all-start.1 = ((bf16[16,144,1152]{2,1,0:T(8,128)(2,1)}), bf16[16,144,1152]{2,1,0:T(8,128)(2,1)}, u32[]{:S(2)}, u32[]{:S(2)}) async-start(bf16[16,144,1152]{2,1,0:T(8,128)(2,1)} %reduce_sum.249), calls=%async_computation.1 | async-start | bytes 10616832 | tf_op jit(solution)/shard_map/all_to_all | solution.py:240
  744.4 44.6 %reduce-scatter.8.cloned.1.call-start = ((), (), s32[]{:S(2)}) async-start(), calls=%async_computation.13 | async-start | bytes 2654208
  744.7 7.0 copy-start.6
  751.6 3.0 copy-start.13
  754.6 1.5 copy-start.15
  754.7 1.5 copy-start.38
  756.2 32.8 %copy-start.34 = (bf16[16,1152]{1,0:T(8,128)(2,1)S(1)}, bf16[16,1152]{1,0:T(8,128)(2,1)}, u32[]{:S(2)}) copy-start(bf16[16,1152]{1,0:T(8,128)(2,1)} %param.12) | copy-start | bytes 110596
  760.3 498.4 %reduce-scatter.10.cloned.1.call-start = ((), (), s32[]{:S(2)}) async-start(), calls=%async_computation.14 | async-start | bytes 16920576
  849.5 190.6 %all-to-all-start.3 = ((bf16[16,144,1152]{2,1,0:T(8,128)(2,1)}), bf16[16,144,1152]{2,1,0:T(8,128)(2,1)}, u32[]{:S(2)}, u32[]{:S(2)}) async-start(bf16[16,144,1152]{2,1,0:T(8,128)(2,1)} %reduce_sum.251), calls=%async_computation.3 | async-start | bytes 10616832 | tf_op jit(solution)/shard_map/all_to_all | solution.py:247
  928.4 147.8 %copy-start.46 = (u32[32]{0:T(128)S(1)}, u32[32]{0:T(128)}, u32[]{:S(2)}) copy-start(u32[32]{0:T(128)} %constant.76) | copy-start | bytes 388
  928.4 148.4 %copy-start.45 = (u32[32]{0:T(128)S(1)}, u32[32]{0:T(128)}, u32[]{:S(2)}) copy-start(u32[32]{0:T(128)} %constant.72) | copy-start | bytes 388
  928.4 151.8 %copy-start.7 = (bf16[3456,16]{1,0:T(8,128)(2,1)S(1)}, bf16[3456,16]{1,0:T(8,128)(2,1)}, u32[]{:S(2)}) copy-start(bf16[3456,16]{1,0:T(8,128)(2,1)} %reduce-scatter.8.cloned.1.call-done) | copy-start | bytes 331780
  1040.1 214.2 %all-to-all-start.5 = ((bf16[16,144,1152]{2,1,0:T(8,128)(2,1)}), bf16[16,144,1152]{2,1,0:T(8,128)(2,1)}, u32[]{:S(2)}, u32[]{:S(2)}) async-start(bf16[16,144,1152]{2,1,0:T(8,128)(2,1)} %reduce_sum.253), calls=%async_computation.5 | async-start | bytes 10616832 | tf_op jit(solution)/shard_map/all_to_all | solution.py:254
  1250.2 8.4 copy-start.1
  (4 other events, 4.4 us)
Sparse Core Ops, SparseCore 0:
  10.9 90.8 all-gather.3
  104.7 85.7 all-gather.7
  193.5 85.7 all-gather.5
  760.4 28.5 reduce-scatter.7
  798.1 262.8 reduce-scatter.9
where the time goes:
time: 1280 us; the launch traced here: 1270 us
  waiting for transfers between devices  681 us (53%)
  blocking collectives  208 us (16%)
  starting transfers between devices  142 us (11%)
  matrix products  107 us (8%)
  other arithmetic  68.5 us (5%)
  local copies, waits for them, and re-layouts  43.1 us (3%)
  between operations  16.1 us (1%)
    unnamed x3, blocking collectives  202 us
    all_to_all x1, waiting for transfers between devices, on_device(): lax.all_to_all(jnp.sum(fcin_pair, axis=1).astype(jnp.bfloat16), 'dp', spl...  112 us
    all_to_all x1, waiting for transfers between devices, on_device(): lax.all_to_all(owner_blocks(grad_attn_w, dp_count, mod_count).astype(jnp....  107 us
    all_to_all x1, waiting for transfers between devices, on_device(): lax.all_to_all(owner_blocks(grad_fcout, dp_count, mod_count).astype(jnp.b...  105 us
    all_to_all x1, waiting for transfers between devices, on_device(): lax.all_to_all(owner_blocks(grad_fcin, dp_count, mod_count).astype(jnp.bf...  105 us
    all_gather x1, waiting for transfers between devices, on_device(): lax.all_gather(fc_in, ('dp', 'mod'), axis=0, tiled=True)  76.3 us
    all_gather x1, waiting for transfers between devices, on_device(): lax.all_gather(fc_out, ('dp', 'mod'), axis=0, tiled=True)  72.2 us
    all_to_all x1, starting transfers between devices, on_device(): lax.all_to_all(jnp.sum(fcin_pair, axis=1).astype(jnp.bfloat16), 'dp', spl...  68.9 us
  transfers between devices with their start and end apart: 13, of which 10 were waited for; matrix products, arithmetic and copies ran while one was open for 12% of the time, Pallas kernels for 0%

commit v1 on v0

v1 whole, which is shorter than its diff:
```python
import jax
import jax.numpy as jnp
from jax import lax
from jax.experimental import pallas as pl
from jax.experimental.pallas import tpu as pltpu
from jax.sharding import PartitionSpec as P

HEADS = 16
highest = lax.Precision.HIGHEST
norm_eps = 1e-06
bf16 = jnp.bfloat16
f32 = jnp.float32


def layer_norm(values):
    center = values - jnp.mean(values, axis=-1, keepdims=True)
    inverse = lax.rsqrt(jnp.mean(center * center, axis=-1, keepdims=True) + norm_eps)
    return (center * inverse, inverse)


def norm_back(grad_in, normed, inverse):
    centered = grad_in - jnp.mean(grad_in, axis=-1, keepdims=True)
    return (centered - normed * jnp.mean(grad_in * normed, axis=-1, keepdims=True)) * inverse


def times_rows(left, right):
    return lax.dot_general(left, right, (((1,), (1,)), ((), ())), preferred_element_type=f32)


def contract_rows(left, right):
    return lax.dot_general(left, right, (((0,), (0,)), ((), ())), preferred_element_type=f32)


def times(left, right):
    return jnp.dot(left, right, preferred_element_type=f32)


def gelu_tanh(values):
    return jax.nn.gelu(values, approximate=True)


class Net:
    def __init__(self):
        self.dp = lax.axis_size("dp")
        self.mod = lax.axis_size("mod")
        self.bits = self.dp.bit_length() - 1
        self.dp_rank = lax.axis_index("dp")
        self.mod_rank = lax.axis_index("mod")
        self.chips = self.dp // 2 * self.mod

    def swap(self, value, dim):
        if dim == "mod":
            return lax.ppermute(value, "mod", [(i, i ^ 1) for i in range(self.mod)])
        return lax.ppermute(value, "dp", [(i, i ^ (1 << dim)) for i in range(self.dp)])

    def mask(self, order, j):
        dp_mask, mod_mask = 0, 0
        for step, dim in enumerate(order):
            if j >> step & 1:
                if dim == "mod":
                    mod_mask ^= 1
                else:
                    dp_mask ^= 1 << dim
        return dp_mask, mod_mask

    def device(self, order, j, core):
        dp_mask, mod_mask = self.mask(order, j)
        return (self.dp_rank ^ (dp_mask ^ core)) * self.mod + (self.mod_rank ^ mod_mask)

    def gather(self, value, order):
        for dim in order[:-1]:
            value = jnp.concatenate([value, self.swap(value, dim)], axis=0)
        return value, self.swap(value, order[-1])

    def scatter(self, own, other, order):
        for step in range(len(order) - 1, -1, -1):
            got = self.swap(other, order[step])
            total = own.astype(f32) + got.astype(f32)
            if step == 0:
                return total
            total = total.astype(bf16)
            half = total.shape[0] // 2
            own, other = total[:half], total[half:]


def copy_kernel(moves, *refs):
    index_ref, refs, sems = refs[0], refs[1:-1], refs[-1]
    copies = []
    for n, (source, source_at, target, target_at, rows) in enumerate(moves):
        if source_at is None:
            source_at = pl.multiple_of(index_ref[n] * rows, rows)
        if target_at is None:
            target_at = pl.multiple_of(index_ref[n] * rows, rows)
        copies.append(
            pltpu.make_async_copy(
                refs[source].at[pl.ds(source_at, rows)],
                refs[target].at[pl.ds(target_at, rows)],
                sems.at[n],
            )
        )
    for copy in copies:
        copy.start()
    for copy in copies:
        copy.wait()


def move_blocks(arrays, shapes, moves, index):
    any_spec = pl.BlockSpec(memory_space=pl.ANY)
    return pl.pallas_call(
        lambda *refs: copy_kernel(moves, *refs),
        grid_spec=pltpu.PrefetchScalarGridSpec(
            num_scalar_prefetch=1,
            grid=(1,),
            in_specs=[any_spec] * len(arrays),
            out_specs=[any_spec] * len(shapes),
            scratch_shapes=[pltpu.SemaphoreType.DMA((len(moves),))],
        ),
        out_shape=[jax.ShapeDtypeStruct(s, bf16) for s in shapes],
        compiler_params=pltpu.CompilerParams(vmem_limit_bytes=4 * 1024 * 1024),
        name="move_blocks",
    )(index, *arrays)


def on_device(
    tokens,
    cond,
    segment_ids,
    crop_slot,
    ada_weight,
    ada_bias,
    attn_weight,
    fc_in,
    fc_out,
    biases,
    out_grad,
):
    net = Net()
    model_width = tokens.shape[2]
    tok_len = tokens.shape[1]
    head_count = HEADS
    head_dim = model_width // head_count
    score_scale = head_dim ** (-0.5)
    dp_count, mod_count = net.dp, net.mod
    crop_count = crop_slot.shape[1] // mod_count
    mod_rank = net.mod_rank
    high = list(range(net.bits - 1, 1, -1))
    order_a = ["mod"] + high + [1]
    order_b = [1] + high + ["mod"]
    attn_orders = [[high[0], "mod"] + high[1:] + [1], high[1:] + [high[0], 1, "mod"], [high[0], 1, "mod"] + high[1:]]
    shard = attn_weight.shape[0]
    chips = net.chips
    third = shard // 3
    attn_cut = [third, third, third]
    part_a = shard * 5 // 9 // 16 * 16 if shard % 16 == 0 else shard // 2
    fc_cut = [part_a, shard - part_a]
    fc_orders = [order_a, order_b]

    attn_parts = []
    for n in range(3):
        attn_parts.append(net.gather(attn_weight[n * third : (n + 1) * third], attn_orders[n]))
    attn_other = [tuple(net.swap(piece, 0) for piece in pair) for pair in attn_parts]
    fcin_pieces, fcout_pieces, fc_order_of = [], [], []
    for weight, pieces in ((fc_in, fcin_pieces), (fc_out, fcout_pieces)):
        start = 0
        for rows, order in zip(fc_cut, fc_orders):
            pieces.extend(net.gather(weight[start : start + rows], order))
            start += rows

    arrays, moves, index = [], [], []
    for core in range(2):
        for n in range(3):
            for side in range(2):
                arrays.append((attn_parts, attn_other)[core][n][side])
                for j in range(chips // 2):
                    moves.append((len(arrays) - 1, j * third, None, None, third))
                    index.append(net.device(attn_orders[n], j + side * (chips // 2), core) * 3 + n)
    index = jnp.stack(index).astype(jnp.int32)
    blocky = third % 16 == 0
    if blocky:
        to_natural = [(s, sa, 12, ta, r) for s, sa, _, ta, r in moves]
        (attn_w,) = move_blocks(arrays, [(shard * dp_count * mod_count, model_width)], to_natural, index)
    else:
        spread = jnp.concatenate(arrays)

        def place(n, whole):
            block = lax.dynamic_slice_in_dim(spread, n * third, third)
            return lax.dynamic_update_slice_in_dim(whole, block, index[n] * third, 0)

        attn_w = lax.fori_loop(0, len(moves), place, jnp.zeros_like(spread))

    silu_cond = jax.nn.silu(cond.astype(f32)).astype(bf16)
    mod_part = times(silu_cond, ada_weight) + ada_bias.reshape(-1).astype(f32)
    mod_own = mod_part.astype(bf16)
    mod_other = net.swap(mod_own, "mod")
    modulation = jnp.concatenate(
        [jnp.where(mod_rank == 0, mod_own, mod_other), jnp.where(mod_rank == 0, mod_other, mod_own)], axis=1
    )
    seg_ids = segment_ids[0]
    slots = lax.dynamic_slice_in_dim(crop_slot[0], mod_rank * crop_count, crop_count)
    crop_onehot = seg_ids[:, None] == jnp.arange(crop_count, dtype=jnp.int32)[None, :]
    token_slot = jnp.sum(jnp.where(crop_onehot, slots[None, :], 0), axis=1)
    slot_pick = token_slot[:, None] == jnp.arange(cond.shape[0], dtype=jnp.int32)[None, :]
    slot_pick = slot_pick.astype(bf16)
    token_mod = times(slot_pick, modulation)
    shift_a, scale_a, gate_a, shift_m, scale_m, gate_m = jnp.split(token_mod, 6, axis=1)

    bias_all = lax.all_gather(biases, ("dp", "mod"), axis=0, tiled=True)
    bias_query = bias_all[:model_width].astype(f32)
    bias_value = bias_all[model_width : 2 * model_width].astype(f32)
    bias_proj = bias_all[2 * model_width : 3 * model_width].astype(f32)
    bias_out = bias_all[3 * model_width : 4 * model_width].astype(f32)
    bias_in = bias_all[4 * model_width :].reshape(dp_count * mod_count, shard)
    bias_pieces, picks = [], []
    start = 0
    for rows, order in zip(fc_cut, fc_orders):
        for side in range(2):
            devices = jnp.stack([net.device(order, j + side * (chips // 2), 0) for j in range(chips // 2)])
            pick = (devices[:, None] == jnp.arange(dp_count * mod_count)[None, :]).astype(bf16)
            picks.append(pick)
            bias_pieces.append(times(pick, bias_in[:, start : start + rows]).reshape(-1))
        start += rows

    qkv_weight = attn_w[: 3 * model_width]
    proj_weight = attn_w[3 * model_width :]
    resid = tokens[0].astype(f32)
    normed_a, inverse_a = layer_norm(resid)
    attn_in = (normed_a * (1.0 + scale_a) + shift_a).astype(bf16)
    qkv_bias = jnp.concatenate([bias_query, jnp.zeros_like(bias_query), bias_value])
    qkv = (times_rows(attn_in, qkv_weight) + qkv_bias).astype(bf16)
    query = qkv[:, :model_width].reshape(tok_len, head_count, head_dim)
    key_part = qkv[:, model_width : 2 * model_width].reshape(tok_len, head_count, head_dim)
    value = qkv[:, 2 * model_width :].reshape(tok_len, head_count, head_dim)
    same_crop = seg_ids[:, None] == seg_ids[None, :]

    def scores_of(left, right):
        raw = jnp.einsum("qhd,khd->hqk", left, right, preferred_element_type=f32) * score_scale
        return jnp.where(same_crop[None], raw, -1e30)

    scores = scores_of(query, key_part)
    row_max = jnp.max(scores, axis=-1, keepdims=True)
    log_total = row_max + jnp.log(jnp.sum(jnp.exp(scores - row_max), axis=-1, keepdims=True))
    probs = jnp.exp(scores - log_total).astype(bf16)
    context = jnp.einsum("hqk,khd->qhd", probs, value, preferred_element_type=f32)
    context = context.reshape(tok_len, model_width).astype(bf16)
    attn_out = times_rows(context, proj_weight) + bias_proj
    mid = resid + gate_a * attn_out
    normed_m, inverse_m = layer_norm(mid)
    mlp_in = (normed_m * (1.0 + scale_m) + shift_m).astype(bf16)
    grad_out = out_grad[0].astype(f32)
    grad_mlp = (gate_m * grad_out).astype(bf16)

    mlp_both = jnp.concatenate([mlp_in, net.swap(mlp_in, 0)], axis=0)
    grad_both = jnp.concatenate([grad_mlp, net.swap(grad_mlp, 0)], axis=0)
    out_sum, back_sum = 0.0, 0.0
    fcin_grads, fcout_grads, grad_bias_in = [], [], 0.0
    hiddens, acts = [], []
    start = 0
    for n, (w_in, b_in) in enumerate(zip(fcin_pieces, bias_pieces)):
        hidden = times_rows(mlp_both, w_in) + b_in
        act = gelu_tanh(hidden).astype(bf16)
        hiddens.append(hidden)
        acts.append(act)
        fcout_grads.append(contract_rows(act, grad_both).astype(bf16))
    for n, (w_in, w_out) in enumerate(zip(fcin_pieces, fcout_pieces)):
        out_sum = out_sum + times(acts[n], w_out)
        gelu_back = jax.vjp(gelu_tanh, hiddens[n])[1]
        grad_hidden = gelu_back(times_rows(grad_both, w_out))[0].astype(bf16)
        fcin_grads.append(contract_rows(grad_hidden, mlp_both).astype(bf16))
        back_sum = back_sum + times(grad_hidden, w_in)
        rows = fc_cut[n // 2]
        column = jnp.sum(grad_hidden.astype(f32), axis=0).reshape(chips // 2, rows)
        placed = jnp.dot(picks[n].astype(f32).T, column, precision=highest)
        lead = 0 if n < 2 else fc_cut[0]
        grad_bias_in = grad_bias_in + jnp.pad(placed, ((0, 0), (lead, shard - lead - rows)))
    mlp_out = out_sum[:tok_len] + net.swap(out_sum[tok_len:], 0) + bias_out
    grad_mlp_in = back_sum[:tok_len] + net.swap(back_sum[tok_len:], 0)

    result = (mid + gate_m * mlp_out).astype(bf16)
    grad_gate_m = grad_out * mlp_out
    grad_scale_m = grad_mlp_in * normed_m
    grad_mid = grad_out + norm_back(grad_mlp_in * (1.0 + scale_m), normed_m, inverse_m)
    grad_gate_a = grad_mid * attn_out
    grad_attn = (gate_a * grad_mid).astype(bf16)
    grad_proj = contract_rows(grad_attn, context)
    grad_context = times(grad_attn, proj_weight)
    grad_context = grad_context.astype(bf16).reshape(tok_len, head_count, head_dim)
    scores_again = scores_of(query, key_part)
    probs_full = jnp.exp(scores_again - log_total)
    probs_low = probs_full.astype(bf16)
    grad_probs = jnp.einsum("qhd,khd->hqk", grad_context, value, preferred_element_type=f32)
    grad_scores = probs_full * (grad_probs - jnp.sum(grad_probs * probs_full, axis=-1, keepdims=True))
    grad_scores = grad_scores.astype(bf16)
    grad_query = jnp.einsum("hqk,khd->qhd", grad_scores, key_part, preferred_element_type=f32) * score_scale
    grad_keys = jnp.einsum("hqk,qhd->khd", grad_scores, query, preferred_element_type=f32) * score_scale
    grad_value = jnp.einsum("hqk,qhd->khd", probs_low, grad_context, preferred_element_type=f32)
    grad_qkv = jnp.concatenate(
        [
            grad_query.reshape(tok_len, model_width),
            grad_keys.reshape(tok_len, model_width),
            grad_value.reshape(tok_len, model_width),
        ],
        axis=1,
    ).astype(bf16)
    grad_qkv_w = contract_rows(grad_qkv, attn_in)
    grad_attn_in = times(grad_qkv, qkv_weight)
    grad_scale_a = grad_attn_in * normed_a
    grad_tokens = grad_mid + norm_back(grad_attn_in * (1.0 + scale_a), normed_a, inverse_a)
    grad_qkv_wide = grad_qkv.astype(f32)
    grad_bias = jnp.concatenate(
        [
            jnp.sum(grad_qkv_wide[:, :model_width], axis=0),
            jnp.sum(grad_qkv_wide[:, 2 * model_width :], axis=0),
            jnp.sum(grad_attn.astype(f32), axis=0),
            jnp.sum(grad_mlp.astype(f32), axis=0),
            grad_bias_in.reshape(-1),
        ]
    )
    bias_sum = lax.psum_scatter(grad_bias, ("dp", "mod"), scatter_dimension=0, tiled=True)

    grad_token_mod = jnp.concatenate(
        [grad_attn_in, grad_scale_a, grad_gate_a, grad_mlp_in, grad_scale_m, grad_gate_m], axis=1
    )
    token_high = lax.reduce_precision(grad_token_mod, 8, 7)
    token_low = (grad_token_mod - token_high).astype(bf16)
    grad_pair = contract_rows(slot_pick, token_high.astype(bf16)) + contract_rows(slot_pick, token_low)
    grad_pair = grad_pair.astype(bf16)
    width = grad_pair.shape[1] // 2
    pair_own = jnp.where(mod_rank == 0, grad_pair[:, :width], grad_pair[:, width:])
    pair_send = jnp.where(mod_rank == 0, grad_pair[:, width:], grad_pair[:, :width])
    grad_mod = (pair_own.astype(f32) + net.swap(pair_send, "mod").astype(f32)).astype(bf16)
    grad_silu = times_rows(grad_mod, ada_weight)
    silu_own = jnp.where(mod_rank == 0, grad_silu[:crop_count], grad_silu[crop_count:])
    silu_send = jnp.where(mod_rank == 0, grad_silu[crop_count:], grad_silu[:crop_count])
    grad_silu = silu_own + net.swap(silu_send.astype(bf16), "mod").astype(f32)
    own_cond = lax.dynamic_slice_in_dim(cond, mod_rank * crop_count, crop_count, 0).astype(f32)
    silu_back = jax.vjp(jax.nn.silu, own_cond)[1]
    grad_cond = silu_back(grad_silu)[0]
    ada_order = [1] + high + [0]
    mod_rows = jnp.concatenate(net.gather(grad_mod, ada_order), axis=0)
    cond_rows = jnp.concatenate(net.gather(silu_cond, ada_order), axis=0)
    own_rows = model_width // dp_count
    cond_cols = lax.dynamic_slice_in_dim(cond_rows, net.dp_rank * own_rows, own_rows, 1)
    ada_w_sum = contract_rows(cond_cols, mod_rows)
    ada_b_sum = jnp.sum(mod_rows.astype(f32), axis=0).reshape(ada_bias.shape[0], model_width)
    ada_b_sum = lax.dynamic_slice_in_dim(ada_b_sum, net.dp_rank * own_rows, own_rows, 1)

    start = 0
    fc_sums = []
    for grads in (fcout_grads, fcin_grads):
        fc_sums.append(
            jnp.concatenate(
                [net.scatter(grads[2 * n], grads[2 * n + 1], fc_orders[n]) for n in range(2)], axis=0
            )
        )
    fcout_sum, fcin_sum = fc_sums
    attn_grad = jnp.concatenate([grad_qkv_w, grad_proj], axis=0).astype(bf16)
    if blocky:
        shapes = [a.shape for a in arrays]
        from_natural = [(0, None, s + 1, sa, r) for s, sa, _, ta, r in moves]
        grads = move_blocks([attn_grad], shapes, from_natural, index)
    else:
        def take(n, whole):
            block = lax.dynamic_slice_in_dim(attn_grad, index[n] * third, third)
            return lax.dynamic_update_slice_in_dim(whole, block, n * third, 0)

        grads = jnp.split(lax.fori_loop(0, len(moves), take, jnp.zeros_like(attn_grad)), 12)
    attn_sum = []
    for n in range(3):
        pair = [
            (grads[2 * n + s].astype(f32) + net.swap(grads[6 + 2 * n + s], 0).astype(f32)).astype(bf16)
            for s in range(2)
        ]
        attn_sum.append(net.scatter(pair[0], pair[1], attn_orders[n]))
    attn_sum = jnp.concatenate(attn_sum, axis=0)
    return (
        result[None],
        grad_tokens[None],
        grad_cond,
        ada_w_sum,
        ada_b_sum,
        attn_sum,
        fcin_sum,
        fcout_sum,
        bias_sum,
    )


def solution(mesh):
    placed = (
        P(("dp", "mod"), None, None),
        P("dp", None),
        P(("dp", "mod"), None),
        P("dp", None),
        P(None, "mod"),
        P("mod", None),
        P(("dp", "mod"), None),
        P(("dp", "mod"), None),
        P(("dp", "mod"), None),
        P(("dp", "mod")),
        P(("dp", "mod"), None, None),
    )
    return jax.shard_map(
        on_device,
        mesh=mesh,
        in_specs=placed,
        out_specs=(
            P(("dp", "mod"), None, None),
            P(("dp", "mod"), None, None),
            P(("dp", "mod"), None),
            P("dp", "mod"),
            P("mod", "dp"),
            P(("dp", "mod"), None),
            P(("dp", "mod"), None),
            P(("dp", "mod"), None),
            P(("dp", "mod")),
        ),
        check_vma=False,
    )
```

time: 1280 us -> 715 us (0.56)
  waiting for transfers between devices: 681 us -> 307 us
  blocking collectives: 208 us -> 79.6 us
  starting transfers between devices: 142 us -> 83 us
  Pallas kernels: 0 us -> 33.7 us
    all_to_all x8 -> x0, waiting for transfers between devices: 471 us -> none  [the longest x1 112 us: on_device(): lax.all_to_all(jnp.sum(fcin_pair, axis=1).astype(jnp.bfloat16), 'dp', spl...]
    ppermute x0 -> x83, waiting for transfers between devices: none -> 307 us  [the longest x66 277 us: swap(): lax.ppermute(value, 'dp', [(i, i ^ 1 << dim) for i in range(self.dp)])]
    all_gather x3 -> x0, waiting for transfers between devices: 179 us -> none  [the longest x1 76.3 us: on_device(): lax.all_gather(fc_in, ('dp', 'mod'), axis=0, tiled=True)]
    all_to_all x8 -> x0, starting transfers between devices: 142 us -> none  [the longest x1 68.9 us: on_device(): lax.all_to_all(jnp.sum(fcin_pair, axis=1).astype(jnp.bfloat16), 'dp', spl...]
    unnamed x3 -> x2, blocking collectives: 202 us -> 79.6 us
    ppermute x0 -> x83, starting transfers between devices: none -> 83 us  [the longest x66 63.1 us: swap(): lax.ppermute(value, 'dp', [(i, i ^ 1 << dim) for i in range(self.dp)])]
    reduce_sum x11 -> x3, other arithmetic: 46.9 us -> 3.88 us  [the longest x1 2.49 us: on_device(): jnp.sum(grad_attn.astype(f32), axis=0)]
    pallas_call x0 -> x2, Pallas kernels: none -> 33.7 us  [move_blocks(): pl.pallas_call(lambda *refs: copy_kernel(moves, *refs), grid_spec=pltpu.P...]
  transfers between devices with their start and end apart: 13 -> 83, of which waited for: 10 -> 34; matrix products, arithmetic and copies ran while one was open for 12% -> 25% of each run, Pallas kernels for 0% -> 5%
where the time goes in v1:
time: 715 us; the launch traced here: 706 us
  waiting for transfers between devices  307 us (43%)
  matrix products  102 us (14%)
  starting transfers between devices  83 us (12%)
  blocking collectives  79.6 us (11%)
  other arithmetic  56 us (8%)
  local copies, waits for them, and re-layouts  41.3 us (6%)
  Pallas kernels  33.7 us (5%)
    ppermute x66, waiting for transfers between devices, swap(): lax.ppermute(value, 'dp', [(i, i ^ 1 << dim) for i in range(self.dp)])  277 us
    unnamed x2, blocking collectives  79.6 us
    ppermute x66, starting transfers between devices, swap(): lax.ppermute(value, 'dp', [(i, i ^ 1 << dim) for i in range(self.dp)])  63.1 us
    pallas_call x2, Pallas kernels, move_blocks(): pl.pallas_call(lambda *refs: copy_kernel(moves, *refs), grid_spec=pltpu.P...  33.7 us
    dot_general x13, matrix products, contract_rows(): lax.dot_general(left, right, (((0,), (0,)), ((), ())), preferred_element_...  31.8 us
    dot_general x16, matrix products, times(): return jnp.dot(left, right, preferred_element_type=f32)  30.6 us
    ppermute x17, waiting for transfers between devices, swap(): return lax.ppermute(value, 'mod', [(i, i ^ 1) for i in range(self.mod)])  30.3 us
    dot_general x11, matrix products, times_rows(): lax.dot_general(left, right, (((1,), (1,)), ((), ())), preferred_element_...  29.5 us
  transfers between devices with their start and end apart: 83, of which 34 were waited for; matrix products, arithmetic and copies ran while one was open for 25% of the time, Pallas kernels for 5%

profile of v1, /device:TPU:0, one launch (start us, length us, event | category | flops | bytes accessed | tf_op | source)
XLA Modules:
  0.0 706.3 jit_solution(457895173048105661)
XLA Ops:
  1.5 3.0 collective-permute-start.41
  5.3 4.5 fusion.12
  14.8 39.8 %all-reduce.4 = bf16[9216]{0:T(1024)(128)(2,1)S(1)} all-reduce(bf16[9216]{0:T(1024)(128)(2,1)S(1)} %dynamic-update-slice), channel_id=1, replica_groups=mesh['dp'=16,'mod'=2] {'dp','mod'}, use_global_device_ids=true, to_apply=%add.4 | all-reduce | flops 9216 | bytes 36864
  61.6 2.3 collective-permute-start.20
  69.4 2.3 collective-permute-start.1
  71.7 4.5 collective-permute-done.1
  77.5 6.6 collective-permute-done.42
  84.0 6.9 collective-permute-done.9
  91.0 14.8 %collective-permute-start.10 = (bf16[96,1152]{1,0:T(8,128)(2,1)S(1)}, bf16[96,1152]{1,0:T(8,128)(2,1)S(1)}, u32[]{:S(2)}, u32[]{:S(2)}) collective-permute-start(bf16[96,1152]{1,0:T(8,128)(2,1)S(1)} %pad_maximum_fusion.30), channel_id=1, source_target_pairs={{0,4},{2,6},{4,0},{6,2},{8,12},{10,14},{12,8},{14,10},{16,20},{18,... | collective-permute-start | bytes 663560 | tf_op jit(solution)/shard_map/ppermute | solution.py:54
  106.1 3.0 collective-permute-start.32
  109.2 2.4 collective-permute-done.10
  114.4 13.5 %collective-permute-done.6 = bf16[96,1152]{1,0:T(8,128)(2,1)S(1)} collective-permute-done((bf16[96,1152]{1,0:T(8,128)(2,1)S(1)}, bf16[96,1152]{1,0:T(8,128)(2,1)S(1)}, u32[]{:S(2)}, u32[]{:S(2)}) %collective-permute-start.6) | collective-permute-done | bytes 221216 | tf_op jit(solution)/shard_map/ppermute | solution.py:54
  129.3 16.5 %collective-permute-done.3 = bf16[192,1152]{1,0:T(8,128)(2,1)S(1)} collective-permute-done((bf16[192,1152]{1,0:T(8,128)(2,1)S(1)}, bf16[192,1152]{1,0:T(8,128)(2,1)S(1)}, u32[]{:S(2)}, u32[]{:S(2)}) %collective-permute-start.3) | collective-permute-done | bytes 442400 | tf_op jit(solution)/shard_map/ppermute | solution.py:54
  150.9 14.2 %collective-permute-done.21 = bf16[160,1152]{1,0:T(8,128)(2,1)S(1)} collective-permute-done((bf16[160,1152]{1,0:T(8,128)(2,1)S(1)}, bf16[160,1152]{1,0:T(8,128)(2,1)S(1)}, u32[]{:S(2)}, u32[]{:S(2)}) %collective-permute-start.21) | collective-permute-done | bytes 368672 | tf_op jit(solution)/shard_map/ppermute | solution.py:54
  166.0 24.8 %collective-permute-done.33 = bf16[256,1152]{1,0:T(8,128)(2,1)S(1)} collective-permute-done((bf16[256,1152]{1,0:T(8,128)(2,1)S(1)}, bf16[256,1152]{1,0:T(8,128)(2,1)S(1)}, u32[]{:S(2)}, u32[]{:S(2)}) %collective-permute-start.33) | collective-permute-done | bytes 589856 | tf_op jit(solution)/shard_map/ppermute | solution.py:54
  198.3 18.3 %move_blocks.2 = bf16[4608,1152]{1,0:T(8,128)(2,1)S(1)} custom-call(s32[96]{0:T(128)S(1)} %stack.463.refs_0_, bf16[384,1152]{1,0:T(8,128)(2,1)S(1)} %pad_maximum_fusion.8.refs_1_, bf16[384,1152]{1,0:T(8,128)(2,1)S(1)} %collective-permute-done.4.refs_2_, bf16[384,1152]{1,0:T(8,128)(2,1)S(1)} %pad_maximum_fusion.9.refs_3_, ...), custom_call_target="tpu_custom_call" | custom-call | tf_op jit(solution)/shard_map/move_blocks/pallas_call | solution.py:109
  216.7 2.6 fusion.9
  223.6 2.3 copy.48
  231.4 3.9 fusion.150
  240.3 2.3 collective-permute-done.22
  249.5 2.3 convert_reduce_fusion.7
  251.7 15.6 %collective-permute-done.34 = bf16[512,1152]{1,0:T(8,128)(2,1)S(1)} collective-permute-done((bf16[512,1152]{1,0:T(8,128)(2,1)S(1)}, bf16[512,1152]{1,0:T(8,128)(2,1)S(1)}, u32[]{:S(2)}, u32[]{:S(2)}) %collective-permute-start.34) | collective-permute-done | bytes 1179680 | tf_op jit(solution)/shard_map/ppermute | solution.py:53
  268.4 3.9 convert_reduce_fusion.6
  272.4 3.9 convolution_convert_fusion.6
  280.9 2.7 convolution_add_fusion.5
  283.6 26.1 %collective-permute-done.27 = bf16[640,1152]{1,0:T(8,128)(2,1)} collective-permute-done((bf16[640,1152]{1,0:T(8,128)(2,1)S(1)}, bf16[640,1152]{1,0:T(8,128)(2,1)}, u32[]{:S(2)}, u32[]{:S(2)}) %collective-permute-start.27) | collective-permute-done | bytes 1474592 | tf_op jit(solution)/shard_map/ppermute | solution.py:54
  309.7 3.9 convert_reduce_fusion.2
  314.0 2.8 convolution_add_fusion.6
  316.8 2.5 convert_reduce_fusion.3
  324.8 2.7 fusion.154
  330.1 2.3 fusion.138
  333.8 3.3 fusion.140
  340.6 2.3 convolution_convert_fusion.2
  347.8 2.5 convert_reduce_fusion.5
  351.1 3.6 convolution_convert_fusion.10
  356.8 3.5 convolution_convert_fusion.11
  365.5 5.8 convolution_convert_fusion
  373.4 2.9 fusion.31
  379.3 4.5 fusion.141
  388.0 2.9 fusion.66
  398.3 12.9 %pad_maximum_fusion.refs_1_ = bf16[4608,1152]{1,0:T(8,128)(2,1)S(1)} fusion(bf16[1152,1152]{1,0:T(8,128)(2,1)S(1)} %convolution_convert_fusion.1, bf16[3456,1152]{1,0:T(8,128)(2,1)} %convolution_convert_fusion), kind=kLoop, calls=%fused_computation.1 | loop fusion | flops 21233664 | bytes 21233664 | tf_op jit(solution)/shard_map/concatenate | solution.py:356
  416.4 15.4 %move_blocks.3 = (bf16[384,1152]{1,0:T(8,128)(2,1)S(1)}, bf16[384,1152]{1,0:T(8,128)(2,1)S(1)}, bf16[384,1152]{1,0:T(8,128)(2,1)S(1)}, bf16[384,1152]{1,0:T(8,12...) custom-call(s32[96]{0:T(128)S(1)} %stack.463.refs_0_, ...), custom_call_target="tpu_custom_call" | custom-call | tf_op jit(solution)/shard_map/move_blocks/pallas_call | solution.py:109
  437.4 39.8 %all-reduce.5 = f32[9216]{0:T(1024)} all-reduce(f32[9216]{0:T(1024)} %copy-done.117), channel_id=2, replica_groups=mesh['dp'=16,'mod'=2] {'dp','mod'}, use_global_device_ids=true, to_apply=%region_21.22.clone | all-reduce | flops 9216 | bytes 73728
  478.6 2.3 collective-permute-start.45
  485.9 3.3 fusion.22
  490.9 2.6 fusion.25
  493.6 8.8 %collective-permute-done.46 = bf16[32,3456]{1,0:T(8,128)(2,1)S(1)} collective-permute-done((bf16[32,3456]{1,0:T(8,128)(2,1)S(1)}, bf16[32,3456]{1,0:T(8,128)(2,1)S(1)}, u32[]{:S(2)}, u32[]{:S(2)}) %collective-permute-start.46) | collective-permute-done | bytes 221216 | tf_op jit(solution)/shard_map/ppermute | solution.py:54
  505.8 14.2 %collective-permute-done.81 = bf16[128,1152]{1,0:T(8,128)(2,1)S(1)} collective-permute-done((bf16[128,1152]{1,0:T(8,128)(2,1)S(1)}, bf16[128,1152]{1,0:T(8,128)(2,1)S(1)}, u32[]{:S(2)}, u32[]{:S(2)}) %collective-permute-start.81) | collective-permute-done | bytes 294944 | tf_op jit(solution)/shard_map/ppermute | solution.py:54
  520.5 15.6 %collective-permute-done.73 = bf16[128,1152]{1,0:T(8,128)(2,1)S(1)} collective-permute-done((bf16[128,1152]{1,0:T(8,128)(2,1)S(1)}, bf16[128,1152]{1,0:T(8,128)(2,1)S(1)}, u32[]{:S(2)}, u32[]{:S(2)}) %collective-permute-start.73) | collective-permute-done | bytes 294944 | tf_op jit(solution)/shard_map/ppermute | solution.py:54
  536.1 12.1 %collective-permute-done.47 = bf16[64,3456]{1,0:T(8,128)(2,1)S(1)} collective-permute-done((bf16[64,3456]{1,0:T(8,128)(2,1)S(1)}, bf16[64,3456]{1,0:T(8,128)(2,1)S(1)}, u32[]{:S(2)}, u32[]{:S(2)}) %collective-permute-start.47) | collective-permute-done | bytes 442400 | tf_op jit(solution)/shard_map/ppermute | solution.py:54
  553.9 2.9 collective-permute-done.82
  558.6 3.6 collective-permute-done.74
  563.3 4.3 collective-permute-done.76
  567.9 15.2 %collective-permute-done.68 = bf16[320,1152]{1,0:T(8,128)(2,1)S(1)} collective-permute-done((bf16[320,1152]{1,0:T(8,128)(2,1)S(1)}, bf16[320,1152]{1,0:T(8,128)(2,1)S(1)}, u32[]{:S(2)}, u32[]{:S(2)}) %collective-permute-start.68) | collective-permute-done | bytes 737312 | tf_op jit(solution)/shard_map/ppermute | solution.py:54
  584.1 17.7 %collective-permute-done.77 = bf16[160,1152]{1,0:T(8,128)(2,1)S(1)} collective-permute-done((bf16[160,1152]{1,0:T(8,128)(2,1)S(1)}, bf16[160,1152]{1,0:T(8,128)(2,1)S(1)}, u32[]{:S(2)}, u32[]{:S(2)}) %collective-permute-start.77) | collective-permute-done | bytes 368672 | tf_op jit(solution)/shard_map/ppermute | solution.py:54
  601.9 18.5 %collective-permute-done.69 = bf16[160,1152]{1,0:T(8,128)(2,1)S(1)} collective-permute-done((bf16[160,1152]{1,0:T(8,128)(2,1)S(1)}, bf16[160,1152]{1,0:T(8,128)(2,1)S(1)}, u32[]{:S(2)}, u32[]{:S(2)}) %collective-permute-start.69) | collective-permute-done | bytes 368672 | tf_op jit(solution)/shard_map/ppermute | solution.py:54
  622.6 4.7 collective-permute-done.78
  629.1 4.3 collective-permute-done.70
  637.7 15.8 %collective-permute-done.51 = bf16[384,1152]{1,0:T(8,128)(2,1)S(1)} collective-permute-done((bf16[384,1152]{1,0:T(8,128)(2,1)S(1)}, bf16[384,1152]{1,0:T(8,128)(2,1)S(1)}, u32[]{:S(2)}, u32[]{:S(2)}) %collective-permute-start.51) | collective-permute-done | bytes 884768 | tf_op jit(solution)/shard_map/ppermute | solution.py:54
  661.2 15.2 %collective-permute-done.63 = bf16[384,1152]{1,0:T(8,128)(2,1)} collective-permute-done((bf16[384,1152]{1,0:T(8,128)(2,1)}, bf16[384,1152]{1,0:T(8,128)(2,1)}, u32[]{:S(2)}, u32[]{:S(2)}) %collective-permute-start.63) | collective-permute-done | bytes 884768 | tf_op jit(solution)/shard_map/ppermute | solution.py:54
  680.9 2.4 fusion.97
  685.0 4.1 collective-permute-done.64
  692.0 7.0 collective-permute-done.59
  699.3 2.4 collective-permute-start.66
  (680 shorter events, 169.3 us)
Async XLA Ops:
  1.5 60.2 %collective-permute-start.41 = (bf16[16,1152]{1,0:T(8,128)(2,1)S(1)}, bf16[16,1152]{1,0:T(8,128)(2,1)S(1)}, u32[]{:S(2)}, u32[]{:S(2)}) collective-permute-start(bf16[16,1152]{1,0:T(8,128)(2,1)S(1)} %fusion.96), channel_id=1, source_target_pairs={{0,4},{2,6},{4,0},{6,2},{8,12},{10,14},{12,8},{14,10},{16,20},{18,... | collective-permute-start | bytes 110600 | tf_op jit(solution)/shard_map/ppermute | solution.py:54
  9.8 54.8 %collective-permute-start = (bf16[16,3456]{1,0:T(8,128)(2,1)S(1)}, bf16[16,3456]{1,0:T(8,128)(2,1)S(1)}, u32[]{:S(2)}, u32[]{:S(2)}) collective-permute-start(bf16[16,3456]{1,0:T(8,128)(2,1)S(1)} %fusion.12), channel_id=1, source_target_pairs={{0,1},{1,0},{2,3},{3,2},{4,5},{5,4},{6,7},{7,6},{8,9},{9,8},{10,11... | collective-permute-start | bytes 331784 | tf_op jit(solution)/shard_map/ppermute | solution.py:53
  11.4 94.5 %collective-permute-start.31 = (bf16[64,1152]{1,0:T(8,128)(2,1)S(1)}, bf16[64,1152]{1,0:T(8,128)(2,1)S(1)}, u32[]{:S(2)}, u32[]{:S(2)}) collective-permute-start(bf16[64,1152]{1,0:T(8,128)(2,1)S(1)} %slice.244), channel_id=1, source_target_pairs={{0,4},{2,6},{4,0},{6,2},{8,12},{10,14},{12,8},{14,10},{16,20},{18,... | collective-permute-start | bytes 442376 | tf_op jit(solution)/shard_map/ppermute | solution.py:54
  12.0 79.0 %collective-permute-start.28 = (bf16[64,1152]{1,0:T(8,128)(2,1)S(1)}, bf16[64,1152]{1,0:T(8,128)(2,1)S(1)}, u32[]{:S(2)}, u32[]{:S(2)}) collective-permute-start(bf16[64,1152]{1,0:T(8,128)(2,1)S(1)} %slice.242), channel_id=1, source_target_pairs={{0,4},{2,6},{4,0},{6,2},{8,12},{10,14},{12,8},{14,10},{16,20},{18,... | collective-permute-start | bytes 442376 | tf_op jit(solution)/shard_map/ppermute | solution.py:54
  13.6 92.5 %collective-permute-start.23 = (bf16[80,1152]{1,0:T(8,128)(2,1)S(1)}, bf16[80,1152]{1,0:T(8,128)(2,1)S(1)}, u32[]{:S(2)}, u32[]{:S(2)}) collective-permute-start(bf16[80,1152]{1,0:T(8,128)(2,1)S(1)} %slice.241), channel_id=1, source_target_pairs={{0,1},{1,0},{2,3},{3,2},{4,5},{5,4},{6,7},{7,6},{8,9},{9,8},{10,11... | collective-permute-start | bytes 552968 | tf_op jit(solution)/shard_map/ppermute | solution.py:53
  61.6 44.3 %collective-permute-start.20 = (bf16[80,1152]{1,0:T(8,128)(2,1)S(1)}, bf16[80,1152]{1,0:T(8,128)(2,1)S(1)}, u32[]{:S(2)}, u32[]{:S(2)}) collective-permute-start(bf16[80,1152]{1,0:T(8,128)(2,1)S(1)} %slice.238), channel_id=1, source_target_pairs={{0,1},{1,0},{2,3},{3,2},{4,5},{5,4},{6,7},{7,6},{8,9},{9,8},{10,11... | collective-permute-start | bytes 552968 | tf_op jit(solution)/shard_map/ppermute | solution.py:53
  76.2 7.8 %collective-permute-start.42 = (bf16[32,1152]{1,0:T(8,128)(2,1)S(1)}, bf16[32,1152]{1,0:T(8,128)(2,1)S(1)}, u32[]{:S(2)}, u32[]{:S(2)}) collective-permute-start(bf16[32,1152]{1,0:T(8,128)(2,1)S(1)} %pad_maximum_fusion.33), channel_id=1, source_target_pairs={{0,16},{2,18},{4,20},{6,22},{8,24},{10,26},{12,28},{14,30},{16,0},... | collective-permute-start | bytes 221192 | tf_op jit(solution)/shard_map/ppermute | solution.py:54
  91.0 18.1 %collective-permute-start.43 = (bf16[64,1152]{1,0:T(8,128)(2,1)S(1)}, bf16[64,1152]{1,0:T(8,128)(2,1)S(1)}, u32[]{:S(2)}, u32[]{:S(2)}) collective-permute-start(bf16[64,1152]{1,0:T(8,128)(2,1)S(1)} %pad_maximum_fusion.32), channel_id=1, source_target_pairs={{0,8},{2,10},{4,12},{6,14},{8,0},{10,2},{12,4},{14,6},{16,24},{18,... | collective-permute-start | bytes 442376 | tf_op jit(solution)/shard_map/ppermute | solution.py:54
  91.0 20.6 %collective-permute-start.10 = (bf16[96,1152]{1,0:T(8,128)(2,1)S(1)}, bf16[96,1152]{1,0:T(8,128)(2,1)S(1)}, u32[]{:S(2)}, u32[]{:S(2)}) collective-permute-start(bf16[96,1152]{1,0:T(8,128)(2,1)S(1)} %pad_maximum_fusion.30), channel_id=1, source_target_pairs={{0,4},{2,6},{4,0},{6,2},{8,12},{10,14},{12,8},{14,10},{16,20},{18,... | collective-permute-start | bytes 663560 | tf_op jit(solution)/shard_map/ppermute | solution.py:54
  106.0 22.0 %collective-permute-start.6 = (bf16[96,1152]{1,0:T(8,128)(2,1)S(1)}, bf16[96,1152]{1,0:T(8,128)(2,1)S(1)}, u32[]{:S(2)}, u32[]{:S(2)}) collective-permute-start(bf16[96,1152]{1,0:T(8,128)(2,1)S(1)} %pad_maximum_fusion.29), channel_id=1, source_target_pairs={{0,16},{2,18},{4,20},{6,22},{8,24},{10,26},{12,28},{14,30},{16,0},... | collective-permute-start | bytes 663560 | tf_op jit(solution)/shard_map/ppermute | solution.py:54
  106.1 39.9 %collective-permute-start.32 = (bf16[128,1152]{1,0:T(8,128)(2,1)S(1)}, bf16[128,1152]{1,0:T(8,128)(2,1)S(1)}, u32[]{:S(2)}, u32[]{:S(2)}) collective-permute-start(bf16[128,1152]{1,0:T(8,128)(2,1)S(1)} %pad_maximum_fusion.26), channel_id=1, source_target_pairs={{0,16},{2,18},{4,20},{6,22},{8,24},{10,26},{12,28},{14,30},{16,0},... | collective-permute-start | bytes 884744 | tf_op jit(solution)/shard_map/ppermute | solution.py:54
  109.1 37.5 %collective-permute-start.29 = (bf16[128,1152]{1,0:T(8,128)(2,1)S(1)}, bf16[128,1152]{1,0:T(8,128)(2,1)S(1)}, u32[]{:S(2)}, u32[]{:S(2)}) collective-permute-start(bf16[128,1152]{1,0:T(8,128)(2,1)S(1)} %pad_maximum_fusion.25), channel_id=1, source_target_pairs={{0,16},{2,18},{4,20},{6,22},{8,24},{10,26},{12,28},{14,30},{16,0},... | collective-permute-start | bytes 884744 | tf_op jit(solution)/shard_map/ppermute | solution.py:54
  111.6 37.1 %collective-permute-start.24 = (bf16[160,1152]{1,0:T(8,128)(2,1)S(1)}, bf16[160,1152]{1,0:T(8,128)(2,1)S(1)}, u32[]{:S(2)}, u32[]{:S(2)}) collective-permute-start(bf16[160,1152]{1,0:T(8,128)(2,1)S(1)} %pad_maximum_fusion.24), channel_id=1, source_target_pairs={{0,16},{2,18},{4,20},{6,22},{8,24},{10,26},{12,28},{14,30},{16,0},... | collective-permute-start | bytes 1105928 | tf_op jit(solution)/shard_map/ppermute | solution.py:54
  112.3 15.7 %collective-permute-start.11 = (bf16[192,1152]{1,0:T(8,128)(2,1)S(1)}, bf16[192,1152]{1,0:T(8,128)(2,1)S(1)}, u32[]{:S(2)}, u32[]{:S(2)}) collective-permute-start(bf16[192,1152]{1,0:T(8,128)(2,1)S(1)} %pad_maximum_fusion.21), channel_id=1, source_target_pairs={{0,1},{1,0},{2,3},{3,2},{4,5},{5,4},{6,7},{7,6},{8,9},{9,8},{10,11... | collective-permute-start | bytes 1327112 | tf_op jit(solution)/shard_map/ppermute | solution.py:53
  127.9 17.8 %collective-permute-start.3 = (bf16[192,1152]{1,0:T(8,128)(2,1)S(1)}, bf16[192,1152]{1,0:T(8,128)(2,1)S(1)}, u32[]{:S(2)}, u32[]{:S(2)}) collective-permute-start(bf16[192,1152]{1,0:T(8,128)(2,1)S(1)} %pad_maximum_fusion.19), channel_id=1, source_target_pairs={{0,8},{2,10},{4,12},{6,14},{8,0},{10,2},{12,4},{14,6},{16,24},{18,... | collective-permute-start | bytes 1327112 | tf_op jit(solution)/shard_map/ppermute | solution.py:54
  128.0 17.9 %collective-permute-start.7 = (bf16[192,1152]{1,0:T(8,128)(2,1)S(1)}, bf16[192,1152]{1,0:T(8,128)(2,1)S(1)}, u32[]{:S(2)}, u32[]{:S(2)}) collective-permute-start(bf16[192,1152]{1,0:T(8,128)(2,1)S(1)} %pad_maximum_fusion.20), channel_id=1, source_target_pairs={{0,4},{2,6},{4,0},{6,2},{8,12},{10,14},{12,8},{14,10},{16,20},{18,... | collective-permute-start | bytes 1327112 | tf_op jit(solution)/shard_map/ppermute | solution.py:54
  145.9 19.2 %collective-permute-start.21 = (bf16[160,1152]{1,0:T(8,128)(2,1)S(1)}, bf16[160,1152]{1,0:T(8,128)(2,1)S(1)}, u32[]{:S(2)}, u32[]{:S(2)}) collective-permute-start(bf16[160,1152]{1,0:T(8,128)(2,1)S(1)} %pad_maximum_fusion.23), channel_id=1, source_target_pairs={{0,16},{2,18},{4,20},{6,22},{8,24},{10,26},{12,28},{14,30},{16,0},... | collective-permute-start | bytes 1105928 | tf_op jit(solution)/shard_map/ppermute | solution.py:54
  146.1 44.8 %collective-permute-start.15 = (bf16[384,1152]{1,0:T(8,128)(2,1)S(1)}, bf16[384,1152]{1,0:T(8,128)(2,1)S(1)}, u32[]{:S(2)}, u32[]{:S(2)}) collective-permute-start(bf16[384,1152]{1,0:T(8,128)(2,1)S(1)} %pad_maximum_fusion.9.refs_3_), channel_id=1, source_target_pairs={{0,2},{2,0},{4,6},{6,4},{8,10},{10,8},{12,14},{14,12},{16,18},{18,... | collective-permute-start | bytes 2654216 | tf_op jit(solution)/shard_map/ppermute | solution.py:54
  146.6 44.7 %collective-permute-start.8 = (bf16[384,1152]{1,0:T(8,128)(2,1)S(1)}, bf16[384,1152]{1,0:T(8,128)(2,1)S(1)}, u32[]{:S(2)}, u32[]{:S(2)}) collective-permute-start(bf16[384,1152]{1,0:T(8,128)(2,1)S(1)} %pad_maximum_fusion.9.refs_3_), channel_id=1, source_target_pairs={{0,1},{1,0},{2,3},{3,2},{4,5},{5,4},{6,7},{7,6},{8,9},{9,8},{10,11... | collective-permute-start | bytes 2654216 | tf_op jit(solution)/shard_map/ppermute | solution.py:53
  147.6 43.8 %collective-permute-start.4 = (bf16[384,1152]{1,0:T(8,128)(2,1)S(1)}, bf16[384,1152]{1,0:T(8,128)(2,1)S(1)}, u32[]{:S(2)}, u32[]{:S(2)}) collective-permute-start(bf16[384,1152]{1,0:T(8,128)(2,1)S(1)} %pad_maximum_fusion.8.refs_1_), channel_id=1, source_target_pairs={{0,4},{2,6},{4,0},{6,2},{8,12},{10,14},{12,8},{14,10},{16,20},{18,... | collective-permute-start | bytes 2654216 | tf_op jit(solution)/shard_map/ppermute | solution.py:54
  148.7 43.2 %collective-permute-start.12 = (bf16[384,1152]{1,0:T(8,128)(2,1)S(1)}, bf16[384,1152]{1,0:T(8,128)(2,1)S(1)}, u32[]{:S(2)}, u32[]{:S(2)}) collective-permute-start(bf16[384,1152]{1,0:T(8,128)(2,1)S(1)} %pad_maximum_fusion.10.refs_5_), channel_id=1, source_target_pairs={{0,8},{2,10},{4,12},{6,14},{8,0},{10,2},{12,4},{14,6},{16,24},{18,... | collective-permute-start | bytes 2654216 | tf_op jit(solution)/shard_map/ppermute | solution.py:54
  165.1 25.7 %collective-permute-start.33 = (bf16[256,1152]{1,0:T(8,128)(2,1)S(1)}, bf16[256,1152]{1,0:T(8,128)(2,1)S(1)}, u32[]{:S(2)}, u32[]{:S(2)}) collective-permute-start(bf16[256,1152]{1,0:T(8,128)(2,1)S(1)} %pad_maximum_fusion.18), channel_id=1, source_target_pairs={{0,8},{2,10},{4,12},{6,14},{8,0},{10,2},{12,4},{14,6},{16,24},{18,... | collective-permute-start | bytes 1769480 | tf_op jit(solution)/shard_map/ppermute | solution.py:54
  195.1 42.7 %collective-permute-start.30 = (bf16[256,1152]{1,0:T(8,128)(2,1)}, bf16[256,1152]{1,0:T(8,128)(2,1)}, u32[]{:S(2)}, u32[]{:S(2)}) collective-permute-start(bf16[256,1152]{1,0:T(8,128)(2,1)} %pad_maximum_fusion.17), channel_id=1, source_target_pairs={{0,8},{2,10},{4,12},{6,14},{8,0},{10,2},{12,4},{14,6},{16,24},{18,... | collective-permute-start | bytes 1769480 | tf_op jit(solution)/shard_map/ppermute | solution.py:54
  195.2 49.3 %collective-permute-start.25 = (bf16[320,1152]{1,0:T(8,128)(2,1)}, bf16[320,1152]{1,0:T(8,128)(2,1)}, u32[]{:S(2)}, u32[]{:S(2)}) collective-permute-start(bf16[320,1152]{1,0:T(8,128)(2,1)} %pad_maximum_fusion.13), channel_id=1, source_target_pairs={{0,8},{2,10},{4,12},{6,14},{8,0},{10,2},{12,4},{14,6},{16,24},{18,... | collective-permute-start | bytes 2211848 | tf_op jit(solution)/shard_map/ppermute | solution.py:54
  197.2 45.4 %collective-permute-start.22 = (bf16[320,1152]{1,0:T(8,128)(2,1)}, bf16[320,1152]{1,0:T(8,128)(2,1)S(1)}, u32[]{:S(2)}, u32[]{:S(2)}) collective-permute-start(bf16[320,1152]{1,0:T(8,128)(2,1)} %pad_maximum_fusion.12), channel_id=1, source_target_pairs={{0,8},{2,10},{4,12},{6,14},{8,0},{10,2},{12,4},{14,6},{16,24},{18,... | collective-permute-start | bytes 2211848 | tf_op jit(solution)/shard_map/ppermute | solution.py:54
  197.3 71.1 %collective-permute-start.35 = (bf16[512,1152]{1,0:T(8,128)(2,1)}, bf16[512,1152]{1,0:T(8,128)(2,1)}, u32[]{:S(2)}, u32[]{:S(2)}) collective-permute-start(bf16[512,1152]{1,0:T(8,128)(2,1)} %pad_maximum_fusion.6), channel_id=1, source_target_pairs={{0,1},{1,0},{2,3},{3,2},{4,5},{5,4},{6,7},{7,6},{8,9},{9,8},{10,11... | collective-permute-start | bytes 3538952 | tf_op jit(solution)/shard_map/ppermute | solution.py:53
  237.6 8.3 %collective-permute-start.19 = (bf16[256,1152]{1,0:T(8,128)(2,1)S(1)}, bf16[256,1152]{1,0:T(8,128)(2,1)S(1)}, u32[]{:S(2)}, u32[]{:S(2)}) collective-permute-start(bf16[256,1152]{1,0:T(8,128)(2,1)S(1)} %get-tuple-element.50), channel_id=1, source_target_pairs={{0,2},{2,0},{4,6},{6,4},{8,10},{10,8},{12,14},{14,12},{16,18},{18,... | collective-permute-start | bytes 1769480 | tf_op jit(solution)/shard_map/ppermute | solution.py:54
  239.2 28.1 %collective-permute-start.34 = (bf16[512,1152]{1,0:T(8,128)(2,1)S(1)}, bf16[512,1152]{1,0:T(8,128)(2,1)S(1)}, u32[]{:S(2)}, u32[]{:S(2)}) collective-permute-start(bf16[512,1152]{1,0:T(8,128)(2,1)S(1)} %pad_maximum_fusion.5), channel_id=1, source_target_pairs={{0,1},{1,0},{2,3},{3,2},{4,5},{5,4},{6,7},{7,6},{8,9},{9,8},{10,11... | collective-permute-start | bytes 3538952 | tf_op jit(solution)/shard_map/ppermute | solution.py:53
  243.9 36.9 %collective-permute-start.26 = (bf16[640,1152]{1,0:T(8,128)(2,1)}, bf16[640,1152]{1,0:T(8,128)(2,1)}, u32[]{:S(2)}, u32[]{:S(2)}) collective-permute-start(bf16[640,1152]{1,0:T(8,128)(2,1)} %pad_maximum_fusion.2), channel_id=1, source_target_pairs={{0,4},{2,6},{4,0},{6,2},{8,12},{10,14},{12,8},{14,10},{16,20},{18,... | collective-permute-start | bytes 4423688 | tf_op jit(solution)/shard_map/ppermute | solution.py:54
  245.9 63.8 %collective-permute-start.27 = (bf16[640,1152]{1,0:T(8,128)(2,1)S(1)}, bf16[640,1152]{1,0:T(8,128)(2,1)}, u32[]{:S(2)}, u32[]{:S(2)}) collective-permute-start(bf16[640,1152]{1,0:T(8,128)(2,1)S(1)} %pad_maximum_fusion.3), channel_id=1, source_target_pairs={{0,4},{2,6},{4,0},{6,2},{8,12},{10,14},{12,8},{14,10},{16,20},{18,... | collective-permute-start | bytes 4423688 | tf_op jit(solution)/shard_map/ppermute | solution.py:54
  276.3 97.1 %collective-permute-start.79 = (bf16[512,1152]{1,0:T(8,128)(2,1)}, bf16[512,1152]{1,0:T(8,128)(2,1)}, u32[]{:S(2)}, u32[]{:S(2)}) collective-permute-start(bf16[512,1152]{1,0:T(8,128)(2,1)} %convolution_convert_fusion.6), channel_id=1, source_target_pairs={{0,1},{1,0},{2,3},{3,2},{4,5},{5,4},{6,7},{7,6},{8,9},{9,8},{10,11... | collective-permute-start | bytes 3538952 | tf_op jit(solution)/shard_map/ppermute | solution.py:53
  279.2 104.6 %collective-permute-start.71 = (bf16[512,1152]{1,0:T(8,128)(2,1)}, bf16[512,1152]{1,0:T(8,128)(2,1)}, u32[]{:S(2)}, u32[]{:S(2)}) collective-permute-start(bf16[512,1152]{1,0:T(8,128)(2,1)} %convolution_convert_fusion.8), channel_id=1, source_target_pairs={{0,1},{1,0},{2,3},{3,2},{4,5},{5,4},{6,7},{7,6},{8,9},{9,8},{10,11... | collective-permute-start | bytes 3538952 | tf_op jit(solution)/shard_map/ppermute | solution.py:53
  329.0 16.6 %collective-permute-start.38 = (f32[256,1152]{1,0:T(8,128)S(1)}, f32[256,1152]{1,0:T(8,128)S(1)}, u32[]{:S(2)}, u32[]{:S(2)}) collective-permute-start(f32[256,1152]{1,0:T(8,128)S(1)} %slice.313), channel_id=1, source_target_pairs={{0,2},{2,0},{4,6},{6,4},{8,10},{10,8},{12,14},{14,12},{16,18},{18,... | collective-permute-start | bytes 3538952 | tf_op jit(solution)/shard_map/ppermute | solution.py:54
  338.6 9.1 %collective-permute-start.36 = (f32[256,1152]{1,0:T(8,128)S(1)}, f32[256,1152]{1,0:T(8,128)S(1)}, u32[]{:S(2)}, u32[]{:S(2)}) collective-permute-start(f32[256,1152]{1,0:T(8,128)S(1)} %slice.310), channel_id=1, source_target_pairs={{0,2},{2,0},{4,6},{6,4},{8,10},{10,8},{12,14},{14,12},{16,18},{18,... | collective-permute-start | bytes 3538952 | tf_op jit(solution)/shard_map/ppermute | solution.py:54
  342.9 142.5 %collective-permute-start.75 = (bf16[640,1152]{1,0:T(8,128)(2,1)}, bf16[640,1152]{1,0:T(8,128)(2,1)}, u32[]{:S(2)}, u32[]{:S(2)}) collective-permute-start(bf16[640,1152]{1,0:T(8,128)(2,1)} %convolution_convert_fusion.2), channel_id=1, source_target_pairs={{0,4},{2,6},{4,0},{6,2},{8,12},{10,14},{12,8},{14,10},{16,20},{18,... | collective-permute-start | bytes 4423688 | tf_op jit(solution)/shard_map/ppermute | solution.py:54
  345.6 143.7 %collective-permute-start.67 = (bf16[640,1152]{1,0:T(8,128)(2,1)}, bf16[640,1152]{1,0:T(8,128)(2,1)}, u32[]{:S(2)}, u32[]{:S(2)}) collective-permute-start(bf16[640,1152]{1,0:T(8,128)(2,1)} %convolution_convert_fusion.4), channel_id=1, source_target_pairs={{0,4},{2,6},{4,0},{6,2},{8,12},{10,14},{12,8},{14,10},{16,20},{18,... | collective-permute-start | bytes 4423688 | tf_op jit(solution)/shard_map/ppermute | solution.py:54
  377.2 125.3 %collective-permute-start.80 = (bf16[256,1152]{1,0:T(8,128)(2,1)}, bf16[256,1152]{1,0:T(8,128)(2,1)}, u32[]{:S(2)}, u32[]{:S(2)}) collective-permute-start(bf16[256,1152]{1,0:T(8,128)(2,1)} %slice.355), channel_id=1, source_target_pairs={{0,8},{2,10},{4,12},{6,14},{8,0},{10,2},{12,4},{14,6},{16,24},{18,... | collective-permute-start | bytes 1769480 | tf_op jit(solution)/shard_map/ppermute | solution.py:54
  386.9 117.5 %collective-permute-start.72 = (bf16[256,1152]{1,0:T(8,128)(2,1)}, bf16[256,1152]{1,0:T(8,128)(2,1)}, u32[]{:S(2)}, u32[]{:S(2)}) collective-permute-start(bf16[256,1152]{1,0:T(8,128)(2,1)} %slice.343), channel_id=1, source_target_pairs={{0,8},{2,10},{4,12},{6,14},{8,0},{10,2},{12,4},{14,6},{16,24},{18,... | collective-permute-start | bytes 1769480 | tf_op jit(solution)/shard_map/ppermute | solution.py:54
  396.7 14.6 %collective-permute-start.39 = (bf16[16,3456]{1,0:T(8,128)(2,1)S(1)}, bf16[16,3456]{1,0:T(8,128)(2,1)S(1)}, u32[]{:S(2)}, u32[]{:S(2)}) collective-permute-start(bf16[16,3456]{1,0:T(8,128)(2,1)S(1)} %broadcast_select_fusion), channel_id=1, source_target_pairs={{0,1},{1,0},{2,3},{3,2},{4,5},{5,4},{6,7},{7,6},{8,9},{9,8},{10,11... | collective-permute-start | bytes 331784 | tf_op jit(solution)/shard_map/ppermute | solution.py:53
  414.8 63.8 %collective-permute-start.40 = (bf16[8,1152]{1,0:T(8,128)(2,1)}, bf16[8,1152]{1,0:T(8,128)(2,1)}, u32[]{:S(2)}, u32[]{:S(2)}) collective-permute-start(bf16[8,1152]{1,0:T(8,128)(2,1)} %select_convert_fusion), channel_id=1, source_target_pairs={{0,1},{1,0},{2,3},{3,2},{4,5},{5,4},{6,7},{7,6},{8,9},{9,8},{10,11... | collective-permute-start | bytes 55304 | tf_op jit(solution)/shard_map/ppermute | solution.py:53
  483.8 152.8 %collective-permute-start.49 = (bf16[384,1152]{1,0:T(8,128)(2,1)}, bf16[384,1152]{1,0:T(8,128)(2,1)S(1)}, u32[]{:S(2)}, u32[]{:S(2)}) collective-permute-start(bf16[384,1152]{1,0:T(8,128)(2,1)} %copy-done.7), channel_id=1, source_target_pairs={{0,2},{2,0},{4,6},{6,4},{8,10},{10,8},{12,14},{14,12},{16,18},{18,... | collective-permute-start | bytes 2654216 | tf_op jit(solution)/shard_map/ppermute | solution.py:54
  485.4 34.8 %collective-permute-start.50 = (bf16[384,1152]{1,0:T(8,128)(2,1)}, bf16[384,1152]{1,0:T(8,128)(2,1)S(1)}, u32[]{:S(2)}, u32[]{:S(2)}) collective-permute-start(bf16[384,1152]{1,0:T(8,128)(2,1)} %copy-done.12), channel_id=1, source_target_pairs={{0,2},{2,0},{4,6},{6,4},{8,10},{10,8},{12,14},{14,12},{16,18},{18,... | collective-permute-start | bytes 2654216 | tf_op jit(solution)/shard_map/ppermute | solution.py:54
  489.4 13.1 %collective-permute-start.46 = (bf16[32,3456]{1,0:T(8,128)(2,1)S(1)}, bf16[32,3456]{1,0:T(8,128)(2,1)S(1)}, u32[]{:S(2)}, u32[]{:S(2)}) collective-permute-start(bf16[32,3456]{1,0:T(8,128)(2,1)S(1)} %pad_maximum_fusion.31), channel_id=1, source_target_pairs={{0,16},{2,18},{4,20},{6,22},{8,24},{10,26},{12,28},{14,30},{16,0},... | collective-permute-start | bytes 663560 | tf_op jit(solution)/shard_map/ppermute | solution.py:54
  502.4 155.7 %collective-permute-start.55 = (bf16[384,1152]{1,0:T(8,128)(2,1)}, bf16[384,1152]{1,0:T(8,128)(2,1)}, u32[]{:S(2)}, u32[]{:S(2)}) collective-permute-start(bf16[384,1152]{1,0:T(8,128)(2,1)} %get-tuple-element.26), channel_id=1, source_target_pairs={{0,2},{2,0},{4,6},{6,4},{8,10},{10,8},{12,14},{14,12},{16,18},{18,... | collective-permute-start | bytes 2654216 | tf_op jit(solution)/shard_map/ppermute | solution.py:54
  502.5 45.8 %collective-permute-start.56 = (bf16[384,1152]{1,0:T(8,128)(2,1)S(1)}, bf16[384,1152]{1,0:T(8,128)(2,1)S(1)}, u32[]{:S(2)}, u32[]{:S(2)}) collective-permute-start(bf16[384,1152]{1,0:T(8,128)(2,1)S(1)} %copy-done.11), channel_id=1, source_target_pairs={{0,2},{2,0},{4,6},{6,4},{8,10},{10,8},{12,14},{14,12},{16,18},{18,... | collective-permute-start | bytes 2654216 | tf_op jit(solution)/shard_map/ppermute | solution.py:54
  504.4 15.6 %collective-permute-start.81 = (bf16[128,1152]{1,0:T(8,128)(2,1)S(1)}, bf16[128,1152]{1,0:T(8,128)(2,1)S(1)}, u32[]{:S(2)}, u32[]{:S(2)}) collective-permute-start(bf16[128,1152]{1,0:T(8,128)(2,1)S(1)} %slice.357), channel_id=1, source_target_pairs={{0,16},{2,18},{4,20},{6,22},{8,24},{10,26},{12,28},{14,30},{16,0},... | collective-permute-start | bytes 884744 | tf_op jit(solution)/shard_map/ppermute | solution.py:54
  520.0 141.2 %collective-permute-start.61 = (bf16[384,1152]{1,0:T(8,128)(2,1)}, bf16[384,1152]{1,0:T(8,128)(2,1)}, u32[]{:S(2)}, u32[]{:S(2)}) collective-permute-start(bf16[384,1152]{1,0:T(8,128)(2,1)} %get-tuple-element.30), channel_id=1, source_target_pairs={{0,2},{2,0},{4,6},{6,4},{8,10},{10,8},{12,14},{14,12},{16,18},{18,... | collective-permute-start | bytes 2654216 | tf_op jit(solution)/shard_map/ppermute | solution.py:54
  520.2 15.9 %collective-permute-start.73 = (bf16[128,1152]{1,0:T(8,128)(2,1)S(1)}, bf16[128,1152]{1,0:T(8,128)(2,1)S(1)}, u32[]{:S(2)}, u32[]{:S(2)}) collective-permute-start(bf16[128,1152]{1,0:T(8,128)(2,1)S(1)} %slice.345), channel_id=1, source_target_pairs={{0,16},{2,18},{4,20},{6,22},{8,24},{10,26},{12,28},{14,30},{16,0},... | collective-permute-start | bytes 884744 | tf_op jit(solution)/shard_map/ppermute | solution.py:54
  536.0 12.1 %collective-permute-start.47 = (bf16[64,3456]{1,0:T(8,128)(2,1)S(1)}, bf16[64,3456]{1,0:T(8,128)(2,1)S(1)}, u32[]{:S(2)}, u32[]{:S(2)}) collective-permute-start(bf16[64,3456]{1,0:T(8,128)(2,1)S(1)} %pad_maximum_fusion.22), channel_id=1, source_target_pairs={{0,8},{2,10},{4,12},{6,14},{8,0},{10,2},{12,4},{14,6},{16,24},{18,... | collective-permute-start | bytes 1327112 | tf_op jit(solution)/shard_map/ppermute | solution.py:54
  548.3 19.3 %collective-permute-start.76 = (bf16[320,1152]{1,0:T(8,128)(2,1)S(1)}, bf16[320,1152]{1,0:T(8,128)(2,1)S(1)}, u32[]{:S(2)}, u32[]{:S(2)}) collective-permute-start(bf16[320,1152]{1,0:T(8,128)(2,1)S(1)} %slice.349), channel_id=1, source_target_pairs={{0,8},{2,10},{4,12},{6,14},{8,0},{10,2},{12,4},{14,6},{16,24},{18,... | collective-permute-start | bytes 2211848 | tf_op jit(solution)/shard_map/ppermute | solution.py:54
  562.2 20.9 %collective-permute-start.68 = (bf16[320,1152]{1,0:T(8,128)(2,1)S(1)}, bf16[320,1152]{1,0:T(8,128)(2,1)S(1)}, u32[]{:S(2)}, u32[]{:S(2)}) collective-permute-start(bf16[320,1152]{1,0:T(8,128)(2,1)S(1)} %slice.337), channel_id=1, source_target_pairs={{0,8},{2,10},{4,12},{6,14},{8,0},{10,2},{12,4},{14,6},{16,24},{18,... | collective-permute-start | bytes 2211848 | tf_op jit(solution)/shard_map/ppermute | solution.py:54
  567.6 86.1 %collective-permute-start.48 = (bf16[128,3456]{1,0:T(8,128)(2,1)S(1)}, bf16[128,3456]{1,0:T(8,128)(2,1)S(1)}, u32[]{:S(2)}, u32[]{:S(2)}) collective-permute-start(bf16[128,3456]{1,0:T(8,128)(2,1)S(1)} %pad_maximum_fusion.11), channel_id=1, source_target_pairs={{0,2},{2,0},{4,6},{6,4},{8,10},{10,8},{12,14},{14,12},{16,18},{18,... | collective-permute-start | bytes 2654216 | tf_op jit(solution)/shard_map/ppermute | solution.py:54
  583.1 18.7 %collective-permute-start.77 = (bf16[160,1152]{1,0:T(8,128)(2,1)S(1)}, bf16[160,1152]{1,0:T(8,128)(2,1)S(1)}, u32[]{:S(2)}, u32[]{:S(2)}) collective-permute-start(bf16[160,1152]{1,0:T(8,128)(2,1)S(1)} %slice.351), channel_id=1, source_target_pairs={{0,16},{2,18},{4,20},{6,22},{8,24},{10,26},{12,28},{14,30},{16,0},... | collective-permute-start | bytes 1105928 | tf_op jit(solution)/shard_map/ppermute | solution.py:54
  601.8 18.6 %collective-permute-start.69 = (bf16[160,1152]{1,0:T(8,128)(2,1)S(1)}, bf16[160,1152]{1,0:T(8,128)(2,1)S(1)}, u32[]{:S(2)}, u32[]{:S(2)}) collective-permute-start(bf16[160,1152]{1,0:T(8,128)(2,1)S(1)} %slice.339), channel_id=1, source_target_pairs={{0,16},{2,18},{4,20},{6,22},{8,24},{10,26},{12,28},{14,30},{16,0},... | collective-permute-start | bytes 1105928 | tf_op jit(solution)/shard_map/ppermute | solution.py:54
  633.3 20.1 %collective-permute-start.51 = (bf16[384,1152]{1,0:T(8,128)(2,1)S(1)}, bf16[384,1152]{1,0:T(8,128)(2,1)S(1)}, u32[]{:S(2)}, u32[]{:S(2)}) collective-permute-start(bf16[384,1152]{1,0:T(8,128)(2,1)S(1)} %add_convert_fusion.7), channel_id=1, source_target_pairs={{0,4},{2,6},{4,0},{6,2},{8,12},{10,14},{12,8},{14,10},{16,20},{18,... | collective-permute-start | bytes 2654216 | tf_op jit(solution)/shard_map/ppermute | solution.py:54
  636.6 21.6 %collective-permute-start.57 = (bf16[384,1152]{1,0:T(8,128)(2,1)}, bf16[384,1152]{1,0:T(8,128)(2,1)}, u32[]{:S(2)}, u32[]{:S(2)}) collective-permute-start(bf16[384,1152]{1,0:T(8,128)(2,1)} %add_convert_fusion.4), channel_id=1, source_target_pairs={{0,1},{1,0},{2,3},{3,2},{4,5},{5,4},{6,7},{7,6},{8,9},{9,8},{10,11... | collective-permute-start | bytes 2654216 | tf_op jit(solution)/shard_map/ppermute | solution.py:53
  653.5 22.9 %collective-permute-start.63 = (bf16[384,1152]{1,0:T(8,128)(2,1)}, bf16[384,1152]{1,0:T(8,128)(2,1)}, u32[]{:S(2)}, u32[]{:S(2)}) collective-permute-start(bf16[384,1152]{1,0:T(8,128)(2,1)} %add_convert_fusion.1), channel_id=1, source_target_pairs={{0,8},{2,10},{4,12},{6,14},{8,0},{10,2},{12,4},{14,6},{16,24},{18,... | collective-permute-start | bytes 2654216 | tf_op jit(solution)/shard_map/ppermute | solution.py:54
  656.1 27.2 %collective-permute-start.52 = (bf16[192,1152]{1,0:T(8,128)(2,1)S(1)}, bf16[192,1152]{1,0:T(8,128)(2,1)S(1)}, u32[]{:S(2)}, u32[]{:S(2)}) collective-permute-start(bf16[192,1152]{1,0:T(8,128)(2,1)S(1)} %slice.319), channel_id=1, source_target_pairs={{0,8},{2,10},{4,12},{6,14},{8,0},{10,2},{12,4},{14,6},{16,24},{18,... | collective-permute-start | bytes 1327112 | tf_op jit(solution)/shard_map/ppermute | solution.py:54
  660.0 24.3 %collective-permute-start.58 = (bf16[192,1152]{1,0:T(8,128)(2,1)S(1)}, bf16[192,1152]{1,0:T(8,128)(2,1)S(1)}, u32[]{:S(2)}, u32[]{:S(2)}) collective-permute-start(bf16[192,1152]{1,0:T(8,128)(2,1)S(1)} %slice.325), channel_id=1, source_target_pairs={{0,4},{2,6},{4,0},{6,2},{8,12},{10,14},{12,8},{14,10},{16,20},{18,... | collective-permute-start | bytes 1327112 | tf_op jit(solution)/shard_map/ppermute | solution.py:54
  678.4 10.7 %collective-permute-start.64 = (bf16[192,1152]{1,0:T(8,128)(2,1)S(1)}, bf16[192,1152]{1,0:T(8,128)(2,1)S(1)}, u32[]{:S(2)}, u32[]{:S(2)}) collective-permute-start(bf16[192,1152]{1,0:T(8,128)(2,1)S(1)} %slice.331), channel_id=1, source_target_pairs={{0,1},{1,0},{2,3},{3,2},{4,5},{5,4},{6,7},{7,6},{8,9},{9,8},{10,11... | collective-permute-start | bytes 1327112 | tf_op jit(solution)/shard_map/ppermute | solution.py:53
  683.4 8.1 %collective-permute-start.53 = (bf16[96,1152]{1,0:T(8,128)(2,1)S(1)}, bf16[96,1152]{1,0:T(8,128)(2,1)S(1)}, u32[]{:S(2)}, u32[]{:S(2)}) collective-permute-start(bf16[96,1152]{1,0:T(8,128)(2,1)S(1)} %slice.321), channel_id=1, source_target_pairs={{0,1},{1,0},{2,3},{3,2},{4,5},{5,4},{6,7},{7,6},{8,9},{9,8},{10,11... | collective-permute-start | bytes 663560 | tf_op jit(solution)/shard_map/ppermute | solution.py:53
  684.5 14.5 %collective-permute-start.59 = (bf16[96,1152]{1,0:T(8,128)(2,1)S(1)}, bf16[96,1152]{1,0:T(8,128)(2,1)S(1)}, u32[]{:S(2)}, u32[]{:S(2)}) collective-permute-start(bf16[96,1152]{1,0:T(8,128)(2,1)S(1)} %slice.327), channel_id=1, source_target_pairs={{0,16},{2,18},{4,20},{6,22},{8,24},{10,26},{12,28},{14,30},{16,0},... | collective-permute-start | bytes 663560 | tf_op jit(solution)/shard_map/ppermute | solution.py:54
  689.2 10.0 %collective-permute-start.65 = (bf16[96,1152]{1,0:T(8,128)(2,1)S(1)}, bf16[96,1152]{1,0:T(8,128)(2,1)S(1)}, u32[]{:S(2)}, u32[]{:S(2)}) collective-permute-start(bf16[96,1152]{1,0:T(8,128)(2,1)S(1)} %slice.333), channel_id=1, source_target_pairs={{0,4},{2,6},{4,0},{6,2},{8,12},{10,14},{12,8},{14,10},{16,20},{18,... | collective-permute-start | bytes 663560 | tf_op jit(solution)/shard_map/ppermute | solution.py:54
  691.5 10.2 %collective-permute-start.54 = (bf16[48,1152]{1,0:T(8,128)(2,1)S(1)}, bf16[48,1152]{1,0:T(8,128)(2,1)S(1)}, u32[]{:S(2)}, u32[]{:S(2)}) collective-permute-start(bf16[48,1152]{1,0:T(8,128)(2,1)S(1)} %slice.323), channel_id=1, source_target_pairs={{0,16},{2,18},{4,20},{6,22},{8,24},{10,26},{12,28},{14,30},{16,0},... | collective-permute-start | bytes 331784 | tf_op jit(solution)/shard_map/ppermute | solution.py:54
  (196 other events, 3061.0 us)

commit v2 on v1

--- a/solution.py
+++ b/solution.py
@@ -1,5 +1,6 @@
 import jax
 import jax.numpy as jnp
+import numpy as np
 from jax import lax
 from jax.experimental import pallas as pl
 from jax.experimental.pallas import tpu as pltpu
@@ -47,6 +48,10 @@
         self.dp_rank = lax.axis_index("dp")
         self.mod_rank = lax.axis_index("mod")
         self.chips = self.dp // 2 * self.mod
+        self.lead = list(range(self.bits - 1, 2, -1))
+        last = ["mod", 1, 2]
+        self.turns = [last[n:] + last[:n] for n in range(3)]
+        self.orders = [self.lead + turn for turn in self.turns]
 
     def swap(self, value, dim):
         if dim == "mod":
@@ -63,24 +68,102 @@
                     dp_mask ^= 1 << dim
         return dp_mask, mod_mask
 
-    def device(self, order, j, core):
-        dp_mask, mod_mask = self.mask(order, j)
-        return (self.dp_rank ^ (dp_mask ^ core)) * self.mod + (self.mod_rank ^ mod_mask)
+    def devices(self, order, core, chunks):
+        masks = np.array([self.mask(order, j) for j in chunks], np.int32)
+        return (self.dp_rank ^ (masks[:, 0] ^ core)) * self.mod + (self.mod_rank ^ masks[:, 1])
 
     def gather(self, value, order):
         for dim in order[:-1]:
             value = jnp.concatenate([value, self.swap(value, dim)], axis=0)
         return value, self.swap(value, order[-1])
 
-    def scatter(self, own, other, order):
-        for step in range(len(order) - 1, -1, -1):
-            got = self.swap(other, order[step])
-            total = own.astype(f32) + got.astype(f32)
-            if step == 0:
-                return total
-            total = total.astype(bf16)
-            half = total.shape[0] // 2
-            own, other = total[:half], total[half:]
+
+def after(value, *others):
+    return lax.optimization_barrier((value, *others))[0]
+
+
+class Gather:
+    def __init__(self, net, shard):
+        self.net, self.count = net, len(net.lead)
+        self.third = shard.shape[0] // 3
+        self.value, self.got, self.phase = shard, None, 0
+
+    def start(self, *others):
+        net, phase = self.net, self.phase
+        if phase < self.count:
+            value = after(self.value, *others) if others else self.value
+            self.value, self.got = value, net.swap(value, net.lead[phase])
+        else:
+            if phase == self.count:
+                whole = self.value.reshape(-1, 3, self.third, self.value.shape[-1])
+                self.value = [whole[:, n].reshape(-1, whole.shape[-1]) for n in range(3)]
+            if others:
+                self.value = list(lax.optimization_barrier((*self.value, *others))[:3])
+            step = phase - self.count
+            self.got = [net.swap(self.value[n], net.turns[n][step]) for n in range(3)]
+        self.phase += 1
+        return self
+
+    def finish(self):
+        if self.phase <= self.count:
+            self.value = jnp.concatenate([self.value, self.got], axis=0)
+        elif self.phase < self.count + 3:
+            self.value = [jnp.concatenate(pair, axis=0) for pair in zip(self.value, self.got)]
+        return self
+
+    def arrived(self):
+        return self.got if isinstance(self.got, list) else [self.got]
+
+
+class Scatter:
+    def __init__(self, net, own, other):
+        self.net, self.own, self.other = net, own, other
+        self.step = 2
+        self.lead = len(net.lead) - 1
+        self.send()
+
+    def send(self):
+        net = self.net
+        if self.step >= 0:
+            self.got = [net.swap(self.other[n], net.turns[n][self.step]) for n in range(3)]
+        else:
+            self.got = [net.swap(self.other, net.lead[self.lead])]
+
+    def arrived(self):
+        return self.got
+
+    def advance(self):
+        if self.step >= 0:
+            totals = [(a.astype(f32) + b.astype(f32)).astype(bf16) for a, b in zip(self.own, self.got)]
+            self.step -= 1
+            if self.step >= 0:
+                half = totals[0].shape[0] // 2
+                self.own, self.other = [t[:half] for t in totals], [t[half:] for t in totals]
+            else:
+                width = totals[0].shape[-1]
+                count = 1 << len(self.net.lead)
+                whole = jnp.concatenate([t.reshape(count, -1, width) for t in totals], axis=1)
+                half = count // 2
+                self.own, self.other = (
+                    whole[:half].reshape(-1, width),
+                    whole[half:].reshape(-1, width),
+                )
+            self.send()
+            return
+        total = self.own.astype(f32) + self.got[0].astype(f32)
+        self.lead -= 1
+        if self.lead < 0:
+            self.total, self.got = total, []
+            return
+        total = total.astype(bf16)
+        half = total.shape[0] // 2
+        self.own, self.other = total[:half], total[half:]
+        self.send()
+
+    def rest(self):
+        while self.got:
+            self.advance()
+        return self.total
 
 
 def copy_kernel(moves, *refs):
@@ -143,29 +226,30 @@
     dp_count, mod_count = net.dp, net.mod
     crop_count = crop_slot.shape[1] // mod_count
     mod_rank = net.mod_rank
-    high = list(range(net.bits - 1, 1, -1))
-    order_a = ["mod"] + high + [1]
-    order_b = [1] + high + ["mod"]
-    attn_orders = [[high[0], "mod"] + high[1:] + [1], high[1:] + [high[0], 1, "mod"], [high[0], 1, "mod"] + high[1:]]
     shard = attn_weight.shape[0]
     chips = net.chips
     third = shard // 3
-    attn_cut = [third, third, third]
-    part_a = shard * 5 // 9 // 16 * 16 if shard % 16 == 0 else shard // 2
-    fc_cut = [part_a, shard - part_a]
-    fc_orders = [order_a, order_b]
-
-    attn_parts = []
-    for n in range(3):
-        attn_parts.append(net.gather(attn_weight[n * third : (n + 1) * third], attn_orders[n]))
-    attn_other = [tuple(net.swap(piece, 0) for piece in pair) for pair in attn_parts]
-    fcin_pieces, fcout_pieces, fc_order_of = [], [], []
-    for weight, pieces in ((fc_in, fcin_pieces), (fc_out, fcout_pieces)):
-        start = 0
-        for rows, order in zip(fc_cut, fc_orders):
-            pieces.extend(net.gather(weight[start : start + rows], order))
-            start += rows
-
+
+    g_attn, g_in, g_out = Gather(net, attn_weight), Gather(net, fc_in), Gather(net, fc_out)
+    for _ in net.lead:
+        g_attn.start().finish()
+    g_attn.start()
+    for _ in net.lead:
+        g_in.start(*g_attn.value).finish()
+    g_attn.finish().start()
+    for _ in net.lead:
+        g_out.start(*g_attn.arrived()).finish()
+    g_attn.finish().start()
+    attn_own = g_attn.value
+    attn_own_other = [net.swap(piece, 0) for piece in attn_own]
+    g_in.start(*attn_own)
+    attn_got = g_attn.arrived()
+    attn_got_other = [net.swap(piece, 0) for piece in attn_got]
+    g_in.finish().start(*attn_got)
+    attn_parts = list(zip(attn_own, attn_got))
+    attn_other = list(zip(attn_own_other, attn_got_other))
+
+    chunks_of = [range(chips // 2), range(chips // 2, chips)]
     arrays, moves, index = [], [], []
     for core in range(2):
         for n in range(3):
@@ -173,8 +257,8 @@
                 arrays.append((attn_parts, attn_other)[core][n][side])
                 for j in range(chips // 2):
                     moves.append((len(arrays) - 1, j * third, None, None, third))
-                    index.append(net.device(attn_orders[n], j + side * (chips // 2), core) * 3 + n)
-    index = jnp.stack(index).astype(jnp.int32)
+                index.append(net.devices(net.orders[n], core, chunks_of[side]) * 3 + n)
+    index = jnp.concatenate(index).astype(jnp.int32)
     blocky = third % 16 == 0
     if blocky:
         to_natural = [(s, sa, 12, ta, r) for s, sa, _, ta, r in moves]
@@ -204,27 +288,34 @@
     token_mod = times(slot_pick, modulation)
     shift_a, scale_a, gate_a, shift_m, scale_m, gate_m = jnp.split(token_mod, 6, axis=1)
 
-    bias_all = lax.all_gather(biases, ("dp", "mod"), axis=0, tiled=True)
+    bias_all = lax.all_to_all(
+        jnp.broadcast_to(biases[None], (dp_count * mod_count, biases.shape[0])),
+        ("dp", "mod"),
+        split_axis=0,
+        concat_axis=0,
+        tiled=True,
+    ).reshape(-1)
     bias_query = bias_all[:model_width].astype(f32)
     bias_value = bias_all[model_width : 2 * model_width].astype(f32)
     bias_proj = bias_all[2 * model_width : 3 * model_width].astype(f32)
     bias_out = bias_all[3 * model_width : 4 * model_width].astype(f32)
     bias_in = bias_all[4 * model_width :].reshape(dp_count * mod_count, shard)
     bias_pieces, picks = [], []
-    start = 0
-    for rows, order in zip(fc_cut, fc_orders):
+    for n in range(3):
         for side in range(2):
-            devices = jnp.stack([net.device(order, j + side * (chips // 2), 0) for j in range(chips // 2)])
+            devices = net.devices(net.orders[n], 0, chunks_of[side])
             pick = (devices[:, None] == jnp.arange(dp_count * mod_count)[None, :]).astype(bf16)
             picks.append(pick)
-            bias_pieces.append(times(pick, bias_in[:, start : start + rows]).reshape(-1))
-        start += rows
+            bias_pieces.append(times(pick, bias_in[:, n * third : (n + 1) * third]).reshape(-1))
 
     qkv_weight = attn_w[: 3 * model_width]
     proj_weight = attn_w[3 * model_width :]
     resid = tokens[0].astype(f32)
     normed_a, inverse_a = layer_norm(resid)
     attn_in = (normed_a * (1.0 + scale_a) + shift_a).astype(bf16)
+    attn_in = after(attn_in, *g_in.arrived())
+    g_in.finish().start()
+    g_out.start()
     qkv_bias = jnp.concatenate([bias_query, jnp.zeros_like(bias_query), bias_value])
     qkv = (times_rows(attn_in, qkv_weight) + qkv_bias).astype(bf16)
     query = qkv[:, :model_width].reshape(tok_len, head_count, head_dim)
@@ -242,6 +333,8 @@
     probs = jnp.exp(scores - log_total).astype(bf16)
     context = jnp.einsum("hqk,khd->qhd", probs, value, preferred_element_type=f32)
     context = context.reshape(tok_len, model_width).astype(bf16)
+    context = after(context, *g_out.arrived())
+    g_out.finish().start()
     attn_out = times_rows(context, proj_weight) + bias_proj
     mid = resid + gate_a * attn_out
     normed_m, inverse_m = layer_norm(mid)
@@ -254,24 +347,35 @@
     out_sum, back_sum = 0.0, 0.0
     fcin_grads, fcout_grads, grad_bias_in = [], [], 0.0
     hiddens, acts = [], []
-    start = 0
+    mlp_both = after(mlp_both, *g_in.arrived(), *g_out.arrived())
+    g_out.finish().start()
+    fcin_pieces = [piece for pair in zip(g_in.value, g_in.arrived()) for piece in pair]
+    fcout_pieces = [piece for pair in zip(g_out.value, g_out.arrived()) for piece in pair]
     for n, (w_in, b_in) in enumerate(zip(fcin_pieces, bias_pieces)):
         hidden = times_rows(mlp_both, w_in) + b_in
         act = gelu_tanh(hidden).astype(bf16)
         hiddens.append(hidden)
         acts.append(act)
         fcout_grads.append(contract_rows(act, grad_both).astype(bf16))
-    for n, (w_in, w_out) in enumerate(zip(fcin_pieces, fcout_pieces)):
+    s_out = Scatter(net, fcout_grads[0::2], fcout_grads[1::2])
+    grad_hiddens = []
+    for n, w_out in enumerate(fcout_pieces):
         out_sum = out_sum + times(acts[n], w_out)
         gelu_back = jax.vjp(gelu_tanh, hiddens[n])[1]
         grad_hidden = gelu_back(times_rows(grad_both, w_out))[0].astype(bf16)
-        fcin_grads.append(contract_rows(grad_hidden, mlp_both).astype(bf16))
-        back_sum = back_sum + times(grad_hidden, w_in)
-        rows = fc_cut[n // 2]
-        column = jnp.sum(grad_hidden.astype(f32), axis=0).reshape(chips // 2, rows)
+        grad_hiddens.append(grad_hidden)
+    grad_hiddens = lax.optimization_barrier((*grad_hiddens, *s_out.arrived()))[:6]
+    s_out.advance()
+    for n, w_in in enumerate(fcin_pieces):
+        fcin_grads.append(contract_rows(grad_hiddens[n], mlp_both).astype(bf16))
+        back_sum = back_sum + times(grad_hiddens[n], w_in)
+        column = jnp.sum(grad_hiddens[n].astype(f32), axis=0).reshape(chips // 2, third)
         placed = jnp.dot(picks[n].astype(f32).T, column, precision=highest)
-        lead = 0 if n < 2 else fc_cut[0]
-        grad_bias_in = grad_bias_in + jnp.pad(placed, ((0, 0), (lead, shard - lead - rows)))
+        lead = n // 2 * third
+        grad_bias_in = grad_bias_in + jnp.pad(placed, ((0, 0), (lead, shard - lead - third)))
+    s_in = Scatter(net, fcin_grads[0::2], fcin_grads[1::2])
+    back_sum = after(back_sum, *s_out.arrived())
+    s_out.advance()
     mlp_out = out_sum[:tok_len] + net.swap(out_sum[tok_len:], 0) + bias_out
     grad_mlp_in = back_sum[:tok_len] + net.swap(back_sum[tok_len:], 0)
 
@@ -281,6 +385,9 @@
     grad_mid = grad_out + norm_back(grad_mlp_in * (1.0 + scale_m), normed_m, inverse_m)
     grad_gate_a = grad_mid * attn_out
     grad_attn = (gate_a * grad_mid).astype(bf16)
+    grad_attn = after(grad_attn, *s_out.arrived(), *s_in.arrived())
+    s_out.advance()
+    s_in.advance()
     grad_proj = contract_rows(grad_attn, context)
     grad_context = times(grad_attn, proj_weight)
     grad_context = grad_context.astype(bf16).reshape(tok_len, head_count, head_dim)
@@ -290,6 +397,8 @@
     grad_probs = jnp.einsum("qhd,khd->hqk", grad_context, value, preferred_element_type=f32)
     grad_scores = probs_full * (grad_probs - jnp.sum(grad_probs * probs_full, axis=-1, keepdims=True))
     grad_scores = grad_scores.astype(bf16)
+    grad_scores = after(grad_scores, *s_in.arrived())
+    s_in.advance()
     grad_query = jnp.einsum("hqk,khd->qhd", grad_scores, key_part, preferred_element_type=f32) * score_scale
     grad_keys = jnp.einsum("hqk,qhd->khd", grad_scores, query, preferred_element_type=f32) * score_scale
     grad_value = jnp.einsum("hqk,qhd->khd", probs_low, grad_context, preferred_element_type=f32)
@@ -301,6 +410,9 @@
         ],
         axis=1,
     ).astype(bf16)
+    grad_qkv = after(grad_qkv, *s_out.arrived(), *s_in.arrived())
+    fcout_sum = s_out.rest()
+    s_in.advance()
     grad_qkv_w = contract_rows(grad_qkv, attn_in)
     grad_attn_in = times(grad_qkv, qkv_weight)
     grad_scale_a = grad_attn_in * normed_a
@@ -315,7 +427,10 @@
             grad_bias_in.reshape(-1),
         ]
     )
-    bias_sum = lax.psum_scatter(grad_bias, ("dp", "mod"), scatter_dimension=0, tiled=True)
+    bias_rows = lax.all_to_all(
+        grad_bias.reshape(dp_count * mod_count, -1), ("dp", "mod"), split_axis=0, concat_axis=0, tiled=True
+    )
+    bias_sum = jnp.sum(bias_rows, axis=0)
 
     grad_token_mod = jnp.concatenate(
         [grad_attn_in, grad_scale_a, grad_gate_a, grad_mlp_in, grad_scale_m, grad_gate_m], axis=1
@@ -335,7 +450,7 @@
     own_cond = lax.dynamic_slice_in_dim(cond, mod_rank * crop_count, crop_count, 0).astype(f32)
     silu_back = jax.vjp(jax.nn.silu, own_cond)[1]
     grad_cond = silu_back(grad_silu)[0]
-    ada_order = [1] + high + [0]
+    ada_order = list(range(1, net.bits)) + [0]
     mod_rows = jnp.concatenate(net.gather(grad_mod, ada_order), axis=0)
     cond_rows = jnp.concatenate(net.gather(silu_cond, ada_order), axis=0)
     own_rows = model_width // dp_count
@@ -344,15 +459,7 @@
     ada_b_sum = jnp.sum(mod_rows.astype(f32), axis=0).reshape(ada_bias.shape[0], model_width)
     ada_b_sum = lax.dynamic_slice_in_dim(ada_b_sum, net.dp_rank * own_rows, own_rows, 1)
 
-    start = 0
-    fc_sums = []
-    for grads in (fcout_grads, fcin_grads):
-        fc_sums.append(
-            jnp.concatenate(
-                [net.scatter(grads[2 * n], grads[2 * n + 1], fc_orders[n]) for n in range(2)], axis=0
-            )
-        )
-    fcout_sum, fcin_sum = fc_sums
+    fcin_sum = s_in.rest()
     attn_grad = jnp.concatenate([grad_qkv_w, grad_proj], axis=0).astype(bf16)
     if blocky:
         shapes = [a.shape for a in arrays]
@@ -364,14 +471,8 @@
             return lax.dynamic_update_slice_in_dim(whole, block, n * third, 0)
 
         grads = jnp.split(lax.fori_loop(0, len(moves), take, jnp.zeros_like(attn_grad)), 12)
-    attn_sum = []
-    for n in range(3):
-        pair = [
-            (grads[2 * n + s].astype(f32) + net.swap(grads[6 + 2 * n + s], 0).astype(f32)).astype(bf16)
-            for s in range(2)
-        ]
-        attn_sum.append(net.scatter(pair[0], pair[1], attn_orders[n]))
-    attn_sum = jnp.concatenate(attn_sum, axis=0)
+    pairs = [(a.astype(f32) + net.swap(b, 0).astype(f32)).astype(bf16) for a, b in zip(grads[:6], grads[6:])]
+    attn_sum = Scatter(net, pairs[0::2], pairs[1::2]).rest()
     return (
         result[None],
         grad_tokens[None],

time: 715 us -> 594 us (0.83)
  blocking collectives: 79.6 us -> 0 us
  waiting for transfers between devices: 307 us -> 242 us
  starting transfers between devices: 83 us -> 97.9 us
  matrix products: 102 us -> 115 us
    unnamed x2 -> x0, blocking collectives: 79.6 us -> none
    ppermute x66, waiting for transfers between devices: 277 us -> 213 us  [swap(): lax.ppermute(value, 'dp', [(i, i ^ 1 << dim) for i in range(self.dp)])]
    all_to_all x0 -> x2, starting transfers between devices: none -> 9.24 us  [the longest x1 4.89 us: on_device(): lax.all_to_all(jnp.broadcast_to(biases[None], (dp_count * mod_count, bias...]
    concatenate x27 -> x6, other arithmetic: 9.53 us -> 1.09 us  [gather(): value = jnp.concatenate([value, self.swap(value, dim)], axis=0)]
    sub x0 -> x1, matrix products: none -> 8.26 us  [on_device(): grad_probs - jnp.sum(grad_probs * probs_full, axis=-1, keepdims=True)]
    dot_general x13 -> x17, matrix products: 31.8 us -> 23.6 us  [contract_rows(): lax.dot_general(left, right, (((0,), (0,)), ((), ())), preferred_element_...]
    dot_general x16 -> x22, matrix products: 30.6 us -> 37.9 us  [times(): return jnp.dot(left, right, preferred_element_type=f32)]
    dot_general x11 -> x15, matrix products: 29.5 us -> 34.3 us  [times_rows(): lax.dot_general(left, right, (((1,), (1,)), ((), ())), preferred_element_...]
  transfers between devices with their start and end apart: 83 -> 89, of which waited for: 34 -> 36; matrix products, arithmetic and copies ran while one was open for 25% -> 32% of each run, Pallas kernels for 5% -> 5%
where the time goes in v2:
time: 594 us; the launch traced here: 585 us
  waiting for transfers between devices  242 us (41%)
  matrix products  115 us (19%)
  starting transfers between devices  97.9 us (16%)
  other arithmetic  57.2 us (10%)
  local copies, waits for them, and re-layouts  38.8 us (7%)
  Pallas kernels  30.9 us (5%)
    ppermute x66, waiting for transfers between devices, swap(): lax.ppermute(value, 'dp', [(i, i ^ 1 << dim) for i in range(self.dp)])  213 us
    ppermute x66, starting transfers between devices, swap(): lax.ppermute(value, 'dp', [(i, i ^ 1 << dim) for i in range(self.dp)])  67.4 us
    dot_general x22, matrix products, times(): return jnp.dot(left, right, preferred_element_type=f32)  37.9 us
    dot_general x15, matrix products, times_rows(): lax.dot_general(left, right, (((1,), (1,)), ((), ())), preferred_element_...  34.3 us
    pallas_call x2, Pallas kernels, move_blocks(): pl.pallas_call(lambda *refs: copy_kernel(moves, *refs), grid_spec=pltpu.P...  30.9 us
    ppermute x21, waiting for transfers between devices, swap(): return lax.ppermute(value, 'mod', [(i, i ^ 1) for i in range(self.mod)])  28.9 us
    dot_general x17, matrix products, contract_rows(): lax.dot_general(left, right, (((0,), (0,)), ((), ())), preferred_element_...  23.6 us
    unnamed x283, local copies, waits for them, and re-layouts  22.7 us
  transfers between devices with their start and end apart: 89, of which 36 were waited for; matrix products, arithmetic and copies ran while one was open for 32% of the time, Pallas kernels for 5%

profile of v2, /device:TPU:0, one launch (start us, length us, event | category | flops | bytes accessed | tf_op | source)
XLA Modules:
  0.0 585.5 jit_solution(13802895255094235721)
XLA Ops:
  1.5 3.0 collective-permute-start.62
  7.2 4.9 all-to-all-start
  13.0 4.5 fusion.13
  19.4 2.4 collective-permute-start.1
  26.9 3.6 collective-permute-done.63
  30.5 2.5 collective-permute-start.64
  34.6 8.7 %collective-permute-done.64 = bf16[64,1152]{1,0:T(8,128)(2,1)S(1)} collective-permute-done((bf16[64,1152]{1,0:T(8,128)(2,1)S(1)}, bf16[64,1152]{1,0:T(8,128)(2,1)S(1)}, u32[]{:S(2)}, u32[]{:S(2)}) %collective-permute-start.64) | collective-permute-done | bytes 147488 | tf_op jit(solution)/shard_map/ppermute | solution.py:59
  46.2 3.4 collective-permute-start.2
  52.0 5.7 collective-permute-done.7
  58.4 6.0 %collective-permute-done.2 = bf16[144,1152]{1,0:T(8,128)(2,1)S(1)} collective-permute-done((bf16[144,1152]{1,0:T(8,128)(2,1)S(1)}, bf16[144,1152]{1,0:T(8,128)(2,1)S(1)}, u32[]{:S(2)}, u32[]{:S(2)}) %collective-permute-start.2) | collective-permute-done | bytes 331808 | tf_op jit(solution)/shard_map/ppermute | solution.py:59
  64.6 4.7 collective-permute-done.6
  71.7 3.5 collective-permute-start.24
  76.9 20.7 %collective-permute-done.10 = bf16[96,1152]{1,0:T(8,128)(2,1)S(1)} collective-permute-done((bf16[96,1152]{1,0:T(8,128)(2,1)S(1)}, bf16[96,1152]{1,0:T(8,128)(2,1)S(1)}, u32[]{:S(2)}, u32[]{:S(2)}) %collective-permute-start.10) | collective-permute-done | bytes 221216 | tf_op jit(solution)/shard_map/ppermute | solution.py:59
  98.9 3.0 collective-permute-start.11
  102.0 5.1 collective-permute-done.11
  108.4 14.8 %collective-permute-done.25 = bf16[96,1152]{1,0:T(8,128)(2,1)S(1)} collective-permute-done((bf16[96,1152]{1,0:T(8,128)(2,1)S(1)}, bf16[96,1152]{1,0:T(8,128)(2,1)S(1)}, u32[]{:S(2)}, u32[]{:S(2)}) %collective-permute-start.25) | collective-permute-done | bytes 221216 | tf_op jit(solution)/shard_map/ppermute | solution.py:58
  125.6 3.6 collective-permute-done.27
  130.5 4.6 collective-permute-done.26
  140.2 8.4 %collective-permute-done.15 = bf16[192,1152]{1,0:T(8,128)(2,1)S(1)} collective-permute-done((bf16[192,1152]{1,0:T(8,128)(2,1)S(1)}, bf16[192,1152]{1,0:T(8,128)(2,1)S(1)}, u32[]{:S(2)}, u32[]{:S(2)}) %collective-permute-start.15) | collective-permute-done | bytes 442400 | tf_op jit(solution)/shard_map/ppermute | solution.py:59
  157.5 18.3 %move_blocks.2 = bf16[4608,1152]{1,0:T(8,128)(2,1)S(1)} custom-call(s32[96]{0:T(128)S(1)} %concatenate.149.refs_0_, bf16[384,1152]{1,0:T(8,128)(2,1)S(1)} %pad_maximum_fusion.4.refs_1_, bf16[384,1152]{1,0:T(8,128)(2,1)S(1)} %collective-permute-done.12.refs_2_, bf16[384,1152]{1,0:T(8,128)(2,1)S(1)} %pad_maximum_fusion.5.refs_3_, ...), custom_call_target="tpu_custom_call" | custom-call | tf_op jit(solution)/shard_map/move_blocks/pallas_call | solution.py:192
  175.9 2.6 fusion.10
  185.5 4.0 fusion.210
  199.4 14.2 %collective-permute-done.29 = bf16[384,1152]{1,0:T(8,128)(2,1)S(1)} collective-permute-done((bf16[384,1152]{1,0:T(8,128)(2,1)S(1)}, bf16[384,1152]{1,0:T(8,128)(2,1)S(1)}, u32[]{:S(2)}, u32[]{:S(2)}) %collective-permute-start.29) | collective-permute-done | bytes 884768 | tf_op jit(solution)/shard_map/ppermute | solution.py:59
  213.6 2.3 convolution_add_fusion.6
  242.6 2.3 fusion.112
  251.0 2.8 fusion.84
  255.7 3.3 fusion.219
  259.2 3.4 fusion.221
  271.9 2.2 fusion.30
  291.2 21.9 %collective-permute-done.49 = bf16[96,1152]{1,0:T(8,128)(2,1)S(1)} collective-permute-done((bf16[96,1152]{1,0:T(8,128)(2,1)S(1)}, bf16[96,1152]{1,0:T(8,128)(2,1)S(1)}, u32[]{:S(2)}, u32[]{:S(2)}) %collective-permute-start.49) | collective-permute-done | bytes 221216 | tf_op jit(solution)/shard_map/ppermute | solution.py:59
  314.5 4.5 collective-permute-done.48
  320.2 4.7 collective-permute-done.47
  325.1 3.5 collective-permute-start.56
  332.8 11.5 %collective-permute-done.56 = bf16[144,1152]{1,0:T(8,128)(2,1)S(1)} collective-permute-done((bf16[144,1152]{1,0:T(8,128)(2,1)S(1)}, bf16[144,1152]{1,0:T(8,128)(2,1)S(1)}, u32[]{:S(2)}, u32[]{:S(2)}) %collective-permute-start.56) | collective-permute-done | bytes 331808 | tf_op jit(solution)/shard_map/ppermute | solution.py:59
  346.7 4.7 collective-permute-done.54
  352.9 4.5 collective-permute-done.53
  358.7 2.4 collective-permute-done.58
  361.1 2.4 collective-permute-done.57
  366.7 3.0 multiply_convert_fusion.1
  370.5 3.6 convolution_convert_fusion.14
  376.2 4.2 convolution_convert_fusion.15
  380.4 8.3 %multiply_convert_fusion = bf16[16,256,256]{1,2,0:T(8,128)(2,1)} fusion(f32[16,256,256]{1,2,0:T(8,128)} %copy-done.11, f32[16,256]{1,0:T(8,128)} %copy-done.99, pred[256,256]{0,1:T(8,128)(4,1)} %copy-done.77, bf16[256,16,72]{0,2,1:T(8,128)(2,1)} %bitcast.245, bf16[256,16,72]{0,2,1:T(8,128)(2,1)} %bitcast.243), kind=kOutput, calls=%fused_computation.17 | convolution fusion | flops 312480000 | bytes 7553024 | tf_op jit(solution)/shard_map/sub | solution.py:398
  388.7 2.7 fusion.62
  392.6 2.5 convolution_convert_fusion.1
  396.2 6.7 %fusion.200 = (f32[256]{0:T(256)S(1)}, f32[256]{0:T(256)S(1)}, f32[256,6912]{1,0:T(8,128)S(1)}, f32[256,1152]{1,0:T(8,128)S(1)}) fusion(f32[256,6912]{1,0:T(8,128)} %copy-done.10, f32[256]{0:T(256)S(1)} %copy-done.104, f32[256]{0:T(256)S(1)} %copy-done.101, bf16[1,256,1152]{2,1,0:T(8,128)(2,1)S(1)} %copy-done.13, ...), kind=kOutput, calls=%fused_computation.418 | convolution fusion | flops 2040790528 | bytes 13864960 | tf_op jit(solution)/shard_map/dot_general | solution.py:36
  404.0 5.7 convolution_convert_fusion
  409.7 2.9 fusion.70
  421.7 4.3 all-to-all-start.1
  426.7 5.6 fusion.223
  434.8 12.8 %pad_maximum_fusion.refs_1_ = bf16[4608,1152]{1,0:T(8,128)(2,1)S(1)} fusion(bf16[1152,1152]{1,0:T(8,128)(2,1)S(1)} %copy-done.20, bf16[3456,1152]{1,0:T(8,128)(2,1)} %convolution_convert_fusion), kind=kLoop, calls=%fused_computation.2 | loop fusion | flops 21233664 | bytes 21233664 | tf_op jit(solution)/shard_map/concatenate | solution.py:463
  447.6 12.6 %move_blocks.3 = (bf16[384,1152]{1,0:T(8,128)(2,1)S(1)}, bf16[384,1152]{1,0:T(8,128)(2,1)S(1)}, bf16[384,1152]{1,0:T(8,128)(2,1)S(1)}, bf16[384,1152]{1,0:T(8,12...) custom-call(s32[96]{0:T(128)S(1)} %concatenate.149.refs_0_, ...), custom_call_target="tpu_custom_call" | custom-call | tf_op jit(solution)/shard_map/move_blocks/pallas_call | solution.py:192
  468.9 2.8 collective-permute-done.66
  476.7 4.4 collective-permute-done.67
  481.9 2.4 collective-permute-start.68
  485.8 19.1 %collective-permute-done.68 = bf16[64,3456]{1,0:T(8,128)(2,1)S(1)} collective-permute-done((bf16[64,3456]{1,0:T(8,128)(2,1)S(1)}, bf16[64,3456]{1,0:T(8,128)(2,1)S(1)}, u32[]{:S(2)}, u32[]{:S(2)}) %collective-permute-start.68) | collective-permute-done | bytes 442400 | tf_op jit(solution)/shard_map/ppermute | solution.py:59
  509.7 19.3 %collective-permute-done.72 = bf16[384,1152]{1,0:T(8,128)(2,1)S(1)} collective-permute-done((bf16[384,1152]{1,0:T(8,128)(2,1)S(1)}, bf16[384,1152]{1,0:T(8,128)(2,1)S(1)}, u32[]{:S(2)}, u32[]{:S(2)}) %collective-permute-start.72) | collective-permute-done | bytes 884768 | tf_op jit(solution)/shard_map/ppermute | solution.py:59
  537.4 14.6 %collective-permute-done.82 = bf16[384,1152]{1,0:T(8,128)(2,1)} collective-permute-done((bf16[384,1152]{1,0:T(8,128)(2,1)}, bf16[384,1152]{1,0:T(8,128)(2,1)}, u32[]{:S(2)}, u32[]{:S(2)}) %collective-permute-start.82) | collective-permute-done | bytes 884768 | tf_op jit(solution)/shard_map/ppermute | solution.py:59
  554.2 5.5 collective-permute-done.73
  562.1 2.4 collective-permute-done.83
  565.2 2.3 collective-permute-done.74
  567.7 4.2 collective-permute-done.84
  572.0 4.0 collective-permute-start.85
  577.4 2.4 fusion.131
  579.8 4.3 collective-permute-done.85
  (639 shorter events, 190.9 us)
Async XLA Ops:
  1.5 23.8 %collective-permute-start.62 = (bf16[16,1152]{1,0:T(8,128)(2,1)S(1)}, bf16[16,1152]{1,0:T(8,128)(2,1)S(1)}, u32[]{:S(2)}, u32[]{:S(2)}) collective-permute-start(bf16[16,1152]{1,0:T(8,128)(2,1)S(1)} %fusion.130), channel_id=1, source_target_pairs={{0,4},{2,6},{4,0},{6,2},{8,12},{10,14},{12,8},{14,10},{16,20},{18,... | collective-permute-start | bytes 110600 | tf_op jit(solution)/shard_map/ppermute | solution.py:59
  7.2 15.7 %all-to-all-start = ((bf16[32,2,144]{2,1,0:T(2,128)(2,1)}), bf16[32,2,144]{2,1,0:T(2,128)(2,1)S(1)}, u32[]{:S(2)}, u32[]{:S(2)}) async-start(bf16[32,2,144]{2,1,0:T(2,128)(2,1)} %reshape.322), calls=%async_computation | async-start | bytes 65536 | tf_op jit(solution)/shard_map/all_to_all | solution.py:291
  17.5 15.5 %collective-permute-start = (bf16[16,3456]{1,0:T(8,128)(2,1)S(1)}, bf16[16,3456]{1,0:T(8,128)(2,1)S(1)}, u32[]{:S(2)}, u32[]{:S(2)}) collective-permute-start(bf16[16,3456]{1,0:T(8,128)(2,1)S(1)} %fusion.13), channel_id=1, source_target_pairs={{0,1},{1,0},{2,3},{3,2},{4,5},{5,4},{6,7},{7,6},{8,9},{9,8},{10,11... | collective-permute-start | bytes 331784 | tf_op jit(solution)/shard_map/ppermute | solution.py:58
  19.4 24.0 %collective-permute-start.1 = (bf16[144,1152]{1,0:T(8,128)(2,1)S(1)}, bf16[144,1152]{1,0:T(8,128)(2,1)S(1)}, u32[]{:S(2)}, u32[]{:S(2)}) collective-permute-start(bf16[144,1152]{1,0:T(8,128)(2,1)S(1)} %copy-done.83), channel_id=1, source_target_pairs={{0,16},{2,18},{4,20},{6,22},{8,24},{10,26},{12,28},{14,30},{16,0},... | collective-permute-start | bytes 995336 | tf_op jit(solution)/shard_map/ppermute | solution.py:59
  30.5 12.8 %collective-permute-start.64 = (bf16[64,1152]{1,0:T(8,128)(2,1)S(1)}, bf16[64,1152]{1,0:T(8,128)(2,1)S(1)}, u32[]{:S(2)}, u32[]{:S(2)}) collective-permute-start(bf16[64,1152]{1,0:T(8,128)(2,1)S(1)} %pad_maximum_fusion.29), channel_id=1, source_target_pairs={{0,16},{2,18},{4,20},{6,22},{8,24},{10,26},{12,28},{14,30},{16,0},... | collective-permute-start | bytes 442376 | tf_op jit(solution)/shard_map/ppermute | solution.py:59
  43.3 27.2 %collective-permute-start.65 = (bf16[128,1152]{1,0:T(8,128)(2,1)S(1)}, bf16[128,1152]{1,0:T(8,128)(2,1)S(1)}, u32[]{:S(2)}, u32[]{:S(2)}) collective-permute-start(bf16[128,1152]{1,0:T(8,128)(2,1)S(1)} %pad_maximum_fusion.27), channel_id=1, source_target_pairs={{0,2},{2,0},{4,6},{6,4},{8,10},{10,8},{12,14},{14,12},{16,18},{18,... | collective-permute-start | bytes 884744 | tf_op jit(solution)/shard_map/ppermute | solution.py:59
  45.1 12.6 %collective-permute-start.7 = (bf16[96,1152]{1,0:T(8,128)(2,1)S(1)}, bf16[96,1152]{1,0:T(8,128)(2,1)S(1)}, u32[]{:S(2)}, u32[]{:S(2)}) collective-permute-start(bf16[96,1152]{1,0:T(8,128)(2,1)S(1)} %bitcast.220), channel_id=1, source_target_pairs={{0,8},{2,10},{4,12},{6,14},{8,0},{10,2},{12,4},{14,6},{16,24},{18,... | collective-permute-start | bytes 663560 | tf_op jit(solution)/shard_map/ppermute | solution.py:59
  45.6 12.1 %collective-permute-start.3 = (bf16[96,1152]{1,0:T(8,128)(2,1)S(1)}, bf16[96,1152]{1,0:T(8,128)(2,1)S(1)}, u32[]{:S(2)}, u32[]{:S(2)}) collective-permute-start(bf16[96,1152]{1,0:T(8,128)(2,1)S(1)} %bitcast.217), channel_id=1, source_target_pairs={{0,1},{1,0},{2,3},{3,2},{4,5},{5,4},{6,7},{7,6},{8,9},{9,8},{10,11... | collective-permute-start | bytes 663560 | tf_op jit(solution)/shard_map/ppermute | solution.py:58
  46.2 18.2 %collective-permute-start.2 = (bf16[144,1152]{1,0:T(8,128)(2,1)S(1)}, bf16[144,1152]{1,0:T(8,128)(2,1)S(1)}, u32[]{:S(2)}, u32[]{:S(2)}) collective-permute-start(bf16[144,1152]{1,0:T(8,128)(2,1)S(1)} %copy-done.84), channel_id=1, source_target_pairs={{0,16},{2,18},{4,20},{6,22},{8,24},{10,26},{12,28},{14,30},{16,0},... | collective-permute-start | bytes 995336 | tf_op jit(solution)/shard_map/ppermute | solution.py:59
  51.4 17.8 %collective-permute-start.6 = (bf16[192,1152]{1,0:T(8,128)(2,1)S(1)}, bf16[192,1152]{1,0:T(8,128)(2,1)S(1)}, u32[]{:S(2)}, u32[]{:S(2)}) collective-permute-start(bf16[192,1152]{1,0:T(8,128)(2,1)S(1)} %pad_maximum_fusion.18), channel_id=1, source_target_pairs={{0,8},{2,10},{4,12},{6,14},{8,0},{10,2},{12,4},{14,6},{16,24},{18,... | collective-permute-start | bytes 1327112 | tf_op jit(solution)/shard_map/ppermute | solution.py:59
  70.5 69.6 %collective-permute-start.18 = (bf16[384,1152]{1,0:T(8,128)(2,1)S(1)}, bf16[384,1152]{1,0:T(8,128)(2,1)S(1)}, u32[]{:S(2)}, u32[]{:S(2)}) collective-permute-start(bf16[384,1152]{1,0:T(8,128)(2,1)S(1)} %pad_maximum_fusion.4.refs_1_), channel_id=1, source_target_pairs={{0,2},{2,0},{4,6},{6,4},{8,10},{10,8},{12,14},{14,12},{16,18},{18,... | collective-permute-start | bytes 2654216 | tf_op jit(solution)/shard_map/ppermute | solution.py:59
  70.6 65.3 %collective-permute-start.12 = (bf16[384,1152]{1,0:T(8,128)(2,1)S(1)}, bf16[384,1152]{1,0:T(8,128)(2,1)S(1)}, u32[]{:S(2)}, u32[]{:S(2)}) collective-permute-start(bf16[384,1152]{1,0:T(8,128)(2,1)S(1)} %pad_maximum_fusion.4.refs_1_), channel_id=1, source_target_pairs={{0,8},{2,10},{4,12},{6,14},{8,0},{10,2},{12,4},{14,6},{16,24},{18,... | collective-permute-start | bytes 2654216 | tf_op jit(solution)/shard_map/ppermute | solution.py:59
  71.1 64.8 %collective-permute-start.14 = (bf16[384,1152]{1,0:T(8,128)(2,1)S(1)}, bf16[384,1152]{1,0:T(8,128)(2,1)S(1)}, u32[]{:S(2)}, u32[]{:S(2)}) collective-permute-start(bf16[384,1152]{1,0:T(8,128)(2,1)S(1)} %pad_maximum_fusion.6.refs_5_), channel_id=1, source_target_pairs={{0,4},{2,6},{4,0},{6,2},{8,12},{10,14},{12,8},{14,10},{16,20},{18,... | collective-permute-start | bytes 2654216 | tf_op jit(solution)/shard_map/ppermute | solution.py:59
  71.7 27.2 %collective-permute-start.24 = (bf16[144,1152]{1,0:T(8,128)(2,1)S(1)}, bf16[144,1152]{1,0:T(8,128)(2,1)S(1)}, u32[]{:S(2)}, u32[]{:S(2)}) collective-permute-start(bf16[144,1152]{1,0:T(8,128)(2,1)S(1)} %copy-done.85), channel_id=1, source_target_pairs={{0,16},{2,18},{4,20},{6,22},{8,24},{10,26},{12,28},{14,30},{16,0},... | collective-permute-start | bytes 995336 | tf_op jit(solution)/shard_map/ppermute | solution.py:59
  76.3 21.3 %collective-permute-start.10 = (bf16[96,1152]{1,0:T(8,128)(2,1)S(1)}, bf16[96,1152]{1,0:T(8,128)(2,1)S(1)}, u32[]{:S(2)}, u32[]{:S(2)}) collective-permute-start(bf16[96,1152]{1,0:T(8,128)(2,1)S(1)} %bitcast.228), channel_id=1, source_target_pairs={{0,4},{2,6},{4,0},{6,2},{8,12},{10,14},{12,8},{14,10},{16,20},{18,... | collective-permute-start | bytes 663560 | tf_op jit(solution)/shard_map/ppermute | solution.py:59
  97.6 38.4 %collective-permute-start.13 = (bf16[384,1152]{1,0:T(8,128)(2,1)S(1)}, bf16[384,1152]{1,0:T(8,128)(2,1)S(1)}, u32[]{:S(2)}, u32[]{:S(2)}) collective-permute-start(bf16[384,1152]{1,0:T(8,128)(2,1)S(1)} %pad_maximum_fusion.5.refs_3_), channel_id=1, source_target_pairs={{0,1},{1,0},{2,3},{3,2},{4,5},{5,4},{6,7},{7,6},{8,9},{9,8},{10,11... | collective-permute-start | bytes 2654216 | tf_op jit(solution)/shard_map/ppermute | solution.py:58
  107.1 16.1 %collective-permute-start.25 = (bf16[96,1152]{1,0:T(8,128)(2,1)S(1)}, bf16[96,1152]{1,0:T(8,128)(2,1)S(1)}, u32[]{:S(2)}, u32[]{:S(2)}) collective-permute-start(bf16[96,1152]{1,0:T(8,128)(2,1)S(1)} %bitcast.195), channel_id=1, source_target_pairs={{0,1},{1,0},{2,3},{3,2},{4,5},{5,4},{6,7},{7,6},{8,9},{9,8},{10,11... | collective-permute-start | bytes 663560 | tf_op jit(solution)/shard_map/ppermute | solution.py:58
  135.1 17.6 %collective-permute-start.22 = (bf16[384,1152]{1,0:T(8,128)(2,1)S(1)}, bf16[384,1152]{1,0:T(8,128)(2,1)S(1)}, u32[]{:S(2)}, u32[]{:S(2)}) collective-permute-start(bf16[384,1152]{1,0:T(8,128)(2,1)S(1)} %pad_maximum_fusion.6.refs_5_), channel_id=1, source_target_pairs={{0,2},{2,0},{4,6},{6,4},{8,10},{10,8},{12,14},{14,12},{16,18},{18,... | collective-permute-start | bytes 2654216 | tf_op jit(solution)/shard_map/ppermute | solution.py:59
  135.9 12.6 %collective-permute-start.15 = (bf16[192,1152]{1,0:T(8,128)(2,1)S(1)}, bf16[192,1152]{1,0:T(8,128)(2,1)S(1)}, u32[]{:S(2)}, u32[]{:S(2)}) collective-permute-start(bf16[192,1152]{1,0:T(8,128)(2,1)S(1)} %pad_maximum_fusion.20), channel_id=1, source_target_pairs={{0,4},{2,6},{4,0},{6,2},{8,12},{10,14},{12,8},{14,10},{16,20},{18,... | collective-permute-start | bytes 1327112 | tf_op jit(solution)/shard_map/ppermute | solution.py:59
  136.5 12.3 %collective-permute-start.16 = (bf16[192,1152]{1,0:T(8,128)(2,1)S(1)}, bf16[192,1152]{1,0:T(8,128)(2,1)S(1)}, u32[]{:S(2)}, u32[]{:S(2)}) collective-permute-start(bf16[192,1152]{1,0:T(8,128)(2,1)S(1)} %pad_maximum_fusion.21), channel_id=1, source_target_pairs={{0,8},{2,10},{4,12},{6,14},{8,0},{10,2},{12,4},{14,6},{16,24},{18,... | collective-permute-start | bytes 1327112 | tf_op jit(solution)/shard_map/ppermute | solution.py:59
  138.1 12.0 %collective-permute-start.17 = (bf16[192,1152]{1,0:T(8,128)(2,1)S(1)}, bf16[192,1152]{1,0:T(8,128)(2,1)S(1)}, u32[]{:S(2)}, u32[]{:S(2)}) collective-permute-start(bf16[192,1152]{1,0:T(8,128)(2,1)S(1)} %pad_maximum_fusion.22), channel_id=1, source_target_pairs={{0,1},{1,0},{2,3},{3,2},{4,5},{5,4},{6,7},{7,6},{8,9},{9,8},{10,11... | collective-permute-start | bytes 1327112 | tf_op jit(solution)/shard_map/ppermute | solution.py:58
  140.2 13.3 %collective-permute-start.20 = (bf16[384,1152]{1,0:T(8,128)(2,1)S(1)}, bf16[384,1152]{1,0:T(8,128)(2,1)S(1)}, u32[]{:S(2)}, u32[]{:S(2)}) collective-permute-start(bf16[384,1152]{1,0:T(8,128)(2,1)S(1)} %pad_maximum_fusion.5.refs_3_), channel_id=1, source_target_pairs={{0,2},{2,0},{4,6},{6,4},{8,10},{10,8},{12,14},{14,12},{16,18},{18,... | collective-permute-start | bytes 2654216 | tf_op jit(solution)/shard_map/ppermute | solution.py:59
  152.7 38.3 %collective-permute-start.33 = (bf16[192,1152]{1,0:T(8,128)(2,1)}, bf16[192,1152]{1,0:T(8,128)(2,1)}, u32[]{:S(2)}, u32[]{:S(2)}) collective-permute-start(bf16[192,1152]{1,0:T(8,128)(2,1)} %pad_maximum_fusion.24), channel_id=1, source_target_pairs={{0,8},{2,10},{4,12},{6,14},{8,0},{10,2},{12,4},{14,6},{16,24},{18,... | collective-permute-start | bytes 1327112 | tf_op jit(solution)/shard_map/ppermute | solution.py:59
  153.4 41.1 %collective-permute-start.34 = (bf16[192,1152]{1,0:T(8,128)(2,1)}, bf16[192,1152]{1,0:T(8,128)(2,1)}, u32[]{:S(2)}, u32[]{:S(2)}) collective-permute-start(bf16[192,1152]{1,0:T(8,128)(2,1)} %pad_maximum_fusion.25), channel_id=1, source_target_pairs={{0,1},{1,0},{2,3},{3,2},{4,5},{5,4},{6,7},{7,6},{8,9},{9,8},{10,11... | collective-permute-start | bytes 1327112 | tf_op jit(solution)/shard_map/ppermute | solution.py:58
  154.6 37.6 %collective-permute-start.32 = (bf16[192,1152]{1,0:T(8,128)(2,1)}, bf16[192,1152]{1,0:T(8,128)(2,1)}, u32[]{:S(2)}, u32[]{:S(2)}) collective-permute-start(bf16[192,1152]{1,0:T(8,128)(2,1)} %pad_maximum_fusion.23), channel_id=1, source_target_pairs={{0,4},{2,6},{4,0},{6,2},{8,12},{10,14},{12,8},{14,10},{16,20},{18,... | collective-permute-start | bytes 1327112 | tf_op jit(solution)/shard_map/ppermute | solution.py:59
  156.1 42.4 %collective-permute-start.31 = (bf16[384,1152]{1,0:T(8,128)(2,1)}, bf16[384,1152]{1,0:T(8,128)(2,1)}, u32[]{:S(2)}, u32[]{:S(2)}) collective-permute-start(bf16[384,1152]{1,0:T(8,128)(2,1)} %constant_dynamic-update-slice_fusion.4), channel_id=1, source_target_pairs={{0,4},{2,6},{4,0},{6,2},{8,12},{10,14},{12,8},{14,10},{16,20},{18,... | collective-permute-start | bytes 2654216 | tf_op jit(solution)/shard_map/ppermute | solution.py:59
  156.7 42.7 %collective-permute-start.30 = (bf16[384,1152]{1,0:T(8,128)(2,1)}, bf16[384,1152]{1,0:T(8,128)(2,1)}, u32[]{:S(2)}, u32[]{:S(2)}) collective-permute-start(bf16[384,1152]{1,0:T(8,128)(2,1)} %constant_dynamic-update-slice_fusion.2), channel_id=1, source_target_pairs={{0,1},{1,0},{2,3},{3,2},{4,5},{5,4},{6,7},{7,6},{8,9},{9,8},{10,11... | collective-permute-start | bytes 2654216 | tf_op jit(solution)/shard_map/ppermute | solution.py:58
  191.0 22.6 %collective-permute-start.29 = (bf16[384,1152]{1,0:T(8,128)(2,1)S(1)}, bf16[384,1152]{1,0:T(8,128)(2,1)S(1)}, u32[]{:S(2)}, u32[]{:S(2)}) collective-permute-start(bf16[384,1152]{1,0:T(8,128)(2,1)S(1)} %copy-done.48), channel_id=1, source_target_pairs={{0,8},{2,10},{4,12},{6,14},{8,0},{10,2},{12,4},{14,6},{16,24},{18,... | collective-permute-start | bytes 2654216 | tf_op jit(solution)/shard_map/ppermute | solution.py:59
  194.5 38.2 %collective-permute-start.36 = (bf16[384,1152]{1,0:T(8,128)(2,1)S(1)}, bf16[384,1152]{1,0:T(8,128)(2,1)S(1)}, u32[]{:S(2)}, u32[]{:S(2)}) collective-permute-start(bf16[384,1152]{1,0:T(8,128)(2,1)S(1)} %pad_maximum_fusion.8), channel_id=1, source_target_pairs={{0,1},{1,0},{2,3},{3,2},{4,5},{5,4},{6,7},{7,6},{8,9},{9,8},{10,11... | collective-permute-start | bytes 2654216 | tf_op jit(solution)/shard_map/ppermute | solution.py:58
  196.9 36.7 %collective-permute-start.37 = (bf16[384,1152]{1,0:T(8,128)(2,1)S(1)}, bf16[384,1152]{1,0:T(8,128)(2,1)S(1)}, u32[]{:S(2)}, u32[]{:S(2)}) collective-permute-start(bf16[384,1152]{1,0:T(8,128)(2,1)S(1)} %pad_maximum_fusion.9), channel_id=1, source_target_pairs={{0,4},{2,6},{4,0},{6,2},{8,12},{10,14},{12,8},{14,10},{16,20},{18,... | collective-permute-start | bytes 2654216 | tf_op jit(solution)/shard_map/ppermute | solution.py:59
  198.5 31.9 %collective-permute-start.35 = (bf16[384,1152]{1,0:T(8,128)(2,1)S(1)}, bf16[384,1152]{1,0:T(8,128)(2,1)S(1)}, u32[]{:S(2)}, u32[]{:S(2)}) collective-permute-start(bf16[384,1152]{1,0:T(8,128)(2,1)S(1)} %pad_maximum_fusion.7), channel_id=1, source_target_pairs={{0,8},{2,10},{4,12},{6,14},{8,0},{10,2},{12,4},{14,6},{16,24},{18,... | collective-permute-start | bytes 2654216 | tf_op jit(solution)/shard_map/ppermute | solution.py:59
  199.4 20.5 %collective-permute-start.39 = (bf16[256,1152]{1,0:T(8,128)(2,1)S(1)}, bf16[256,1152]{1,0:T(8,128)(2,1)S(1)}, u32[]{:S(2)}, u32[]{:S(2)}) collective-permute-start(bf16[256,1152]{1,0:T(8,128)(2,1)S(1)} %get-tuple-element.86), channel_id=1, source_target_pairs={{0,2},{2,0},{4,6},{6,4},{8,10},{10,8},{12,14},{14,12},{16,18},{18,... | collective-permute-start | bytes 1769480 | tf_op jit(solution)/shard_map/ppermute | solution.py:59
  220.7 33.1 %collective-permute-start.42 = (bf16[384,1152]{1,0:T(8,128)(2,1)S(1)}, bf16[384,1152]{1,0:T(8,128)(2,1)S(1)}, u32[]{:S(2)}, u32[]{:S(2)}) collective-permute-start(bf16[384,1152]{1,0:T(8,128)(2,1)S(1)} %convolution_convert_fusion.11), channel_id=1, source_target_pairs={{0,4},{2,6},{4,0},{6,2},{8,12},{10,14},{12,8},{14,10},{16,20},{18,... | collective-permute-start | bytes 2654216 | tf_op jit(solution)/shard_map/ppermute | solution.py:59
  225.2 28.7 %collective-permute-start.41 = (bf16[384,1152]{1,0:T(8,128)(2,1)S(1)}, bf16[384,1152]{1,0:T(8,128)(2,1)S(1)}, u32[]{:S(2)}, u32[]{:S(2)}) collective-permute-start(bf16[384,1152]{1,0:T(8,128)(2,1)S(1)} %convolution_convert_fusion.12), channel_id=1, source_target_pairs={{0,1},{1,0},{2,3},{3,2},{4,5},{5,4},{6,7},{7,6},{8,9},{9,8},{10,11... | collective-permute-start | bytes 2654216 | tf_op jit(solution)/shard_map/ppermute | solution.py:58
  230.4 23.4 %collective-permute-start.40 = (bf16[384,1152]{1,0:T(8,128)(2,1)S(1)}, bf16[384,1152]{1,0:T(8,128)(2,1)S(1)}, u32[]{:S(2)}, u32[]{:S(2)}) collective-permute-start(bf16[384,1152]{1,0:T(8,128)(2,1)S(1)} %convolution_convert_fusion.13), channel_id=1, source_target_pairs={{0,8},{2,10},{4,12},{6,14},{8,0},{10,2},{12,4},{14,6},{16,24},{18,... | collective-permute-start | bytes 2654216 | tf_op jit(solution)/shard_map/ppermute | solution.py:59
  241.4 124.4 %collective-permute-start.38 = (f32[256,1152]{1,0:T(8,128)}, f32[256,1152]{1,0:T(8,128)}, u32[]{:S(2)}, u32[]{:S(2)}) collective-permute-start(f32[256,1152]{1,0:T(8,128)} %slice.335), channel_id=1, source_target_pairs={{0,2},{2,0},{4,6},{6,4},{8,10},{10,8},{12,14},{14,12},{16,18},{18,... | collective-permute-start | bytes 3538952 | tf_op jit(solution)/shard_map/ppermute | solution.py:59
  264.4 21.1 %collective-permute-start.45 = (bf16[192,1152]{1,0:T(8,128)(2,1)}, bf16[192,1152]{1,0:T(8,128)(2,1)}, u32[]{:S(2)}, u32[]{:S(2)}) collective-permute-start(bf16[192,1152]{1,0:T(8,128)(2,1)} %slice.339), channel_id=1, source_target_pairs={{0,1},{1,0},{2,3},{3,2},{4,5},{5,4},{6,7},{7,6},{8,9},{9,8},{10,11... | collective-permute-start | bytes 1327112 | tf_op jit(solution)/shard_map/ppermute | solution.py:58
  268.1 19.4 %collective-permute-start.44 = (bf16[192,1152]{1,0:T(8,128)(2,1)}, bf16[192,1152]{1,0:T(8,128)(2,1)}, u32[]{:S(2)}, u32[]{:S(2)}) collective-permute-start(bf16[192,1152]{1,0:T(8,128)(2,1)} %slice.338), channel_id=1, source_target_pairs={{0,8},{2,10},{4,12},{6,14},{8,0},{10,2},{12,4},{14,6},{16,24},{18,... | collective-permute-start | bytes 1327112 | tf_op jit(solution)/shard_map/ppermute | solution.py:59
  274.2 16.1 %collective-permute-start.43 = (bf16[192,1152]{1,0:T(8,128)(2,1)S(1)}, bf16[192,1152]{1,0:T(8,128)(2,1)S(1)}, u32[]{:S(2)}, u32[]{:S(2)}) collective-permute-start(bf16[192,1152]{1,0:T(8,128)(2,1)S(1)} %slice.337), channel_id=1, source_target_pairs={{0,4},{2,6},{4,0},{6,2},{8,12},{10,14},{12,8},{14,10},{16,20},{18,... | collective-permute-start | bytes 1327112 | tf_op jit(solution)/shard_map/ppermute | solution.py:59
  275.7 49.4 %collective-permute-start.52 = (bf16[384,1152]{1,0:T(8,128)(2,1)S(1)}, bf16[384,1152]{1,0:T(8,128)(2,1)S(1)}, u32[]{:S(2)}, u32[]{:S(2)}) collective-permute-start(bf16[384,1152]{1,0:T(8,128)(2,1)S(1)} %copy-done.127), channel_id=1, source_target_pairs={{0,4},{2,6},{4,0},{6,2},{8,12},{10,14},{12,8},{14,10},{16,20},{18,... | collective-permute-start | bytes 2654216 | tf_op jit(solution)/shard_map/ppermute | solution.py:59
  285.5 44.1 %collective-permute-start.51 = (bf16[384,1152]{1,0:T(8,128)(2,1)S(1)}, bf16[384,1152]{1,0:T(8,128)(2,1)S(1)}, u32[]{:S(2)}, u32[]{:S(2)}) collective-permute-start(bf16[384,1152]{1,0:T(8,128)(2,1)S(1)} %convolution_convert_fusion.6), channel_id=1, source_target_pairs={{0,1},{1,0},{2,3},{3,2},{4,5},{5,4},{6,7},{7,6},{8,9},{9,8},{10,11... | collective-permute-start | bytes 2654216 | tf_op jit(solution)/shard_map/ppermute | solution.py:58
  287.6 43.8 %collective-permute-start.50 = (bf16[384,1152]{1,0:T(8,128)(2,1)S(1)}, bf16[384,1152]{1,0:T(8,128)(2,1)S(1)}, u32[]{:S(2)}, u32[]{:S(2)}) collective-permute-start(bf16[384,1152]{1,0:T(8,128)(2,1)S(1)} %convolution_convert_fusion.7), channel_id=1, source_target_pairs={{0,8},{2,10},{4,12},{6,14},{8,0},{10,2},{12,4},{14,6},{16,24},{18,... | collective-permute-start | bytes 2654216 | tf_op jit(solution)/shard_map/ppermute | solution.py:59
  290.3 22.7 %collective-permute-start.49 = (bf16[96,1152]{1,0:T(8,128)(2,1)S(1)}, bf16[96,1152]{1,0:T(8,128)(2,1)S(1)}, u32[]{:S(2)}, u32[]{:S(2)}) collective-permute-start(bf16[96,1152]{1,0:T(8,128)(2,1)S(1)} %slice.345), channel_id=1, source_target_pairs={{0,8},{2,10},{4,12},{6,14},{8,0},{10,2},{12,4},{14,6},{16,24},{18,... | collective-permute-start | bytes 663560 | tf_op jit(solution)/shard_map/ppermute | solution.py:59
  324.9 39.7 %collective-permute-start.46 = (f32[256,1152]{1,0:T(8,128)S(1)}, f32[256,1152]{1,0:T(8,128)S(1)}, u32[]{:S(2)}, u32[]{:S(2)}) collective-permute-start(f32[256,1152]{1,0:T(8,128)S(1)} %slice.267), channel_id=1, source_target_pairs={{0,2},{2,0},{4,6},{6,4},{8,10},{10,8},{12,14},{14,12},{16,18},{18,... | collective-permute-start | bytes 3538952 | tf_op jit(solution)/shard_map/ppermute | solution.py:59
  325.1 19.2 %collective-permute-start.56 = (bf16[144,1152]{1,0:T(8,128)(2,1)S(1)}, bf16[144,1152]{1,0:T(8,128)(2,1)S(1)}, u32[]{:S(2)}, u32[]{:S(2)}) collective-permute-start(bf16[144,1152]{1,0:T(8,128)(2,1)S(1)} %slice_bitcast_fusion.5), channel_id=1, source_target_pairs={{0,16},{2,18},{4,20},{6,22},{8,24},{10,26},{12,28},{14,30},{16,0},... | collective-permute-start | bytes 995336 | tf_op jit(solution)/shard_map/ppermute | solution.py:59
  329.6 16.9 %collective-permute-start.55 = (bf16[192,1152]{1,0:T(8,128)(2,1)S(1)}, bf16[192,1152]{1,0:T(8,128)(2,1)S(1)}, u32[]{:S(2)}, u32[]{:S(2)}) collective-permute-start(bf16[192,1152]{1,0:T(8,128)(2,1)S(1)} %slice.348), channel_id=1, source_target_pairs={{0,1},{1,0},{2,3},{3,2},{4,5},{5,4},{6,7},{7,6},{8,9},{9,8},{10,11... | collective-permute-start | bytes 1327112 | tf_op jit(solution)/shard_map/ppermute | solution.py:58
  331.4 20.0 %collective-permute-start.54 = (bf16[192,1152]{1,0:T(8,128)(2,1)S(1)}, bf16[192,1152]{1,0:T(8,128)(2,1)S(1)}, u32[]{:S(2)}, u32[]{:S(2)}) collective-permute-start(bf16[192,1152]{1,0:T(8,128)(2,1)S(1)} %slice.347), channel_id=1, source_target_pairs={{0,8},{2,10},{4,12},{6,14},{8,0},{10,2},{12,4},{14,6},{16,24},{18,... | collective-permute-start | bytes 1327112 | tf_op jit(solution)/shard_map/ppermute | solution.py:59
  344.3 13.0 %collective-permute-start.53 = (bf16[192,1152]{1,0:T(8,128)(2,1)S(1)}, bf16[192,1152]{1,0:T(8,128)(2,1)S(1)}, u32[]{:S(2)}, u32[]{:S(2)}) collective-permute-start(bf16[192,1152]{1,0:T(8,128)(2,1)S(1)} %slice.346), channel_id=1, source_target_pairs={{0,4},{2,6},{4,0},{6,2},{8,12},{10,14},{12,8},{14,10},{16,20},{18,... | collective-permute-start | bytes 1327112 | tf_op jit(solution)/shard_map/ppermute | solution.py:59
  364.5 108.8 %collective-permute-start.86 = (bf16[144,1152]{1,0:T(8,128)(2,1)}, bf16[144,1152]{1,0:T(8,128)(2,1)}, u32[]{:S(2)}, u32[]{:S(2)}) collective-permute-start(bf16[144,1152]{1,0:T(8,128)(2,1)} %slice_bitcast_fusion.1), channel_id=1, source_target_pairs={{0,16},{2,18},{4,20},{6,22},{8,24},{10,26},{12,28},{14,30},{16,0},... | collective-permute-start | bytes 995336 | tf_op jit(solution)/shard_map/ppermute | solution.py:59
  421.7 42.9 %all-to-all-start.1 = ((f32[32,1,288]{2,1,0:T(1,128)}), f32[32,1,288]{2,1,0:T(1,128)}, u32[]{:S(2)}, u32[]{:S(2)}) async-start(f32[32,1,288]{2,1,0:T(1,128)} %all_to_all.11), calls=%async_computation.1 | async-start | bytes 98304 | tf_op jit(solution)/shard_map/all_to_all | solution.py:430
  432.9 33.0 %collective-permute-start.61 = (bf16[8,1152]{1,0:T(8,128)(2,1)}, bf16[8,1152]{1,0:T(8,128)(2,1)}, u32[]{:S(2)}, u32[]{:S(2)}) collective-permute-start(bf16[8,1152]{1,0:T(8,128)(2,1)} %select_convert_fusion), channel_id=1, source_target_pairs={{0,1},{1,0},{2,3},{3,2},{4,5},{5,4},{6,7},{7,6},{8,9},{9,8},{10,11... | collective-permute-start | bytes 55304 | tf_op jit(solution)/shard_map/ppermute | solution.py:58
  464.0 45.0 %collective-permute-start.70 = (bf16[384,1152]{1,0:T(8,128)(2,1)}, bf16[384,1152]{1,0:T(8,128)(2,1)}, u32[]{:S(2)}, u32[]{:S(2)}) collective-permute-start(bf16[384,1152]{1,0:T(8,128)(2,1)} %get-tuple-element.64), channel_id=1, source_target_pairs={{0,2},{2,0},{4,6},{6,4},{8,10},{10,8},{12,14},{14,12},{16,18},{18,... | collective-permute-start | bytes 2654216 | tf_op jit(solution)/shard_map/ppermute | solution.py:59
  464.0 17.8 %collective-permute-start.71 = (bf16[384,1152]{1,0:T(8,128)(2,1)}, bf16[384,1152]{1,0:T(8,128)(2,1)}, u32[]{:S(2)}, u32[]{:S(2)}) collective-permute-start(bf16[384,1152]{1,0:T(8,128)(2,1)} %get-tuple-element.66), channel_id=1, source_target_pairs={{0,2},{2,0},{4,6},{6,4},{8,10},{10,8},{12,14},{14,12},{16,18},{18,... | collective-permute-start | bytes 2654216 | tf_op jit(solution)/shard_map/ppermute | solution.py:59
  464.5 70.4 %collective-permute-start.75 = (bf16[384,1152]{1,0:T(8,128)(2,1)}, bf16[384,1152]{1,0:T(8,128)(2,1)}, u32[]{:S(2)}, u32[]{:S(2)}) collective-permute-start(bf16[384,1152]{1,0:T(8,128)(2,1)} %get-tuple-element.68), channel_id=1, source_target_pairs={{0,2},{2,0},{4,6},{6,4},{8,10},{10,8},{12,14},{14,12},{16,18},{18,... | collective-permute-start | bytes 2654216 | tf_op jit(solution)/shard_map/ppermute | solution.py:59
  471.7 33.3 %collective-permute-start.76 = (bf16[384,1152]{1,0:T(8,128)(2,1)}, bf16[384,1152]{1,0:T(8,128)(2,1)S(1)}, u32[]{:S(2)}, u32[]{:S(2)}) collective-permute-start(bf16[384,1152]{1,0:T(8,128)(2,1)} %copy-done.9), channel_id=1, source_target_pairs={{0,2},{2,0},{4,6},{6,4},{8,10},{10,8},{12,14},{14,12},{16,18},{18,... | collective-permute-start | bytes 2654216 | tf_op jit(solution)/shard_map/ppermute | solution.py:59
  481.1 56.3 %collective-permute-start.80 = (bf16[384,1152]{1,0:T(8,128)(2,1)}, bf16[384,1152]{1,0:T(8,128)(2,1)}, u32[]{:S(2)}, u32[]{:S(2)}) collective-permute-start(bf16[384,1152]{1,0:T(8,128)(2,1)} %get-tuple-element.72), channel_id=1, source_target_pairs={{0,2},{2,0},{4,6},{6,4},{8,10},{10,8},{12,14},{14,12},{16,18},{18,... | collective-permute-start | bytes 2654216 | tf_op jit(solution)/shard_map/ppermute | solution.py:59
  481.9 23.0 %collective-permute-start.68 = (bf16[64,3456]{1,0:T(8,128)(2,1)S(1)}, bf16[64,3456]{1,0:T(8,128)(2,1)S(1)}, u32[]{:S(2)}, u32[]{:S(2)}) collective-permute-start(bf16[64,3456]{1,0:T(8,128)(2,1)S(1)} %pad_maximum_fusion.26), channel_id=1, source_target_pairs={{0,16},{2,18},{4,20},{6,22},{8,24},{10,26},{12,28},{14,30},{16,0},... | collective-permute-start | bytes 1327112 | tf_op jit(solution)/shard_map/ppermute | solution.py:59
  505.0 27.0 %collective-permute-start.69 = (bf16[128,3456]{1,0:T(8,128)(2,1)S(1)}, bf16[128,3456]{1,0:T(8,128)(2,1)S(1)}, u32[]{:S(2)}, u32[]{:S(2)}) collective-permute-start(bf16[128,3456]{1,0:T(8,128)(2,1)S(1)} %pad_maximum_fusion.10), channel_id=1, source_target_pairs={{0,2},{2,0},{4,6},{6,4},{8,10},{10,8},{12,14},{14,12},{16,18},{18,... | collective-permute-start | bytes 2654216 | tf_op jit(solution)/shard_map/ppermute | solution.py:59
  507.3 21.7 %collective-permute-start.72 = (bf16[384,1152]{1,0:T(8,128)(2,1)S(1)}, bf16[384,1152]{1,0:T(8,128)(2,1)S(1)}, u32[]{:S(2)}, u32[]{:S(2)}) collective-permute-start(bf16[384,1152]{1,0:T(8,128)(2,1)S(1)} %add_convert_fusion.7), channel_id=1, source_target_pairs={{0,8},{2,10},{4,12},{6,14},{8,0},{10,2},{12,4},{14,6},{16,24},{18,... | collective-permute-start | bytes 2654216 | tf_op jit(solution)/shard_map/ppermute | solution.py:59
  509.1 25.9 %collective-permute-start.77 = (bf16[384,1152]{1,0:T(8,128)(2,1)}, bf16[384,1152]{1,0:T(8,128)(2,1)}, u32[]{:S(2)}, u32[]{:S(2)}) collective-permute-start(bf16[384,1152]{1,0:T(8,128)(2,1)} %add_convert_fusion.4), channel_id=1, source_target_pairs={{0,1},{1,0},{2,3},{3,2},{4,5},{5,4},{6,7},{7,6},{8,9},{9,8},{10,11... | collective-permute-start | bytes 2654216 | tf_op jit(solution)/shard_map/ppermute | solution.py:58
  529.0 22.9 %collective-permute-start.82 = (bf16[384,1152]{1,0:T(8,128)(2,1)}, bf16[384,1152]{1,0:T(8,128)(2,1)}, u32[]{:S(2)}, u32[]{:S(2)}) collective-permute-start(bf16[384,1152]{1,0:T(8,128)(2,1)} %add_convert_fusion.1), channel_id=1, source_target_pairs={{0,4},{2,6},{4,0},{6,2},{8,12},{10,14},{12,8},{14,10},{16,20},{18,... | collective-permute-start | bytes 2654216 | tf_op jit(solution)/shard_map/ppermute | solution.py:59
  534.3 25.4 %collective-permute-start.73 = (bf16[192,1152]{1,0:T(8,128)(2,1)S(1)}, bf16[192,1152]{1,0:T(8,128)(2,1)S(1)}, u32[]{:S(2)}, u32[]{:S(2)}) collective-permute-start(bf16[192,1152]{1,0:T(8,128)(2,1)S(1)} %slice.364), channel_id=1, source_target_pairs={{0,4},{2,6},{4,0},{6,2},{8,12},{10,14},{12,8},{14,10},{16,20},{18,... | collective-permute-start | bytes 1327112 | tf_op jit(solution)/shard_map/ppermute | solution.py:59
  536.8 23.4 %collective-permute-start.78 = (bf16[192,1152]{1,0:T(8,128)(2,1)S(1)}, bf16[192,1152]{1,0:T(8,128)(2,1)S(1)}, u32[]{:S(2)}, u32[]{:S(2)}) collective-permute-start(bf16[192,1152]{1,0:T(8,128)(2,1)S(1)} %slice.368), channel_id=1, source_target_pairs={{0,8},{2,10},{4,12},{6,14},{8,0},{10,2},{12,4},{14,6},{16,24},{18,... | collective-permute-start | bytes 1327112 | tf_op jit(solution)/shard_map/ppermute | solution.py:59
  572.0 12.0 %collective-permute-start.85 = (bf16[144,1152]{1,0:T(8,128)(2,1)S(1)}, bf16[144,1152]{1,0:T(8,128)(2,1)S(1)}, u32[]{:S(2)}, u32[]{:S(2)}) collective-permute-start(bf16[144,1152]{1,0:T(8,128)(2,1)S(1)} %slice_bitcast_fusion.3), channel_id=1, source_target_pairs={{0,16},{2,18},{4,20},{6,22},{8,24},{10,26},{12,28},{14,30},{16,0},... | collective-permute-start | bytes 995336 | tf_op jit(solution)/shard_map/ppermute | solution.py:59
  (159 other events, 1541.7 us)

commit v3 on v1

v3 whole, which is shorter than its diff:
```python
import functools

import jax
import jax.numpy as jnp
import numpy as np
from jax import lax
from jax.experimental import pallas as pl
from jax.experimental.pallas import tpu as pltpu
from jax.sharding import PartitionSpec as P

HEADS = 16
norm_eps = 1e-06
bf16 = jnp.bfloat16
f32 = jnp.float32
MIB = 1024 * 1024


def layer_norm(values):
    center = values - jnp.mean(values, axis=-1, keepdims=True)
    inverse = lax.rsqrt(jnp.mean(center * center, axis=-1, keepdims=True) + norm_eps)
    return (center * inverse, inverse)


def norm_back(grad_in, normed, inverse):
    centered = grad_in - jnp.mean(grad_in, axis=-1, keepdims=True)
    return (centered - normed * jnp.mean(grad_in * normed, axis=-1, keepdims=True)) * inverse


def dot(left, right, left_dim, right_dim):
    return lax.dot_general(left, right, (((left_dim,), (right_dim,)), ((), ())), preferred_element_type=f32)


def times(left, right):
    return dot(left, right, 1, 0)


def times_rows(left, right):
    return dot(left, right, 1, 1)


def contract_rows(left, right):
    return dot(left, right, 0, 0)


def after(value, *others):
    return lax.optimization_barrier((value, *others))[0]


def summed(left, right):
    return (left.astype(f32) + right.astype(f32)).astype(bf16)


class Net:
    def __init__(self):
        self.dp = lax.axis_size("dp")
        self.mod = lax.axis_size("mod")
        self.bits = self.dp.bit_length() - 1
        self.dp_rank = lax.axis_index("dp")
        self.mod_rank = lax.axis_index("mod")
        self.core = self.dp_rank & 1
        self.chips = self.dp // 2 * self.mod
        self.lead = list(range(self.bits - 1, 2, -1))
        last = ["mod", 1, 2]
        self.turns = [last[n:] + last[:n] for n in range(3)]
        self.orders = [self.lead + turn for turn in self.turns]

    def swap(self, value, dim):
        if dim == "mod":
            return lax.ppermute(value, "mod", [(i, i ^ 1) for i in range(self.mod)])
        return lax.ppermute(value, "dp", [(i, i ^ (1 << dim)) for i in range(self.dp)])

    def ranks(self, order, chunks, core=0):
        masks = []
        for j in chunks:
            dp_mask, mod_mask = core, 0
            for step, dim in enumerate(order):
                if j >> step & 1:
                    if dim == "mod":
                        mod_mask ^= 1
                    else:
                        dp_mask ^= 1 << dim
            masks.append((dp_mask, mod_mask))
        masks = np.array(masks, np.int32)
        return self.dp_rank ^ masks[:, 0], self.mod_rank ^ masks[:, 1]

    def devices(self, order, chunks, core=0):
        dp, mod = self.ranks(order, chunks, core)
        return dp * self.mod + mod

    def local(self, order, chunks):
        dp, mod = self.ranks(order, chunks)
        return (dp >> 1) * self.mod + mod


class Gather:
    def __init__(self, net, shard):
        self.net, self.count = net, len(net.lead)
        self.third = shard.shape[1] // 3
        self.value, self.got, self.phase = shard, None, 0

    def start(self, *others):
        net, phase = self.net, self.phase
        if phase < self.count:
            self.value = after(self.value, *others) if others else self.value
            self.got = [net.swap(self.value, net.lead[phase])]
        else:
            if phase == self.count:
                kinds, _, width = self.value.shape
                whole = self.value.reshape(kinds, -1, 3, self.third, width)
                self.value = [whole[:, :, n].reshape(kinds, -1, width) for n in range(3)]
            if others:
                self.value = list(lax.optimization_barrier((*self.value, *others))[:3])
            step = phase - self.count
            self.got = [net.swap(self.value[n], net.turns[n][step]) for n in range(3)]
        self.phase += 1
        return self

    def finish(self):
        if self.phase <= self.count:
            self.value = jnp.concatenate([self.value, self.got[0]], axis=1)
        elif self.phase < self.count + 3:
            self.value = [jnp.concatenate(pair, axis=1) for pair in zip(self.value, self.got)]
        return self


class Scatter:
    def __init__(self, net):
        self.net = net
        self.own, self.got, self.step = [None] * 3, [None] * 3, [2] * 3
        self.whole = None

    def begin(self, n, own, other):
        self.own[n] = own
        self.got[n] = self.net.swap(other, self.net.turns[n][2])

    def arrived(self):
        return [got for got in self.got if got is not None]

    def advance(self, which=(0, 1, 2)):
        net = self.net
        if self.whole is None:
            for n in which:
                own, got = self.own[n], self.got[n]
                self.step[n] -= 1
                if self.step[n] >= 0:
                    half = own.shape[1] // 2
                    other = summed(own[:, half:], got[:, half:])
                    self.own[n] = summed(own[:, :half], got[:, :half])
                    self.got[n] = net.swap(other, net.turns[n][self.step[n]])
                else:
                    self.own[n], self.got[n] = summed(own, got), None
            if self.arrived():
                return self
            kinds, _, width = self.own[0].shape
            count = 1 << len(net.lead)
            whole = jnp.concatenate([own.reshape(kinds, count, -1, width) for own in self.own], axis=2)
            self.whole, self.left = whole.reshape(kinds, -1, width), len(net.lead)
        else:
            total = self.whole.astype(f32) + self.got[0].astype(f32)
            if self.left == 0:
                self.total, self.got = total, []
                return self
            self.whole = total.astype(bf16)
        half = self.whole.shape[1] // 2
        self.left -= 1
        self.got = [net.swap(self.whole[:, half:], net.lead[self.left])]
        self.whole = self.whole[:, :half]
        return self

    def rest(self):
        while self.got:
            self.advance()
        return self.total


any_spec = pl.BlockSpec(memory_space=pl.ANY)
vmem_spec = pl.BlockSpec(memory_space=pltpu.VMEM)


def run_copies(copies):
    for copy in copies:
        copy.start()
    for copy in copies:
        copy.wait()


def assemble_kernel(rows, each, index_ref, *refs):
    pieces, out_ref, hold, sems, last = refs[:-4], *refs[-4:]
    copies = []
    for n, piece in enumerate(pieces):
        for j in range(each):
            at = pl.multiple_of(index_ref[n * each + j] * rows, rows)
            copies.append(
                pltpu.make_async_copy(
                    piece.at[0, pl.ds(j * rows, rows)], hold.at[pl.ds(at, rows)], sems.at[n * each + j]
                )
            )
    run_copies(copies)
    run_copies([pltpu.make_async_copy(hold, out_ref, last)])


def assemble(pieces, index, rows):
    each, width = pieces[0].shape[1] // rows, pieces[0].shape[2]
    total = len(pieces) * each
    return pl.pallas_call(
        functools.partial(assemble_kernel, rows, each),
        grid_spec=pltpu.PrefetchScalarGridSpec(
            num_scalar_prefetch=1,
            grid=(1,),
            in_specs=[any_spec] * len(pieces),
            out_specs=any_spec,
            scratch_shapes=[
                pltpu.VMEM((total * rows, width), bf16),
                pltpu.SemaphoreType.DMA((total,)),
                pltpu.SemaphoreType.DMA,
            ],
        ),
        out_shape=jax.ShapeDtypeStruct((total * rows, width), bf16),
        compiler_params=pltpu.CompilerParams(vmem_limit_bytes=10 * MIB),
        name="assemble",
    )(index, *pieces)


def split_kernel(rows, each, index_ref, first_ref, second_ref, *refs):
    outs, hold, sems, ins = refs[:-3], *refs[-3:]
    top = first_ref.shape[0]
    run_copies(
        [
            pltpu.make_async_copy(first_ref, hold.at[pl.ds(0, top)], ins.at[0]),
            pltpu.make_async_copy(second_ref, hold.at[pl.ds(top, second_ref.shape[0])], ins.at[1]),
        ]
    )
    copies = []
    for n, out in enumerate(outs):
        for j in range(each):
            at = pl.multiple_of(index_ref[n * each + j] * rows, rows)
            copies.append(
                pltpu.make_async_copy(
                    hold.at[pl.ds(at, rows)], out.at[0, pl.ds(j * rows, rows)], sems.at[n * each + j]
                )
            )
    run_copies(copies)


def split_pieces(first, second, index, rows, count):
    total, width = first.shape[0] + second.shape[0], first.shape[1]
    each = total // rows // count
    return pl.pallas_call(
        functools.partial(split_kernel, rows, each),
        grid_spec=pltpu.PrefetchScalarGridSpec(
            num_scalar_prefetch=1,
            grid=(1,),
            in_specs=[any_spec] * 2,
            out_specs=[any_spec] * count,
            scratch_shapes=[
                pltpu.VMEM((total, width), bf16),
                pltpu.SemaphoreType.DMA((each * count,)),
                pltpu.SemaphoreType.DMA((2,)),
            ],
        ),
        out_shape=[jax.ShapeDtypeStruct((1, each * rows, width), bf16)] * count,
        compiler_params=pltpu.CompilerParams(vmem_limit_bytes=10 * MIB),
        name="split_pieces",
    )(index, first, second)


def softmax_t(key, query, same, scale):
    scores = jnp.where(same, dot(key, query, 0, 0) * scale, -1e30)
    weights = jnp.exp(scores - jnp.max(scores, axis=0, keepdims=True))
    return weights * (1.0 / jnp.sum(weights, axis=0, keepdims=True))


def heads_of(block, dim, cols):
    wide = block[:, cols].astype(f32)
    return [wide[n * dim : (n + 1) * dim].astype(bf16) for n in range(wide.shape[0] // dim)]


def attn_forward(dim, scale, row_ref, col_ref, q_ref, k_ref, v_ref, out_ref):
    length = col_ref.shape[0]
    for s in range(row_ref.shape[0]):
        cols = slice(s * length, (s + 1) * length)
        same = row_ref[s : s + 1] == col_ref[:, s : s + 1]
        outs = []
        for q, k, v in zip(*[heads_of(r[0, 0], dim, cols) for r in (q_ref, k_ref, v_ref)]):
            probs = softmax_t(k, q, same, scale).astype(bf16)
            outs.append(dot(v, probs, 1, 0))
        out_ref[0, :, cols] = jnp.concatenate(outs, axis=0).astype(bf16)


def attn_backward(dim, scale, row_ref, col_ref, q_ref, k_ref, v_ref, g_ref, out_ref):
    length = col_ref.shape[0]
    for s in range(row_ref.shape[0]):
        cols = slice(s * length, (s + 1) * length)
        same = row_ref[s : s + 1] == col_ref[:, s : s + 1]
        gq, gk, gv = [], [], []
        qs, ks, vs = [heads_of(r[0, 0], dim, cols) for r in (q_ref, k_ref, v_ref)]
        for q, k, v, g in zip(qs, ks, vs, heads_of(g_ref[0], dim, cols)):
            probs = softmax_t(k, q, same, scale)
            back = dot(v, g, 0, 0)
            back = probs * (back - jnp.sum(back * probs, axis=0, keepdims=True))
            back = back.astype(bf16)
            gq.append(dot(k, back, 1, 0) * scale)
            gk.append(dot(q, back, 1, 1) * scale)
            gv.append(dot(g, probs.astype(bf16), 1, 1))
        for n, parts in enumerate((gq, gk, gv)):
            out_ref[n, 0, :, cols] = jnp.concatenate(parts, axis=0).astype(bf16)


def attention(qkv, ids, dim, grad=None):
    _, groups, rows, tokens = qkv.shape
    scale = dim**-0.5
    ids_t = ids.T
    flops = groups * rows * tokens * ids.shape[1] * 2

    def one(n):
        return pl.BlockSpec((1, 1, rows, tokens), lambda i: (n, i, 0, 0))

    flat = pl.BlockSpec((1, rows, tokens), lambda i: (i, 0, 0))
    args = [ids, ids_t, qkv, qkv, qkv]
    specs = [pl.BlockSpec(a.shape, lambda i: (0, 0)) for a in (ids, ids_t)] + [one(0), one(1), one(2)]
    if grad is None:
        return pl.pallas_call(
            functools.partial(attn_forward, dim, scale),
            grid=(groups,),
            in_specs=specs,
            out_specs=flat,
            out_shape=jax.ShapeDtypeStruct((groups, rows, tokens), bf16),
            cost_estimate=pl.CostEstimate(flops=2 * flops, bytes_accessed=qkv.size * 3, transcendentals=0),
            compiler_params=pltpu.CompilerParams(vmem_limit_bytes=24 * MIB),
            name="attention",
        )(*args)
    return pl.pallas_call(
        functools.partial(attn_backward, dim, scale),
        grid=(groups,),
        in_specs=specs + [flat],
        out_specs=pl.BlockSpec((3, 1, rows, tokens), lambda i: (0, i, 0, 0)),
        out_shape=jax.ShapeDtypeStruct(qkv.shape, bf16),
        cost_estimate=pl.CostEstimate(flops=5 * flops, bytes_accessed=qkv.size * 5, transcendentals=0),
        compiler_params=pltpu.CompilerParams(vmem_limit_bytes=24 * MIB),
        name="attention_back",
    )(*args, grad)


def mlp_kernel(first, x_ref, g_ref, b_ref, *refs):
    if first:
        pieces, sums, before = refs[:2], refs[-4:], [None] * 4
    else:
        pieces, before, sums = refs[:2], refs[2:6], refs[-4:]
    grads, columns = refs[-7:-5], refs[-5]
    x, g = x_ref[...], g_ref[...]
    half = x.shape[0] // 2
    out_sum, back_sum = 0.0, 0.0
    root = 0.7978845608028654
    for n, piece in enumerate(pieces):
        w_in, w_out = piece[0], piece[1]
        hidden = dot(x, w_in, 1, 1) + b_ref[n : n + 1]
        square = hidden * hidden
        tanh = jnp.tanh(root * hidden * (1.0 + 0.044715 * square))
        act = (0.5 * hidden * (1.0 + tanh)).astype(bf16)
        slope = 0.5 * (1.0 + tanh) + 0.5 * hidden * (1.0 - tanh * tanh) * (root * (1.0 + 0.134145 * square))
        back = dot(g, w_out, 1, 1) * slope
        back = back.astype(bf16)
        grads[n][1] = dot(act, g, 0, 0).astype(bf16)
        grads[n][0] = dot(back, x, 0, 0).astype(bf16)
        columns[n : n + 1] = jnp.sum(back.astype(f32), axis=0, keepdims=True)
        out_sum = out_sum + dot(act, w_out, 1, 0)
        back_sum = back_sum + dot(back, w_in, 1, 0)
    for ref, prior, value in zip(
        sums, before, (out_sum[:half], out_sum[half:], back_sum[:half], back_sum[half:])
    ):
        ref[...] = value if prior is None else value + prior[...]


def mlp_part(x, g, bias, own, other, before):
    tokens, width = x.shape
    units = own.shape[1]
    sums = [jax.ShapeDtypeStruct((tokens // 2, width), f32)] * 4
    outs = [jax.ShapeDtypeStruct(own.shape, bf16)] * 2 + [jax.ShapeDtypeStruct((2, units), f32)] + sums
    args = [x, g, bias, own, other, *before]
    return pl.pallas_call(
        functools.partial(mlp_kernel, not before),
        in_specs=[vmem_spec] * len(args),
        out_specs=[vmem_spec] * len(outs),
        out_shape=outs,
        cost_estimate=pl.CostEstimate(
            flops=24 * tokens * width * units, bytes_accessed=units * width * 32, transcendentals=0
        ),
        compiler_params=pltpu.CompilerParams(vmem_limit_bytes=48 * MIB),
        name="mlp_part",
    )(*args)


def on_device(
    tokens,
    cond,
    segment_ids,
    crop_slot,
    ada_weight,
    ada_bias,
    attn_weight,
    fc_in,
    fc_out,
    biases,
    out_grad,
):
    net = Net()
    tok_len, width = tokens.shape[1:]
    head_dim = width // HEADS
    mod_rank, core, chips = net.mod_rank, net.core, net.chips
    device_count = net.dp * net.mod
    crop_count = crop_slot.shape[1] // net.mod
    shard = attn_weight.shape[0]
    third = shard // 3
    chunks_of = [range(chips // 2), range(chips // 2, chips)]
    halves = [(n, side) for n in range(3) for side in range(2)]
    aligned = shard % (2 * head_dim) == 0 and third % 16 == 0 and width % (2 * net.mod * shard) == 0

    g_attn = Gather(net, attn_weight[None])
    g_fc = Gather(net, jnp.stack([fc_in, fc_out]))
    for n in range(g_attn.count):
        g_attn.start().finish()
    g_attn.start()
    for n in range(g_fc.count):
        g_fc.start(*g_attn.value).finish()
    g_attn.finish().start()
    g_attn.finish().start()
    g_fc.start(*g_attn.got)
    attn_pieces = [(g_attn.value, g_attn.got)[side][n] for n, side in halves]

    silu_cond = jax.nn.silu(cond.astype(f32)).astype(bf16)
    mod_part = times(silu_cond, ada_weight) + ada_bias.reshape(-1).astype(f32)
    mod_own = mod_part.astype(bf16)
    mod_other = net.swap(mod_own, "mod")
    modulation = jnp.concatenate(
        [jnp.where(mod_rank == 0, mod_own, mod_other), jnp.where(mod_rank == 0, mod_other, mod_own)], axis=1
    )
    seg_ids = segment_ids[0]
    slots = lax.dynamic_slice_in_dim(crop_slot[0], mod_rank * crop_count, crop_count)
    crop_onehot = seg_ids[:, None] == jnp.arange(crop_count, dtype=jnp.int32)[None, :]
    token_slot = jnp.sum(jnp.where(crop_onehot, slots[None, :], 0), axis=1)
    slot_pick = token_slot[:, None] == jnp.arange(cond.shape[0], dtype=jnp.int32)[None, :]
    slot_pick = slot_pick.astype(bf16)
    token_mod = times(slot_pick, modulation)
    shift_a, scale_a, gate_a, shift_m, scale_m, gate_m = jnp.split(token_mod, 6, axis=1)

    bias_all = lax.all_to_all(
        jnp.broadcast_to(biases[None], (device_count, biases.shape[0])),
        ("dp", "mod"),
        split_axis=0,
        concat_axis=0,
        tiled=True,
    ).reshape(-1)
    bias_query, bias_value, bias_proj, bias_out = [
        bias_all[n * width : (n + 1) * width].astype(f32) for n in range(4)
    ]
    bias_in = bias_all[4 * width :].reshape(device_count, shard)
    bias_pieces, picks = [], []
    for n, side in halves:
        devices = net.devices(net.orders[n], chunks_of[side])
        pick = (devices[:, None] == jnp.arange(device_count)[None, :]).astype(bf16)
        picks.append(pick)
        bias_pieces.append(times(pick, bias_in[:, n * third : (n + 1) * third]).reshape(1, -1))

    def join(own, other):
        own, other = [a.reshape(-1, 1, net.mod * shard, a.shape[-1]) for a in (own, other)]
        both = jnp.where(core == 0, jnp.concatenate([own, other], 1), jnp.concatenate([other, own], 1))
        return both.reshape(-1, both.shape[-1])

    def part(whole):
        whole = whole.reshape(-1, 2, net.mod * shard, whole.shape[-1])
        return [
            jnp.where(core == c, whole[:, 0], whole[:, 1]).reshape(-1, whole.shape[-1]) for c in range(2)
        ]

    resid = tokens[0].astype(f32)
    normed_a, inverse_a = layer_norm(resid)
    attn_in = (normed_a * (1.0 + scale_a) + shift_a).astype(bf16)
    if aligned:
        index = jnp.concatenate([net.local(net.orders[n], chunks_of[side]) * 3 + n for n, side in halves])
        own_weight = assemble(attn_pieces, index, third)
        qkv_rows = own_weight.shape[0] * 3 // 4
        qkv_weight = own_weight[:qkv_rows]
        proj_own = own_weight[qkv_rows:]
        proj_weight = join(proj_own, net.swap(proj_own, 0))
        ids = jnp.stack([seg_ids, net.swap(seg_ids, 0)])
        attn_both = jnp.concatenate([attn_in, net.swap(attn_in, 0)], axis=0)
        own_query, own_value = part(bias_query[:, None])[0], part(bias_value[:, None])[0]
        qkv_bias = jnp.concatenate([own_query, jnp.zeros_like(own_query), own_value], axis=0)
        attn_both = after(attn_both, *g_fc.got)
        g_fc.finish().start()
        qkv = (times_rows(qkv_weight, attn_both) + qkv_bias).astype(bf16)
        qkv = qkv.reshape(3, -1, 2 * head_dim, 2 * tok_len)
        context_both = attention(qkv, ids, head_dim).reshape(-1, 2 * tok_len)
        context_both = after(context_both, *g_fc.got)
        g_fc.finish().start()
        context = join(context_both[:, :tok_len], net.swap(context_both[:, tok_len:], 0))
        attn_out = dot(context, proj_weight, 0, 1) + bias_proj
    else:
        arrays = attn_pieces + [net.swap(piece, 0) for piece in attn_pieces]
        places = jnp.concatenate(
            [net.devices(net.orders[n], chunks_of[side], c) * 3 + n for c in range(2) for n, side in halves]
        )
        spread = jnp.concatenate(arrays, axis=1)[0]

        def place(n, whole):
            block = lax.dynamic_slice_in_dim(spread, n * third, third)
            return lax.dynamic_update_slice_in_dim(whole, block, places[n] * third, 0)

        attn_w = lax.fori_loop(0, places.shape[0], place, jnp.zeros_like(spread))
        g_fc.finish().start()
        g_fc.finish().start()
        qkv_weight, proj_weight = attn_w[: 3 * width], attn_w[3 * width :]
        qkv_bias = jnp.concatenate([bias_query, jnp.zeros_like(bias_query), bias_value])
        qkv = (times_rows(qkv_weight, attn_in) + qkv_bias[:, None]).astype(bf16)
        qkv = qkv.reshape(3, -1, 2 * head_dim, tok_len)
        context = attention(qkv, seg_ids[None], head_dim).reshape(-1, tok_len)
        attn_out = dot(context, proj_weight, 0, 1) + bias_proj
    mid = resid + gate_a * attn_out
    normed_m, inverse_m = layer_norm(mid)
    mlp_in = (normed_m * (1.0 + scale_m) + shift_m).astype(bf16)
    grad_out = out_grad[0].astype(f32)
    grad_mlp = (gate_m * grad_out).astype(bf16)

    mlp_both = jnp.concatenate([mlp_in, net.swap(mlp_in, 0)], axis=0)
    grad_both = jnp.concatenate([grad_mlp, net.swap(grad_mlp, 0)], axis=0)
    s_fc = Scatter(net)
    sums, columns = [], []
    for n in range(3):
        bias = jnp.concatenate(bias_pieces[2 * n : 2 * n + 2], axis=0)
        own, other, column, *sums = mlp_part(mlp_both, grad_both, bias, g_fc.value[n], g_fc.got[n], sums)
        s_fc.begin(n, own, other)
        columns.extend([column[0], column[1]])
    out_own, out_other, back_own, back_other = sums
    mlp_out = out_own + net.swap(out_other, 0) + bias_out
    grad_mlp_in = back_own + net.swap(back_other, 0)
    grad_bias_in = []
    for n in range(3):
        placed = 0.0
        for side in range(2):
            column = columns[2 * n + side].reshape(chips // 2, third)
            placed = placed + jnp.dot(
                picks[2 * n + side].astype(f32).T, column, precision=lax.Precision.HIGHEST
            )
        grad_bias_in.append(placed)
    grad_bias_in = jnp.concatenate(grad_bias_in, axis=1)

    ada_order = list(range(1, net.bits)) + [0]

    def all_rows(value):
        for dim in ada_order:
            value = jnp.concatenate([value, net.swap(value, dim)], axis=0)
        return value

    cond_rows = all_rows(after(silu_cond, mlp_both))

    result = (mid + gate_m * mlp_out).astype(bf16)
    grad_gate_m = grad_out * mlp_out
    grad_scale_m = grad_mlp_in * normed_m
    grad_mid = grad_out + norm_back(grad_mlp_in * (1.0 + scale_m), normed_m, inverse_m)
    grad_gate_a = grad_mid * attn_out
    grad_attn = (gate_a * grad_mid).astype(bf16)
    grad_proj = dot(grad_attn, context, 0, 1).astype(bf16)
    grad_context = dot(proj_weight, grad_attn, 0, 1).astype(bf16)
    s_attn = Scatter(net)
    if aligned:
        proj_mine, proj_other = part(grad_proj)
        proj_mine = summed(proj_mine, net.swap(proj_other, 0))
        mine, other = part(grad_context)
        context_grads = jnp.concatenate([mine, net.swap(other, 0)], axis=1)
        grad_qkv = attention(qkv, ids, head_dim, context_grads.reshape(-1, 2 * head_dim, 2 * tok_len))
        grad_qkv = grad_qkv.reshape(-1, 2 * tok_len)
        grad_qkv = after(grad_qkv, *s_fc.arrived())
        s_fc.advance()
        grad_qkv_w = times(grad_qkv, attn_both).astype(bf16)
        pieces = split_pieces(grad_qkv_w, proj_mine, index, third, 6)
        back_both = contract_rows(grad_qkv, qkv_weight)
        grad_attn_in = back_both[:tok_len] + net.swap(back_both[tok_len:], 0)
        column = jnp.sum(grad_qkv.astype(f32), axis=1, keepdims=True).reshape(3, -1, 1)
        none = jnp.zeros_like(column[0])
        grad_bias_query, grad_bias_value = join(column[0], none)[:, 0], join(column[2], none)[:, 0]
    else:
        grad_qkv = attention(
            qkv, seg_ids[None], head_dim, grad_context.reshape(-1, 2 * head_dim, tok_len)
        ).reshape(-1, tok_len)
        s_fc.advance()
        attn_grad = jnp.concatenate([times(grad_qkv, attn_in).astype(bf16), grad_proj], axis=0)

        def take(n, whole):
            block = lax.dynamic_slice_in_dim(attn_grad, places[n] * third, third)
            return lax.dynamic_update_slice_in_dim(whole, block, n * third, 0)

        grads = lax.fori_loop(0, places.shape[0], take, jnp.zeros_like(attn_grad))
        grads = jnp.split(grads[None], 12, axis=1)
        pieces = [summed(a, net.swap(b, 0)) for a, b in zip(grads[:6], grads[6:])]
        grad_attn_in = contract_rows(grad_qkv, qkv_weight)
        column = jnp.sum(grad_qkv.astype(f32), axis=1).reshape(3, -1)
        grad_bias_query, grad_bias_value = column[0], column[2]
    for n in range(3):
        s_attn.begin(n, pieces[2 * n], pieces[2 * n + 1])
    grad_scale_a = grad_attn_in * normed_a
    grad_tokens = grad_mid + norm_back(grad_attn_in * (1.0 + scale_a), normed_a, inverse_a)
    grad_bias = jnp.concatenate(
        [
            grad_bias_query,
            grad_bias_value,
            jnp.sum(grad_attn.astype(f32), axis=0),
            jnp.sum(grad_mlp.astype(f32), axis=0),
            grad_bias_in.reshape(-1),
        ]
    )
    bias_rows = lax.all_to_all(
        grad_bias.reshape(device_count, -1), ("dp", "mod"), split_axis=0, concat_axis=0, tiled=True
    )
    bias_sum = jnp.sum(bias_rows, axis=0)

    grad_token_mod = jnp.concatenate(
        [grad_attn_in, grad_scale_a, grad_gate_a, grad_mlp_in, grad_scale_m, grad_gate_m], axis=1
    )
    token_high = lax.reduce_precision(grad_token_mod, 8, 7)
    token_low = (grad_token_mod - token_high).astype(bf16)
    grad_pair = contract_rows(slot_pick, token_high.astype(bf16)) + contract_rows(slot_pick, token_low)
    grad_pair = grad_pair.astype(bf16)
    columns = grad_pair.shape[1] // 2
    pair_own = jnp.where(mod_rank == 0, grad_pair[:, :columns], grad_pair[:, columns:])
    pair_send = jnp.where(mod_rank == 0, grad_pair[:, columns:], grad_pair[:, :columns])
    grad_mod = summed(pair_own, net.swap(pair_send, "mod"))
    grad_silu = times_rows(grad_mod, ada_weight)
    silu_own = jnp.where(mod_rank == 0, grad_silu[:crop_count], grad_silu[crop_count:])
    silu_send = jnp.where(mod_rank == 0, grad_silu[crop_count:], grad_silu[:crop_count])
    grad_silu = silu_own + net.swap(silu_send.astype(bf16), "mod").astype(f32)
    own_cond = lax.dynamic_slice_in_dim(cond, mod_rank * crop_count, crop_count, 0).astype(f32)
    silu_back = jax.vjp(jax.nn.silu, own_cond)[1]
    grad_cond = silu_back(grad_silu)[0]
    mod_rows = all_rows(grad_mod)
    own_cols = width // net.dp
    cond_cols = lax.dynamic_slice_in_dim(cond_rows, net.dp_rank * own_cols, own_cols, 1)
    ada_w_sum = contract_rows(cond_cols, mod_rows)
    ada_b_sum = jnp.sum(mod_rows.astype(f32), axis=0).reshape(ada_bias.shape[0], width)
    ada_b_sum = lax.dynamic_slice_in_dim(ada_b_sum, net.dp_rank * own_cols, own_cols, 1)

    fc_sum = s_fc.rest()
    attn_sum = s_attn.rest()[0]
    return (
        result[None],
        grad_tokens[None],
        grad_cond,
        ada_w_sum,
        ada_b_sum,
        attn_sum,
        fc_sum[0],
        fc_sum[1],
        bias_sum,
    )


def solution(mesh):
    placed = (
        P(("dp", "mod"), None, None),
        P("dp", None),
        P(("dp", "mod"), None),
        P("dp", None),
        P(None, "mod"),
        P("mod", None),
        P(("dp", "mod"), None),
        P(("dp", "mod"), None),
        P(("dp", "mod"), None),
        P(("dp", "mod")),
        P(("dp", "mod"), None, None),
    )
    return jax.shard_map(
        on_device,
        mesh=mesh,
        in_specs=placed,
        out_specs=(
            P(("dp", "mod"), None, None),
            P(("dp", "mod"), None, None),
            P(("dp", "mod"), None),
            P("dp", "mod"),
            P("mod", "dp"),
            P(("dp", "mod"), None),
            P(("dp", "mod"), None),
            P(("dp", "mod"), None),
            P(("dp", "mod")),
        ),
        check_vma=False,
    )
```

time: 715 us -> 502 us (0.70)
  waiting for transfers between devices: 307 us -> 215 us
  blocking collectives: 79.6 us -> 0 us
  matrix products: 102 us -> 36.2 us
  Pallas kernels: 33.7 us -> 66.7 us
  local copies, waits for them, and re-layouts: 41.3 us -> 55.9 us
  starting transfers between devices: 83 us -> 70.3 us
  other arithmetic: 56 us -> 45.2 us
    ppermute x66 -> x47, waiting for transfers between devices: 277 us -> 180 us  [swap(): lax.ppermute(value, 'dp', [(i, i ^ 1 << dim) for i in range(self.dp)])]
    unnamed x2 -> x0, blocking collectives: 79.6 us -> none
    dot_general x50 -> x24, matrix products: 102 us -> 36.2 us  [the longest x18 27.9 us: dot(): lax.dot_general(left, right, (((left_dim,), (right_dim,)), ((), ())), pre...]
    pallas_call x2 -> x7, Pallas kernels: 33.7 us -> 66.7 us  [the longest x3 34 us: mlp_part(): pl.pallas_call(functools.partial(mlp_kernel, not before), in_specs=[vmem_...]
    concatenate x32 -> x28, other arithmetic: 25.7 us -> 3.88 us  [the longest x1 1.44 us: on_device(): grad_bias_in = jnp.concatenate(grad_bias_in, axis=1)]
    ppermute x66 -> x47, starting transfers between devices: 63.1 us -> 46.6 us  [swap(): lax.ppermute(value, 'dp', [(i, i ^ 1 << dim) for i in range(self.dp)])]
    another operation x5 -> x11, local copies, waits for them, and re-layouts: 0.52 us -> 11.1 us  [the longest x6 6.24 us: on_device(): column = columns[2 * n + side].reshape(chips // 2, third)]
    all_to_all x0 -> x2, starting transfers between devices: none -> 8.08 us  [the longest x1 5.19 us: on_device(): lax.all_to_all(grad_bias.reshape(device_count, -1), ('dp', 'mod'), split_...]
  transfers between devices with their start and end apart: 83 -> 64, of which waited for: 34 -> 31; matrix products, arithmetic and copies ran while one was open for 25% -> 20% of each run, Pallas kernels for 5% -> 11%
where the time goes in v3:
time: 502 us; the launch traced here: 492 us
  waiting for transfers between devices  215 us (43%)
  starting transfers between devices  70.3 us (14%)
  Pallas kernels  66.7 us (13%)
  local copies, waits for them, and re-layouts  55.9 us (11%)
  other arithmetic  45.2 us (9%)
  matrix products  36.2 us (7%)
    ppermute x47, waiting for transfers between devices, swap(): lax.ppermute(value, 'dp', [(i, i ^ 1 << dim) for i in range(self.dp)])  180 us
    ppermute x47, starting transfers between devices, swap(): lax.ppermute(value, 'dp', [(i, i ^ 1 << dim) for i in range(self.dp)])  46.6 us
    pallas_call x3, Pallas kernels, mlp_part(): pl.pallas_call(functools.partial(mlp_kernel, not before), in_specs=[vmem_...  34 us
    ppermute x15, waiting for transfers between devices, swap(): return lax.ppermute(value, 'mod', [(i, i ^ 1) for i in range(self.mod)])  30.3 us
    unnamed x209, local copies, waits for them, and re-layouts  28.3 us
    dot_general x18, matrix products, dot(): lax.dot_general(left, right, (((left_dim,), (right_dim,)), ((), ())), pre...  27.9 us
    ppermute x15, starting transfers between devices, swap(): return lax.ppermute(value, 'mod', [(i, i ^ 1) for i in range(self.mod)])  15.7 us
    convert_element_type x19, other arithmetic, summed(): return (left.astype(f32) + right.astype(f32)).astype(bf16)  14.1 us
  transfers between devices with their start and end apart: 64, of which 31 were waited for; matrix products, arithmetic and copies ran while one was open for 20% of the time, Pallas kernels for 11%

profile of v3, /device:TPU:0, one launch (start us, length us, event | category | flops | bytes accessed | tf_op | source)
XLA Modules:
  0.0 492.1 jit_solution(13536016411768636347)
XLA Ops:
  0.7 4.1 collective-permute-start.2
  5.5 4.5 fusion.2
  10.1 1.6 collective-permute-start
  13.7 2.9 all-to-all-start
  18.8 5.2 %all-to-all-done = bf16[32,2,144]{2,1,0:T(2,128)(2,1)S(1)} async-done(((bf16[32,2,144]{2,1,0:T(2,128)(2,1)}), bf16[32,2,144]{2,1,0:T(2,128)(2,1)S(1)}, u32[]{:S(2)}, u32[]{:S(2)}) %all-to-all-start) | async-done | bytes 18464 | tf_op jit(solution)/shard_map/all_to_all | solution.py:446
  30.8 2.0 collective-permute-start.13
  32.8 5.0 %collective-permute-done.9 = bf16[1,96,1152]{2,1,0:T(8,128)(2,1)S(1)} collective-permute-done((bf16[1,96,1152]{2,1,0:T(8,128)(2,1)S(1)}, bf16[1,96,1152]{2,1,0:T(8,128)(2,1)S(1)}, u32[]{:S(2)}, u32[]{:S(2)}) %collective-permute-start.9) | collective-permute-done | bytes 221216 | tf_op jit(solution)/shard_map/ppermute | solution.py:70
  40.0 7.8 %collective-permute-done.10 = bf16[1,192,1152]{2,1,0:T(8,128)(2,1)S(1)} collective-permute-done((bf16[1,192,1152]{2,1,0:T(8,128)(2,1)S(1)}, bf16[1,192,1152]{2,1,0:T(8,128)(2,1)S(1)}, u32[]{:S(2)}, u32[]{:S(2)}) %collective-permute-start.10) | collective-permute-done | bytes 442400 | tf_op jit(solution)/shard_map/ppermute | solution.py:69
  48.0 2.5 collective-permute-done.4
  50.6 2.0 collective-permute-start.5
  52.6 5.9 %collective-permute-done.7 = bf16[1,192,1152]{2,1,0:T(8,128)(2,1)S(1)} collective-permute-done((bf16[1,192,1152]{2,1,0:T(8,128)(2,1)S(1)}, bf16[1,192,1152]{2,1,0:T(8,128)(2,1)S(1)}, u32[]{:S(2)}, u32[]{:S(2)}) %collective-permute-start.7) | collective-permute-done | bytes 442400 | tf_op jit(solution)/shard_map/ppermute | solution.py:70
  59.2 3.5 collective-permute-done.13
  63.0 5.0 %collective-permute-done.11.refs_5_ = bf16[1,384,1152]{2,1,0:T(8,128)(2,1)S(1)} collective-permute-done((bf16[1,384,1152]{2,1,0:T(8,128)(2,1)S(1)}, bf16[1,384,1152]{2,1,0:T(8,128)(2,1)S(1)}, u32[]{:S(2)}, u32[]{:S(2)}) %collective-permute-start.11) | collective-permute-done | bytes 884768 | tf_op jit(solution)/shard_map/ppermute | solution.py:70
  68.0 12.8 %collective-permute-done.5.refs_1_ = bf16[1,384,1152]{2,1,0:T(8,128)(2,1)S(1)} collective-permute-done((bf16[1,384,1152]{2,1,0:T(8,128)(2,1)S(1)}, bf16[1,384,1152]{2,1,0:T(8,128)(2,1)S(1)}, u32[]{:S(2)}, u32[]{:S(2)}) %collective-permute-start.5) | collective-permute-done | bytes 884768 | tf_op jit(solution)/shard_map/ppermute | solution.py:70
  82.3 9.7 %assemble.1 = bf16[2304,1152]{1,0:T(8,128)(2,1)S(1)} custom-call(s32[48]{0:T(128)S(1)} %concatenate.151.index_ref, bf16[1,384,1152]{2,1,0:T(8,128)(2,1)S(1)} %pad_maximum_fusion.5.refs_0_, bf16[1,384,1152]{2,1,0:T(8,128)(2,1)S(1)} %collective-permute-done.5.refs_1_, bf16[1,384,1152]{2,1,0:T(8,128)(2,1)S(1)} %pad_maximum_fusion.6.refs_2_, ...), custom_call_target="tpu_custom_call" | custom-call | tf_op jit(solution)/shard_map/assemble/pallas_call | solution.py:205
  95.9 9.3 %collective-permute-done.15 = bf16[2,96,1152]{2,1,0:T(8,128)(2,1)S(1)} collective-permute-done((bf16[2,96,1152]{2,1,0:T(8,128)(2,1)S(1)}, bf16[2,96,1152]{2,1,0:T(8,128)(2,1)S(1)}, u32[]{:S(2)}, u32[]{:S(2)}) %collective-permute-start.15) | collective-permute-done | bytes 442400 | tf_op jit(solution)/shard_map/ppermute | solution.py:70
  107.5 2.5 add_convert_fusion
  110.1 5.8 %attention.1 = bf16[4,144,512]{2,1,0:T(8,128)(2,1)S(1)} custom-call(s32[2,256]{1,0:T(2,128)S(1)} %pad_add_fusion.row_ref, s32[256,2]{1,0:T(8,128)S(1)} %bitcast.180, bf16[3,4,144,512]{3,2,1,0:T(8,128)(2,1)S(1)} %bitcast.168, bf16[3,4,144,512]{3,2,1,0:T(8,128)(2,1)S(1)} %bitcast.169, bf16[3,4,144,512]{3,2,1,0:T(8,128)(2,1)S(1)} %bitcast.170), custom_call_target="tpu_custom_call" | custom-call | flops 301989888 | bytes 2654208 | tf_op jit(solution)/shard_map/attention/pallas_call | solution.py:322
  117.5 6.2 %collective-permute-done.17 = bf16[2,192,1152]{2,1,0:T(8,128)(2,1)S(1)} collective-permute-done((bf16[2,192,1152]{2,1,0:T(8,128)(2,1)S(1)}, bf16[2,192,1152]{2,1,0:T(8,128)(2,1)S(1)}, u32[]{:S(2)}, u32[]{:S(2)}) %collective-permute-start.17) | collective-permute-done | bytes 884768 | tf_op jit(solution)/shard_map/ppermute | solution.py:70
  123.7 3.2 collective-permute-done.19
  129.6 2.2 fusion.105
  140.5 38.3 %collective-permute-done.36 = bf16[16,1152]{1,0:T(8,128)(2,1)S(1)} collective-permute-done((bf16[16,1152]{1,0:T(8,128)(2,1)S(1)}, bf16[16,1152]{1,0:T(8,128)(2,1)S(1)}, u32[]{:S(2)}, u32[]{:S(2)}) %collective-permute-start.36) | collective-permute-done | bytes 36896 | tf_op jit(solution)/shard_map/ppermute | solution.py:70
  180.3 2.9 collective-permute-done.37
  183.2 4.0 collective-permute-start.38
  187.2 5.0 %collective-permute-done.38 = bf16[64,1152]{1,0:T(8,128)(2,1)S(1)} collective-permute-done((bf16[64,1152]{1,0:T(8,128)(2,1)S(1)}, bf16[64,1152]{1,0:T(8,128)(2,1)S(1)}, u32[]{:S(2)}, u32[]{:S(2)}) %collective-permute-start.38) | collective-permute-done | bytes 147488 | tf_op jit(solution)/shard_map/ppermute | solution.py:70
  192.4 1.5 collective-permute-done.39
  196.1 10.3 %mlp_part.3 = (bf16[2,384,1152]{2,1,0:T(8,128)(2,1)}, bf16[2,384,1152]{2,1,0:T(8,128)(2,1)}, f32[2,384]{1,0:T(2,128)S(1)}, f32[256,1152]{1,0:T(8,128)S(1)}, f32[...) custom-call(bf16[512,1152]{1,0:T(8,128)(2,1)S(1)} %pad_maximum_fusion.3.x_ref, ...), custom_call_target="tpu_custom_call" | custom-call | flops 5435817984 | bytes 14155776 | tf_op jit(solution)/shard_map/mlp_part/pallas_call | solution.py:380
  211.7 12.0 %mlp_part.4 = (bf16[2,384,1152]{2,1,0:T(8,128)(2,1)}, bf16[2,384,1152]{2,1,0:T(8,128)(2,1)}, f32[2,384]{1,0:T(2,128)S(1)}, f32[256,1152]{1,0:T(8,128)S(1)}, f32[...) custom-call(bf16[512,1152]{1,0:T(8,128)(2,1)S(1)} %pad_maximum_fusion.3.x_ref, ...), custom_call_target="tpu_custom_call" | custom-call | flops 5435817984 | bytes 14155776 | tf_op jit(solution)/shard_map/mlp_part/pallas_call | solution.py:380
  229.2 11.6 %mlp_part.5 = (bf16[2,384,1152]{2,1,0:T(8,128)(2,1)}, bf16[2,384,1152]{2,1,0:T(8,128)(2,1)}, f32[2,384]{1,0:T(2,128)S(1)}, f32[256,1152]{1,0:T(8,128)S(1)}, f32[...) custom-call(bf16[512,1152]{1,0:T(8,128)(2,1)S(1)} %pad_maximum_fusion.3.x_ref, ...), custom_call_target="tpu_custom_call" | custom-call | flops 5435817984 | bytes 14155776 | tf_op jit(solution)/shard_map/mlp_part/pallas_call | solution.py:380
  245.9 1.6 fusion.69
  255.0 1.8 convolution_add_fusion.3
  256.8 1.6 convolution_add_fusion.4
  258.3 1.5 fusion.67
  264.8 2.9 fusion.101
  267.8 5.3 %convert_reduce_fusion.4 = (f32[1152]{0:T(1024)}, bf16[256,1152]{1,0:T(8,128)(2,1)S(1)}, f32[256,1152]{1,0:T(8,128)}, bf16[1,256,1152]{2,1,0:T(8,128)(2,1)}) fusion(f32[256,6912]{1,0:T(8,128)} %copy-done.19, f32[256]{0:T(256)S(1)} %broadcast_multiply_fusion.2, f32[256]{0:T(256)S(1)} %copy-done.66, f32[256,1152]{1,0:T(8,128)S(1)} %copy-done.21, ...), kind=kLoop, calls=%fused_computation.68 | loop fusion | flops 5602176 | bytes 11219968 | tf_op jit(solution)/shard_map/reduce_sum | solution.py:606
  275.2 1.8 broadcast_select_fusion.1
  277.6 7.5 %attention_back.1 = bf16[3,4,144,512]{3,2,1,0:T(8,128)(2,1)S(1)} custom-call(s32[2,256]{1,0:T(2,128)S(1)} %pad_add_fusion.row_ref, s32[256,2]{1,0:T(8,128)S(1)} %bitcast.181, bf16[3,4,144,512]{3,2,1,0:T(8,128)(2,1)S(1)} %bitcast.171, bf16[3,4,144,512]{3,2,1,0:T(8,128)(2,1)S(1)} %bitcast.172, bf16[3,4,144,512]{3,2,1,0:T(8,128)(2,1)S(1)} %bitcast.173, ...), custom_call_target="tpu_custom_call" | custom-call | flops 754974720 | bytes 4423680 | tf_op jit(solution)/shard_map/attention_back/pallas_call | solution.py:332
  285.0 19.6 %collective-permute-done.32 = bf16[2,384,1152]{2,1,0:T(8,128)(2,1)S(1)} collective-permute-done((bf16[2,384,1152]{2,1,0:T(8,128)(2,1)}, bf16[2,384,1152]{2,1,0:T(8,128)(2,1)S(1)}, u32[]{:S(2)}, u32[]{:S(2)}) %collective-permute-start.32) | collective-permute-done | bytes 1769504 | tf_op jit(solution)/shard_map/ppermute | solution.py:70
  305.4 4.0 fusion.5
  325.6 5.2 %all-to-all-start.1 = ((f32[32,1,288]{2,1,0:T(1,128)}), f32[32,1,288]{2,1,0:T(1,128)}, u32[]{:S(2)}, u32[]{:S(2)}) async-start(f32[32,1,288]{2,1,0:T(1,128)} %all_to_all.11), calls=%async_computation.1 | async-start | bytes 98304 | tf_op jit(solution)/shard_map/all_to_all | solution.py:611
  330.8 3.3 add_convert_fusion.6
  334.2 1.7 collective-permute-start.55
  335.9 1.6 add_convert_fusion.4
  340.1 4.4 convolution_convert_fusion.1.first_ref
  348.8 1.8 fusion.11.second_ref
  351.3 9.9 %split_pieces.1 = (bf16[1,384,1152]{2,1,0:T(8,128)(2,1)S(1)}, bf16[1,384,1152]{2,1,0:T(8,128)(2,1)S(1)}, bf16[1,384,1152]{2,1,0:T(8,128)(2,1)S(1)}, bf16[1,384,1...) custom-call(s32[48]{0:T(128)S(1)} %concatenate.151.index_ref, ...), custom_call_target="tpu_custom_call" | custom-call | tf_op jit(solution)/shard_map/split_pieces/pallas_call | solution.py:248
  365.7 2.4 fusion.102
  375.5 1.5 collective-permute-start.34
  378.1 11.3 %collective-permute-done.34 = bf16[16,3456]{1,0:T(8,128)(2,1)S(1)} collective-permute-done((bf16[16,3456]{1,0:T(8,128)(2,1)S(1)}, bf16[16,3456]{1,0:T(8,128)(2,1)S(1)}, u32[]{:S(2)}, u32[]{:S(2)}) %collective-permute-start.34) | collective-permute-done | bytes 110624 | tf_op jit(solution)/shard_map/ppermute | solution.py:69
  391.0 2.2 fusion.112
  393.9 7.7 %collective-permute-done.35 = bf16[8,1152]{1,0:T(8,128)(2,1)S(1)} collective-permute-done((bf16[8,1152]{1,0:T(8,128)(2,1)S(1)}, bf16[8,1152]{1,0:T(8,128)(2,1)S(1)}, u32[]{:S(2)}, u32[]{:S(2)}) %collective-permute-start.35) | collective-permute-done | bytes 18464 | tf_op jit(solution)/shard_map/ppermute | solution.py:69
  404.7 7.8 %collective-permute-done.58 = bf16[2,96,1152]{2,1,0:T(8,128)(2,1)S(1)} collective-permute-done((bf16[2,96,1152]{2,1,0:T(8,128)(2,1)S(1)}, bf16[2,96,1152]{2,1,0:T(8,128)(2,1)S(1)}, u32[]{:S(2)}, u32[]{:S(2)}) %collective-permute-start.58) | collective-permute-done | bytes 442400 | tf_op jit(solution)/shard_map/ppermute | solution.py:70
  414.7 2.5 collective-permute-start.61
  418.1 17.1 %collective-permute-done.41 = bf16[32,3456]{1,0:T(8,128)(2,1)S(1)} collective-permute-done((bf16[32,3456]{1,0:T(8,128)(2,1)S(1)}, bf16[32,3456]{1,0:T(8,128)(2,1)S(1)}, u32[]{:S(2)}, u32[]{:S(2)}) %collective-permute-start.41) | collective-permute-done | bytes 221216 | tf_op jit(solution)/shard_map/ppermute | solution.py:70
  435.9 1.5 collective-permute-start.46
  437.7 2.3 collective-permute-start.49
  440.1 1.6 collective-permute-start.52
  441.7 12.4 %collective-permute-done.61 = bf16[2,144,1152]{2,1,0:T(8,128)(2,1)S(1)} collective-permute-done((bf16[2,144,1152]{2,1,0:T(8,128)(2,1)S(1)}, bf16[2,144,1152]{2,1,0:T(8,128)(2,1)S(1)}, u32[]{:S(2)}, u32[]{:S(2)}) %collective-permute-start.61) | collective-permute-done | bytes 663584 | tf_op jit(solution)/shard_map/ppermute | solution.py:70
  455.4 1.5 collective-permute-start.47
  457.0 6.6 %collective-permute-done.49 = bf16[1,192,1152]{2,1,0:T(8,128)(2,1)S(1)} collective-permute-done((bf16[1,192,1152]{2,1,0:T(8,128)(2,1)S(1)}, bf16[1,192,1152]{2,1,0:T(8,128)(2,1)S(1)}, u32[]{:S(2)}, u32[]{:S(2)}) %collective-permute-start.49) | collective-permute-done | bytes 442400 | tf_op jit(solution)/shard_map/ppermute | solution.py:70
  464.2 5.5 %collective-permute-done.50 = bf16[1,96,1152]{2,1,0:T(8,128)(2,1)S(1)} collective-permute-done((bf16[1,96,1152]{2,1,0:T(8,128)(2,1)S(1)}, bf16[1,96,1152]{2,1,0:T(8,128)(2,1)S(1)}, u32[]{:S(2)}, u32[]{:S(2)}) %collective-permute-start.50) | collective-permute-done | bytes 221216 | tf_op jit(solution)/shard_map/ppermute | solution.py:70
  470.0 7.8 %collective-permute-start.54 = (bf16[1,144,1152]{2,1,0:T(8,128)(2,1)S(1)}, bf16[1,144,1152]{2,1,0:T(8,128)(2,1)S(1)}, u32[]{:S(2)}, u32[]{:S(2)}) collective-permute-start(bf16[1,144,1152]{2,1,0:T(8,128)(2,1)S(1)} %slice.464), channel_id=1, source_target_pairs={{0,16},{2,18},{4,20},{6,22},{8,24},{10,26},{12,28},{14,30},{16,0},... | collective-permute-start | bytes 995336 | tf_op jit(solution)/shard_map/ppermute | solution.py:70
  477.8 9.7 %collective-permute-done.54 = bf16[1,144,1152]{2,1,0:T(8,128)(2,1)S(1)} collective-permute-done((bf16[1,144,1152]{2,1,0:T(8,128)(2,1)S(1)}, bf16[1,144,1152]{2,1,0:T(8,128)(2,1)S(1)}, u32[]{:S(2)}, u32[]{:S(2)}) %collective-permute-start.54) | collective-permute-done | bytes 331808 | tf_op jit(solution)/shard_map/ppermute | solution.py:70
  488.9 2.4 fusion.43
  (456 shorter events, 120.9 us)
Async XLA Ops:
  0.7 27.7 %collective-permute-start.2 = (bf16[1,144,1152]{2,1,0:T(8,128)(2,1)}, bf16[1,144,1152]{2,1,0:T(8,128)(2,1)S(1)}, u32[]{:S(2)}, u32[]{:S(2)}) collective-permute-start(bf16[1,144,1152]{2,1,0:T(8,128)(2,1)} %bitcast.226), channel_id=1, source_target_pairs={{0,16},{2,18},{4,20},{6,22},{8,24},{10,26},{12,28},{14,30},{16,0},... | collective-permute-start | bytes 995336 | tf_op jit(solution)/shard_map/ppermute | solution.py:70
  10.1 17.0 %collective-permute-start = (bf16[16,3456]{1,0:T(8,128)(2,1)S(1)}, bf16[16,3456]{1,0:T(8,128)(2,1)S(1)}, u32[]{:S(2)}, u32[]{:S(2)}) collective-permute-start(bf16[16,3456]{1,0:T(8,128)(2,1)S(1)} %fusion.2), channel_id=1, source_target_pairs={{0,1},{1,0},{2,3},{3,2},{4,5},{5,4},{6,7},{7,6},{8,9},{9,8},{10,11... | collective-permute-start | bytes 331784 | tf_op jit(solution)/shard_map/ppermute | solution.py:69
  13.7 10.3 %all-to-all-start = ((bf16[32,2,144]{2,1,0:T(2,128)(2,1)}), bf16[32,2,144]{2,1,0:T(2,128)(2,1)S(1)}, u32[]{:S(2)}, u32[]{:S(2)}) async-start(bf16[32,2,144]{2,1,0:T(2,128)(2,1)} %reshape.402), calls=%async_computation | async-start | bytes 65536 | tf_op jit(solution)/shard_map/all_to_all | solution.py:446
  16.7 2.0 collective-permute-start.1
  28.5 9.3 %collective-permute-start.9 = (bf16[1,96,1152]{2,1,0:T(8,128)(2,1)S(1)}, bf16[1,96,1152]{2,1,0:T(8,128)(2,1)S(1)}, u32[]{:S(2)}, u32[]{:S(2)}) collective-permute-start(bf16[1,96,1152]{2,1,0:T(8,128)(2,1)S(1)} %bitcast.211), channel_id=1, source_target_pairs={{0,8},{2,10},{4,12},{6,14},{8,0},{10,2},{12,4},{14,6},{16,24},{18,... | collective-permute-start | bytes 663560 | tf_op jit(solution)/shard_map/ppermute | solution.py:70
  29.3 29.8 %collective-permute-start.12 = (bf16[256,1152]{1,0:T(8,128)(2,1)S(1)}, bf16[256,1152]{1,0:T(8,128)(2,1)S(1)}, u32[]{:S(2)}, u32[]{:S(2)}) collective-permute-start(bf16[256,1152]{1,0:T(8,128)(2,1)S(1)} %fusion.21), channel_id=1, source_target_pairs={{0,2},{2,0},{4,6},{6,4},{8,10},{10,8},{12,14},{14,12},{16,18},{18,... | collective-permute-start | bytes 1769480 | tf_op jit(solution)/shard_map/ppermute | solution.py:70
  29.4 8.6 %collective-permute-start.3 = (bf16[1,96,1152]{2,1,0:T(8,128)(2,1)S(1)}, bf16[1,96,1152]{2,1,0:T(8,128)(2,1)S(1)}, u32[]{:S(2)}, u32[]{:S(2)}) collective-permute-start(bf16[1,96,1152]{2,1,0:T(8,128)(2,1)S(1)} %bitcast.208), channel_id=1, source_target_pairs={{0,1},{1,0},{2,3},{3,2},{4,5},{5,4},{6,7},{7,6},{8,9},{9,8},{10,11... | collective-permute-start | bytes 663560 | tf_op jit(solution)/shard_map/ppermute | solution.py:69
  30.2 8.3 %collective-permute-start.6 = (bf16[1,96,1152]{2,1,0:T(8,128)(2,1)S(1)}, bf16[1,96,1152]{2,1,0:T(8,128)(2,1)S(1)}, u32[]{:S(2)}, u32[]{:S(2)}) collective-permute-start(bf16[1,96,1152]{2,1,0:T(8,128)(2,1)S(1)} %bitcast.205), channel_id=1, source_target_pairs={{0,4},{2,6},{4,0},{6,2},{8,12},{10,14},{12,8},{14,10},{16,20},{18,... | collective-permute-start | bytes 663560 | tf_op jit(solution)/shard_map/ppermute | solution.py:70
  30.8 31.9 %collective-permute-start.13 = (bf16[2,144,1152]{2,1,0:T(8,128)(2,1)S(1)}, bf16[2,144,1152]{2,1,0:T(8,128)(2,1)S(1)}, u32[]{:S(2)}, u32[]{:S(2)}) collective-permute-start(bf16[2,144,1152]{2,1,0:T(8,128)(2,1)S(1)} %pad_maximum_fusion.13), channel_id=1, source_target_pairs={{0,16},{2,18},{4,20},{6,22},{8,24},{10,26},{12,28},{14,30},{16,0},... | collective-permute-start | bytes 1990664 | tf_op jit(solution)/shard_map/ppermute | solution.py:70
  37.9 10.0 %collective-permute-start.10 = (bf16[1,192,1152]{2,1,0:T(8,128)(2,1)S(1)}, bf16[1,192,1152]{2,1,0:T(8,128)(2,1)S(1)}, u32[]{:S(2)}, u32[]{:S(2)}) collective-permute-start(bf16[1,192,1152]{2,1,0:T(8,128)(2,1)S(1)} %pad_maximum_fusion.18), channel_id=1, source_target_pairs={{0,1},{1,0},{2,3},{3,2},{4,5},{5,4},{6,7},{7,6},{8,9},{9,8},{10,11... | collective-permute-start | bytes 1327112 | tf_op jit(solution)/shard_map/ppermute | solution.py:69
  38.0 12.5 %collective-permute-start.4 = (bf16[1,192,1152]{2,1,0:T(8,128)(2,1)S(1)}, bf16[1,192,1152]{2,1,0:T(8,128)(2,1)S(1)}, u32[]{:S(2)}, u32[]{:S(2)}) collective-permute-start(bf16[1,192,1152]{2,1,0:T(8,128)(2,1)S(1)} %pad_maximum_fusion.16), channel_id=1, source_target_pairs={{0,4},{2,6},{4,0},{6,2},{8,12},{10,14},{12,8},{14,10},{16,20},{18,... | collective-permute-start | bytes 1327112 | tf_op jit(solution)/shard_map/ppermute | solution.py:70
  38.6 19.9 %collective-permute-start.7 = (bf16[1,192,1152]{2,1,0:T(8,128)(2,1)S(1)}, bf16[1,192,1152]{2,1,0:T(8,128)(2,1)S(1)}, u32[]{:S(2)}, u32[]{:S(2)}) collective-permute-start(bf16[1,192,1152]{2,1,0:T(8,128)(2,1)S(1)} %pad_maximum_fusion.17), channel_id=1, source_target_pairs={{0,8},{2,10},{4,12},{6,14},{8,0},{10,2},{12,4},{14,6},{16,24},{18,... | collective-permute-start | bytes 1327112 | tf_op jit(solution)/shard_map/ppermute | solution.py:70
  48.0 20.1 %collective-permute-start.11 = (bf16[1,384,1152]{2,1,0:T(8,128)(2,1)S(1)}, bf16[1,384,1152]{2,1,0:T(8,128)(2,1)S(1)}, u32[]{:S(2)}, u32[]{:S(2)}) collective-permute-start(bf16[1,384,1152]{2,1,0:T(8,128)(2,1)S(1)} %pad_maximum_fusion.7.refs_4_), channel_id=1, source_target_pairs={{0,4},{2,6},{4,0},{6,2},{8,12},{10,14},{12,8},{14,10},{16,20},{18,... | collective-permute-start | bytes 2654216 | tf_op jit(solution)/shard_map/ppermute | solution.py:70
  50.6 30.3 %collective-permute-start.5 = (bf16[1,384,1152]{2,1,0:T(8,128)(2,1)S(1)}, bf16[1,384,1152]{2,1,0:T(8,128)(2,1)S(1)}, u32[]{:S(2)}, u32[]{:S(2)}) collective-permute-start(bf16[1,384,1152]{2,1,0:T(8,128)(2,1)S(1)} %pad_maximum_fusion.5.refs_0_), channel_id=1, source_target_pairs={{0,8},{2,10},{4,12},{6,14},{8,0},{10,2},{12,4},{14,6},{16,24},{18,... | collective-permute-start | bytes 2654216 | tf_op jit(solution)/shard_map/ppermute | solution.py:70
  58.5 22.3 %collective-permute-start.8 = (bf16[1,384,1152]{2,1,0:T(8,128)(2,1)S(1)}, bf16[1,384,1152]{2,1,0:T(8,128)(2,1)S(1)}, u32[]{:S(2)}, u32[]{:S(2)}) collective-permute-start(bf16[1,384,1152]{2,1,0:T(8,128)(2,1)S(1)} %pad_maximum_fusion.6.refs_2_), channel_id=1, source_target_pairs={{0,1},{1,0},{2,3},{3,2},{4,5},{5,4},{6,7},{7,6},{8,9},{9,8},{10,11... | collective-permute-start | bytes 2654216 | tf_op jit(solution)/shard_map/ppermute | solution.py:69
  80.8 13.8 %collective-permute-start.14 = (bf16[2,96,1152]{2,1,0:T(8,128)(2,1)S(1)}, bf16[2,96,1152]{2,1,0:T(8,128)(2,1)S(1)}, u32[]{:S(2)}, u32[]{:S(2)}) collective-permute-start(bf16[2,96,1152]{2,1,0:T(8,128)(2,1)S(1)} %bitcast.199), channel_id=1, source_target_pairs={{0,1},{1,0},{2,3},{3,2},{4,5},{5,4},{6,7},{7,6},{8,9},{9,8},{10,11... | collective-permute-start | bytes 1327112 | tf_op jit(solution)/shard_map/ppermute | solution.py:69
  92.1 35.9 %collective-permute-start.21 = (bf16[576,1152]{1,0:T(8,128)(2,1)S(1)}, bf16[576,1152]{1,0:T(8,128)(2,1)S(1)}, u32[]{:S(2)}, u32[]{:S(2)}) collective-permute-start(bf16[576,1152]{1,0:T(8,128)(2,1)S(1)} %slice.428), channel_id=1, source_target_pairs={{0,2},{2,0},{4,6},{6,4},{8,10},{10,8},{12,14},{14,12},{16,18},{18,... | collective-permute-start | bytes 3981320 | tf_op jit(solution)/shard_map/ppermute | solution.py:70
  92.2 13.0 %collective-permute-start.15 = (bf16[2,96,1152]{2,1,0:T(8,128)(2,1)S(1)}, bf16[2,96,1152]{2,1,0:T(8,128)(2,1)S(1)}, u32[]{:S(2)}, u32[]{:S(2)}) collective-permute-start(bf16[2,96,1152]{2,1,0:T(8,128)(2,1)S(1)} %bitcast.193), channel_id=1, source_target_pairs={{0,4},{2,6},{4,0},{6,2},{8,12},{10,14},{12,8},{14,10},{16,20},{18,... | collective-permute-start | bytes 1327112 | tf_op jit(solution)/shard_map/ppermute | solution.py:70
  93.6 12.2 %collective-permute-start.16 = (bf16[2,96,1152]{2,1,0:T(8,128)(2,1)S(1)}, bf16[2,96,1152]{2,1,0:T(8,128)(2,1)S(1)}, u32[]{:S(2)}, u32[]{:S(2)}) collective-permute-start(bf16[2,96,1152]{2,1,0:T(8,128)(2,1)S(1)} %bitcast.196), channel_id=1, source_target_pairs={{0,8},{2,10},{4,12},{6,14},{8,0},{10,2},{12,4},{14,6},{16,24},{18,... | collective-permute-start | bytes 1327112 | tf_op jit(solution)/shard_map/ppermute | solution.py:70
  94.7 29.0 %collective-permute-start.17 = (bf16[2,192,1152]{2,1,0:T(8,128)(2,1)S(1)}, bf16[2,192,1152]{2,1,0:T(8,128)(2,1)S(1)}, u32[]{:S(2)}, u32[]{:S(2)}) collective-permute-start(bf16[2,192,1152]{2,1,0:T(8,128)(2,1)S(1)} %pad_maximum_fusion.8), channel_id=1, source_target_pairs={{0,4},{2,6},{4,0},{6,2},{8,12},{10,14},{12,8},{14,10},{16,20},{18,... | collective-permute-start | bytes 2654216 | tf_op jit(solution)/shard_map/ppermute | solution.py:70
  105.9 21.0 %collective-permute-start.19 = (bf16[2,192,1152]{2,1,0:T(8,128)(2,1)S(1)}, bf16[2,192,1152]{2,1,0:T(8,128)(2,1)S(1)}, u32[]{:S(2)}, u32[]{:S(2)}) collective-permute-start(bf16[2,192,1152]{2,1,0:T(8,128)(2,1)S(1)} %pad_maximum_fusion.10), channel_id=1, source_target_pairs={{0,1},{1,0},{2,3},{3,2},{4,5},{5,4},{6,7},{7,6},{8,9},{9,8},{10,11... | collective-permute-start | bytes 2654216 | tf_op jit(solution)/shard_map/ppermute | solution.py:69
  107.2 20.7 %collective-permute-start.18 = (bf16[2,192,1152]{2,1,0:T(8,128)(2,1)S(1)}, bf16[2,192,1152]{2,1,0:T(8,128)(2,1)S(1)}, u32[]{:S(2)}, u32[]{:S(2)}) collective-permute-start(bf16[2,192,1152]{2,1,0:T(8,128)(2,1)S(1)} %pad_maximum_fusion.9), channel_id=1, source_target_pairs={{0,8},{2,10},{4,12},{6,14},{8,0},{10,2},{12,4},{14,6},{16,24},{18,... | collective-permute-start | bytes 2654216 | tf_op jit(solution)/shard_map/ppermute | solution.py:70
  127.9 1.6 collective-permute-start.20
  133.3 4.5 collective-permute-start.22
  133.6 61.3 %collective-permute-start.26 = (bf16[2,384,1152]{2,1,0:T(8,128)(2,1)S(1)}, bf16[2,384,1152]{2,1,0:T(8,128)(2,1)S(1)}, u32[]{:S(2)}, u32[]{:S(2)}) collective-permute-start(bf16[2,384,1152]{2,1,0:T(8,128)(2,1)S(1)} %constant_dynamic-update-slice_fusion.6.refs_0_), channel_id=1, source_target_pairs={{0,8},{2,10},{4,12},{6,14},{8,0},{10,2},{12,4},{14,6},{16,24},{18,... | collective-permute-start | bytes 5308424 | tf_op jit(solution)/shard_map/ppermute | solution.py:70
  134.2 5.2 %collective-permute-start.23 = (bf16[256,1152]{1,0:T(8,128)(2,1)S(1)}, bf16[256,1152]{1,0:T(8,128)(2,1)S(1)}, u32[]{:S(2)}, u32[]{:S(2)}) collective-permute-start(bf16[256,1152]{1,0:T(8,128)(2,1)S(1)} %get-tuple-element.92), channel_id=1, source_target_pairs={{0,2},{2,0},{4,6},{6,4},{8,10},{10,8},{12,14},{14,12},{16,18},{18,... | collective-permute-start | bytes 1769480 | tf_op jit(solution)/shard_map/ppermute | solution.py:70
  135.3 75.2 %collective-permute-start.25 = (bf16[2,384,1152]{2,1,0:T(8,128)(2,1)}, bf16[2,384,1152]{2,1,0:T(8,128)(2,1)S(1)}, u32[]{:S(2)}, u32[]{:S(2)}) collective-permute-start(bf16[2,384,1152]{2,1,0:T(8,128)(2,1)} %constant_dynamic-update-slice_fusion.3.refs_0_), channel_id=1, source_target_pairs={{0,1},{1,0},{2,3},{3,2},{4,5},{5,4},{6,7},{7,6},{8,9},{9,8},{10,11... | collective-permute-start | bytes 5308424 | tf_op jit(solution)/shard_map/ppermute | solution.py:69
  137.2 90.7 %collective-permute-start.24 = (bf16[2,384,1152]{2,1,0:T(8,128)(2,1)}, bf16[2,384,1152]{2,1,0:T(8,128)(2,1)S(1)}, u32[]{:S(2)}, u32[]{:S(2)}) collective-permute-start(bf16[2,384,1152]{2,1,0:T(8,128)(2,1)} %constant_dynamic-update-slice_fusion.refs_0_), channel_id=1, source_target_pairs={{0,4},{2,6},{4,0},{6,2},{8,12},{10,14},{12,8},{14,10},{16,20},{18,... | collective-permute-start | bytes 5308424 | tf_op jit(solution)/shard_map/ppermute | solution.py:70
  137.9 40.9 %collective-permute-start.36 = (bf16[16,1152]{1,0:T(8,128)(2,1)S(1)}, bf16[16,1152]{1,0:T(8,128)(2,1)S(1)}, u32[]{:S(2)}, u32[]{:S(2)}) collective-permute-start(bf16[16,1152]{1,0:T(8,128)(2,1)S(1)} %copy-done.50), channel_id=1, source_target_pairs={{0,4},{2,6},{4,0},{6,2},{8,12},{10,14},{12,8},{14,10},{16,20},{18,... | collective-permute-start | bytes 110600 | tf_op jit(solution)/shard_map/ppermute | solution.py:70
  178.9 4.4 collective-permute-start.37
  183.2 9.0 %collective-permute-start.38 = (bf16[64,1152]{1,0:T(8,128)(2,1)S(1)}, bf16[64,1152]{1,0:T(8,128)(2,1)S(1)}, u32[]{:S(2)}, u32[]{:S(2)}) collective-permute-start(bf16[64,1152]{1,0:T(8,128)(2,1)S(1)} %pad_maximum_fusion.22), channel_id=1, source_target_pairs={{0,16},{2,18},{4,20},{6,22},{8,24},{10,26},{12,28},{14,30},{16,0},... | collective-permute-start | bytes 442376 | tf_op jit(solution)/shard_map/ppermute | solution.py:70
  192.3 1.6 collective-permute-start.39
  253.5 11.2 %collective-permute-start.28 = (f32[256,1152]{1,0:T(8,128)}, f32[256,1152]{1,0:T(8,128)}, u32[]{:S(2)}, u32[]{:S(2)}) collective-permute-start(f32[256,1152]{1,0:T(8,128)} %copy-done.10), channel_id=1, source_target_pairs={{0,2},{2,0},{4,6},{6,4},{8,10},{10,8},{12,14},{14,12},{16,18},{18,... | collective-permute-start | bytes 3538952 | tf_op jit(solution)/shard_map/ppermute | solution.py:70
  253.7 14.1 %collective-permute-start.27 = (f32[256,1152]{1,0:T(8,128)}, f32[256,1152]{1,0:T(8,128)}, u32[]{:S(2)}, u32[]{:S(2)}) collective-permute-start(f32[256,1152]{1,0:T(8,128)} %copy-done.9), channel_id=1, source_target_pairs={{0,2},{2,0},{4,6},{6,4},{8,10},{10,8},{12,14},{14,12},{16,18},{18,... | collective-permute-start | bytes 3538952 | tf_op jit(solution)/shard_map/ppermute | solution.py:70
  263.8 40.9 %collective-permute-start.32 = (bf16[2,384,1152]{2,1,0:T(8,128)(2,1)}, bf16[2,384,1152]{2,1,0:T(8,128)(2,1)S(1)}, u32[]{:S(2)}, u32[]{:S(2)}) collective-permute-start(bf16[2,384,1152]{2,1,0:T(8,128)(2,1)} %get-tuple-element.64), channel_id=1, source_target_pairs={{0,4},{2,6},{4,0},{6,2},{8,12},{10,14},{12,8},{14,10},{16,20},{18,... | collective-permute-start | bytes 5308424 | tf_op jit(solution)/shard_map/ppermute | solution.py:70
  264.4 40.6 %collective-permute-start.31 = (bf16[2,384,1152]{2,1,0:T(8,128)(2,1)}, bf16[2,384,1152]{2,1,0:T(8,128)(2,1)S(1)}, u32[]{:S(2)}, u32[]{:S(2)}) collective-permute-start(bf16[2,384,1152]{2,1,0:T(8,128)(2,1)} %get-tuple-element.63), channel_id=1, source_target_pairs={{0,1},{1,0},{2,3},{3,2},{4,5},{5,4},{6,7},{7,6},{8,9},{9,8},{10,11... | collective-permute-start | bytes 5308424 | tf_op jit(solution)/shard_map/ppermute | solution.py:69
  264.7 40.3 %collective-permute-start.30 = (bf16[2,384,1152]{2,1,0:T(8,128)(2,1)}, bf16[2,384,1152]{2,1,0:T(8,128)(2,1)S(1)}, u32[]{:S(2)}, u32[]{:S(2)}) collective-permute-start(bf16[2,384,1152]{2,1,0:T(8,128)(2,1)} %get-tuple-element.62), channel_id=1, source_target_pairs={{0,8},{2,10},{4,12},{6,14},{8,0},{10,2},{12,4},{14,6},{16,24},{18,... | collective-permute-start | bytes 5308424 | tf_op jit(solution)/shard_map/ppermute | solution.py:70
  274.1 3.3 collective-permute-start.29
  277.0 71.8 %collective-permute-start.44 = (bf16[576,1152]{1,0:T(8,128)(2,1)}, bf16[576,1152]{1,0:T(8,128)(2,1)}, u32[]{:S(2)}, u32[]{:S(2)}) collective-permute-start(bf16[576,1152]{1,0:T(8,128)(2,1)} %bitcast.43), channel_id=1, source_target_pairs={{0,2},{2,0},{4,6},{6,4},{8,10},{10,8},{12,14},{14,12},{16,18},{18,... | collective-permute-start | bytes 3981320 | tf_op jit(solution)/shard_map/ppermute | solution.py:70
  325.6 21.7 %all-to-all-start.1 = ((f32[32,1,288]{2,1,0:T(1,128)}), f32[32,1,288]{2,1,0:T(1,128)}, u32[]{:S(2)}, u32[]{:S(2)}) async-start(f32[32,1,288]{2,1,0:T(1,128)} %all_to_all.11), calls=%async_computation.1 | async-start | bytes 98304 | tf_op jit(solution)/shard_map/all_to_all | solution.py:611
  334.2 27.7 %collective-permute-start.55 = (bf16[2,192,1152]{2,1,0:T(8,128)(2,1)}, bf16[2,192,1152]{2,1,0:T(8,128)(2,1)}, u32[]{:S(2)}, u32[]{:S(2)}) collective-permute-start(bf16[2,192,1152]{2,1,0:T(8,128)(2,1)} %get-tuple-element.106), channel_id=1, source_target_pairs={{0,4},{2,6},{4,0},{6,2},{8,12},{10,14},{12,8},{14,10},{16,20},{18,... | collective-permute-start | bytes 2654216 | tf_op jit(solution)/shard_map/ppermute | solution.py:70
  337.5 38.0 %collective-permute-start.57 = (bf16[2,192,1152]{2,1,0:T(8,128)(2,1)}, bf16[2,192,1152]{2,1,0:T(8,128)(2,1)}, u32[]{:S(2)}, u32[]{:S(2)}) collective-permute-start(bf16[2,192,1152]{2,1,0:T(8,128)(2,1)} %get-tuple-element.108), channel_id=1, source_target_pairs={{0,8},{2,10},{4,12},{6,14},{8,0},{10,2},{12,4},{14,6},{16,24},{18,... | collective-permute-start | bytes 2654216 | tf_op jit(solution)/shard_map/ppermute | solution.py:70
  340.1 23.5 %collective-permute-start.33 = (f32[256,1152]{1,0:T(8,128)}, f32[256,1152]{1,0:T(8,128)}, u32[]{:S(2)}, u32[]{:S(2)}) collective-permute-start(f32[256,1152]{1,0:T(8,128)} %slice.438), channel_id=1, source_target_pairs={{0,2},{2,0},{4,6},{6,4},{8,10},{10,8},{12,14},{14,12},{16,18},{18,... | collective-permute-start | bytes 3538952 | tf_op jit(solution)/shard_map/ppermute | solution.py:70
  345.9 47.3 %collective-permute-start.59 = (bf16[2,192,1152]{2,1,0:T(8,128)(2,1)}, bf16[2,192,1152]{2,1,0:T(8,128)(2,1)S(1)}, u32[]{:S(2)}, u32[]{:S(2)}) collective-permute-start(bf16[2,192,1152]{2,1,0:T(8,128)(2,1)} %get-tuple-element.110), channel_id=1, source_target_pairs={{0,1},{1,0},{2,3},{3,2},{4,5},{5,4},{6,7},{7,6},{8,9},{9,8},{10,11... | collective-permute-start | bytes 2654216 | tf_op jit(solution)/shard_map/ppermute | solution.py:69
  361.2 74.5 %collective-permute-start.45 = (bf16[1,384,1152]{2,1,0:T(8,128)(2,1)S(1)}, bf16[1,384,1152]{2,1,0:T(8,128)(2,1)S(1)}, u32[]{:S(2)}, u32[]{:S(2)}) collective-permute-start(bf16[1,384,1152]{2,1,0:T(8,128)(2,1)S(1)} %get-tuple-element.68), channel_id=1, source_target_pairs={{0,8},{2,10},{4,12},{6,14},{8,0},{10,2},{12,4},{14,6},{16,24},{18,... | collective-permute-start | bytes 2654216 | tf_op jit(solution)/shard_map/ppermute | solution.py:70
  361.9 75.5 %collective-permute-start.48 = (bf16[1,384,1152]{2,1,0:T(8,128)(2,1)S(1)}, bf16[1,384,1152]{2,1,0:T(8,128)(2,1)S(1)}, u32[]{:S(2)}, u32[]{:S(2)}) collective-permute-start(bf16[1,384,1152]{2,1,0:T(8,128)(2,1)S(1)} %get-tuple-element.70), channel_id=1, source_target_pairs={{0,1},{1,0},{2,3},{3,2},{4,5},{5,4},{6,7},{7,6},{8,9},{9,8},{10,11... | collective-permute-start | bytes 2654216 | tf_op jit(solution)/shard_map/ppermute | solution.py:69
  363.6 76.3 %collective-permute-start.51 = (bf16[1,384,1152]{2,1,0:T(8,128)(2,1)S(1)}, bf16[1,384,1152]{2,1,0:T(8,128)(2,1)S(1)}, u32[]{:S(2)}, u32[]{:S(2)}) collective-permute-start(bf16[1,384,1152]{2,1,0:T(8,128)(2,1)S(1)} %get-tuple-element.72), channel_id=1, source_target_pairs={{0,4},{2,6},{4,0},{6,2},{8,12},{10,14},{12,8},{14,10},{16,20},{18,... | collective-permute-start | bytes 2654216 | tf_op jit(solution)/shard_map/ppermute | solution.py:70
  375.5 14.0 %collective-permute-start.34 = (bf16[16,3456]{1,0:T(8,128)(2,1)S(1)}, bf16[16,3456]{1,0:T(8,128)(2,1)S(1)}, u32[]{:S(2)}, u32[]{:S(2)}) collective-permute-start(bf16[16,3456]{1,0:T(8,128)(2,1)S(1)} %broadcast_select_fusion.4), channel_id=1, source_target_pairs={{0,1},{1,0},{2,3},{3,2},{4,5},{5,4},{6,7},{7,6},{8,9},{9,8},{10,11... | collective-permute-start | bytes 331784 | tf_op jit(solution)/shard_map/ppermute | solution.py:69
  389.4 13.4 %collective-permute-start.56 = (bf16[2,96,1152]{2,1,0:T(8,128)(2,1)S(1)}, bf16[2,96,1152]{2,1,0:T(8,128)(2,1)S(1)}, u32[]{:S(2)}, u32[]{:S(2)}) collective-permute-start(bf16[2,96,1152]{2,1,0:T(8,128)(2,1)S(1)} %add_convert_fusion.15), channel_id=1, source_target_pairs={{0,1},{1,0},{2,3},{3,2},{4,5},{5,4},{6,7},{7,6},{8,9},{9,8},{10,11... | collective-permute-start | bytes 1327112 | tf_op jit(solution)/shard_map/ppermute | solution.py:69
  393.2 8.4 %collective-permute-start.35 = (bf16[8,1152]{1,0:T(8,128)(2,1)S(1)}, bf16[8,1152]{1,0:T(8,128)(2,1)S(1)}, u32[]{:S(2)}, u32[]{:S(2)}) collective-permute-start(bf16[8,1152]{1,0:T(8,128)(2,1)S(1)} %select_convert_fusion), channel_id=1, source_target_pairs={{0,1},{1,0},{2,3},{3,2},{4,5},{5,4},{6,7},{7,6},{8,9},{9,8},{10,11... | collective-permute-start | bytes 55304 | tf_op jit(solution)/shard_map/ppermute | solution.py:69
  401.6 10.9 %collective-permute-start.58 = (bf16[2,96,1152]{2,1,0:T(8,128)(2,1)S(1)}, bf16[2,96,1152]{2,1,0:T(8,128)(2,1)S(1)}, u32[]{:S(2)}, u32[]{:S(2)}) collective-permute-start(bf16[2,96,1152]{2,1,0:T(8,128)(2,1)S(1)} %add_convert_fusion.12), channel_id=1, source_target_pairs={{0,4},{2,6},{4,0},{6,2},{8,12},{10,14},{12,8},{14,10},{16,20},{18,... | collective-permute-start | bytes 1327112 | tf_op jit(solution)/shard_map/ppermute | solution.py:70
  402.9 11.4 %collective-permute-start.60 = (bf16[2,96,1152]{2,1,0:T(8,128)(2,1)S(1)}, bf16[2,96,1152]{2,1,0:T(8,128)(2,1)S(1)}, u32[]{:S(2)}, u32[]{:S(2)}) collective-permute-start(bf16[2,96,1152]{2,1,0:T(8,128)(2,1)S(1)} %add_convert_fusion.9), channel_id=1, source_target_pairs={{0,8},{2,10},{4,12},{6,14},{8,0},{10,2},{12,4},{14,6},{16,24},{18,... | collective-permute-start | bytes 1327112 | tf_op jit(solution)/shard_map/ppermute | solution.py:70
  412.5 4.7 collective-permute-start.40
  414.7 39.4 %collective-permute-start.61 = (bf16[2,144,1152]{2,1,0:T(8,128)(2,1)S(1)}, bf16[2,144,1152]{2,1,0:T(8,128)(2,1)S(1)}, u32[]{:S(2)}, u32[]{:S(2)}) collective-permute-start(bf16[2,144,1152]{2,1,0:T(8,128)(2,1)S(1)} %slice.484), channel_id=1, source_target_pairs={{0,16},{2,18},{4,20},{6,22},{8,24},{10,26},{12,28},{14,30},{16,0},... | collective-permute-start | bytes 1990664 | tf_op jit(solution)/shard_map/ppermute | solution.py:70
  417.3 17.9 %collective-permute-start.41 = (bf16[32,3456]{1,0:T(8,128)(2,1)S(1)}, bf16[32,3456]{1,0:T(8,128)(2,1)S(1)}, u32[]{:S(2)}, u32[]{:S(2)}) collective-permute-start(bf16[32,3456]{1,0:T(8,128)(2,1)S(1)} %pad_maximum_fusion.21), channel_id=1, source_target_pairs={{0,8},{2,10},{4,12},{6,14},{8,0},{10,2},{12,4},{14,6},{16,24},{18,... | collective-permute-start | bytes 663560 | tf_op jit(solution)/shard_map/ppermute | solution.py:70
  435.2 28.7 %collective-permute-start.42 = (bf16[64,3456]{1,0:T(8,128)(2,1)S(1)}, bf16[64,3456]{1,0:T(8,128)(2,1)S(1)}, u32[]{:S(2)}, u32[]{:S(2)}) collective-permute-start(bf16[64,3456]{1,0:T(8,128)(2,1)S(1)} %pad_maximum_fusion.19), channel_id=1, source_target_pairs={{0,16},{2,18},{4,20},{6,22},{8,24},{10,26},{12,28},{14,30},{16,0},... | collective-permute-start | bytes 1327112 | tf_op jit(solution)/shard_map/ppermute | solution.py:70
  435.9 19.5 %collective-permute-start.46 = (bf16[1,192,1152]{2,1,0:T(8,128)(2,1)S(1)}, bf16[1,192,1152]{2,1,0:T(8,128)(2,1)S(1)}, u32[]{:S(2)}, u32[]{:S(2)}) collective-permute-start(bf16[1,192,1152]{2,1,0:T(8,128)(2,1)S(1)} %get-tuple-element.114), channel_id=1, source_target_pairs={{0,4},{2,6},{4,0},{6,2},{8,12},{10,14},{12,8},{14,10},{16,20},{18,... | collective-permute-start | bytes 1327112 | tf_op jit(solution)/shard_map/ppermute | solution.py:70
  437.7 25.9 %collective-permute-start.49 = (bf16[1,192,1152]{2,1,0:T(8,128)(2,1)S(1)}, bf16[1,192,1152]{2,1,0:T(8,128)(2,1)S(1)}, u32[]{:S(2)}, u32[]{:S(2)}) collective-permute-start(bf16[1,192,1152]{2,1,0:T(8,128)(2,1)S(1)} %get-tuple-element.116), channel_id=1, source_target_pairs={{0,8},{2,10},{4,12},{6,14},{8,0},{10,2},{12,4},{14,6},{16,24},{18,... | collective-permute-start | bytes 1327112 | tf_op jit(solution)/shard_map/ppermute | solution.py:70
  440.1 23.6 %collective-permute-start.52 = (bf16[1,192,1152]{2,1,0:T(8,128)(2,1)S(1)}, bf16[1,192,1152]{2,1,0:T(8,128)(2,1)S(1)}, u32[]{:S(2)}, u32[]{:S(2)}) collective-permute-start(bf16[1,192,1152]{2,1,0:T(8,128)(2,1)S(1)} %get-tuple-element.118), channel_id=1, source_target_pairs={{0,1},{1,0},{2,3},{3,2},{4,5},{5,4},{6,7},{7,6},{8,9},{9,8},{10,11... | collective-permute-start | bytes 1327112 | tf_op jit(solution)/shard_map/ppermute | solution.py:69
  455.4 8.6 %collective-permute-start.47 = (bf16[1,96,1152]{2,1,0:T(8,128)(2,1)S(1)}, bf16[1,96,1152]{2,1,0:T(8,128)(2,1)S(1)}, u32[]{:S(2)}, u32[]{:S(2)}) collective-permute-start(bf16[1,96,1152]{2,1,0:T(8,128)(2,1)S(1)} %add_convert_fusion.30), channel_id=1, source_target_pairs={{0,1},{1,0},{2,3},{3,2},{4,5},{5,4},{6,7},{7,6},{8,9},{9,8},{10,11... | collective-permute-start | bytes 663560 | tf_op jit(solution)/shard_map/ppermute | solution.py:69
  463.7 6.0 %collective-permute-start.50 = (bf16[1,96,1152]{2,1,0:T(8,128)(2,1)S(1)}, bf16[1,96,1152]{2,1,0:T(8,128)(2,1)S(1)}, u32[]{:S(2)}, u32[]{:S(2)}) collective-permute-start(bf16[1,96,1152]{2,1,0:T(8,128)(2,1)S(1)} %add_convert_fusion.27), channel_id=1, source_target_pairs={{0,4},{2,6},{4,0},{6,2},{8,12},{10,14},{12,8},{14,10},{16,20},{18,... | collective-permute-start | bytes 663560 | tf_op jit(solution)/shard_map/ppermute | solution.py:70
  463.8 6.0 %collective-permute-start.53 = (bf16[1,96,1152]{2,1,0:T(8,128)(2,1)S(1)}, bf16[1,96,1152]{2,1,0:T(8,128)(2,1)S(1)}, u32[]{:S(2)}, u32[]{:S(2)}) collective-permute-start(bf16[1,96,1152]{2,1,0:T(8,128)(2,1)S(1)} %add_convert_fusion.24), channel_id=1, source_target_pairs={{0,8},{2,10},{4,12},{6,14},{8,0},{10,2},{12,4},{14,6},{16,24},{18,... | collective-permute-start | bytes 663560 | tf_op jit(solution)/shard_map/ppermute | solution.py:70
  464.0 24.4 %collective-permute-start.43 = (bf16[128,3456]{1,0:T(8,128)(2,1)S(1)}, bf16[128,3456]{1,0:T(8,128)(2,1)S(1)}, u32[]{:S(2)}, u32[]{:S(2)}) collective-permute-start(bf16[128,3456]{1,0:T(8,128)(2,1)S(1)} %pad_maximum_fusion.11), channel_id=1, source_target_pairs={{0,2},{2,0},{4,6},{6,4},{8,10},{10,8},{12,14},{14,12},{16,18},{18,... | collective-permute-start | bytes 2654216 | tf_op jit(solution)/shard_map/ppermute | solution.py:70
  470.0 17.5 %collective-permute-start.54 = (bf16[1,144,1152]{2,1,0:T(8,128)(2,1)S(1)}, bf16[1,144,1152]{2,1,0:T(8,128)(2,1)S(1)}, u32[]{:S(2)}, u32[]{:S(2)}) collective-permute-start(bf16[1,144,1152]{2,1,0:T(8,128)(2,1)S(1)} %slice.464), channel_id=1, source_target_pairs={{0,16},{2,18},{4,20},{6,22},{8,24},{10,26},{12,28},{14,30},{16,0},... | collective-permute-start | bytes 995336 | tf_op jit(solution)/shard_map/ppermute | solution.py:70
  (95 other events, 806.7 us)

commit v4 on v3

--- a/solution.py
+++ b/solution.py
@@ -175,6 +175,7 @@
 
 any_spec = pl.BlockSpec(memory_space=pl.ANY)
 vmem_spec = pl.BlockSpec(memory_space=pltpu.VMEM)
+tiny = pl.CostEstimate(flops=1024, bytes_accessed=1024, transcendentals=0)
 
 
 def run_copies(copies):
@@ -221,15 +222,14 @@
     )(index, *pieces)
 
 
-def split_kernel(rows, each, index_ref, first_ref, second_ref, *refs):
-    outs, hold, sems, ins = refs[:-3], *refs[-3:]
-    top = first_ref.shape[0]
-    run_copies(
-        [
-            pltpu.make_async_copy(first_ref, hold.at[pl.ds(0, top)], ins.at[0]),
-            pltpu.make_async_copy(second_ref, hold.at[pl.ds(top, second_ref.shape[0])], ins.at[1]),
-        ]
-    )
+def weight_grad_kernel(rows, each, index_ref, grad_ref, x_ref, mine_ref, other_ref, *refs):
+    outs, hold, sems = refs[:-2], *refs[-2:]
+    top = grad_ref.shape[0]
+    step = top // 3
+    for n in range(3):
+        here = slice(n * step, (n + 1) * step)
+        hold[here] = dot(grad_ref[here], x_ref[...], 1, 0).astype(bf16)
+    hold[top:] = summed(mine_ref[...], other_ref[...])
     copies = []
     for n, out in enumerate(outs):
         for j in range(each):
@@ -242,26 +242,135 @@
     run_copies(copies)
 
 
-def split_pieces(first, second, index, rows, count):
-    total, width = first.shape[0] + second.shape[0], first.shape[1]
+def weight_grad(grad, x, mine, other, index, rows, count):
+    total, width = grad.shape[0] + mine.shape[0], x.shape[1]
     each = total // rows // count
     return pl.pallas_call(
-        functools.partial(split_kernel, rows, each),
+        functools.partial(weight_grad_kernel, rows, each),
         grid_spec=pltpu.PrefetchScalarGridSpec(
             num_scalar_prefetch=1,
             grid=(1,),
-            in_specs=[any_spec] * 2,
+            in_specs=[vmem_spec] * 4,
             out_specs=[any_spec] * count,
-            scratch_shapes=[
-                pltpu.VMEM((total, width), bf16),
-                pltpu.SemaphoreType.DMA((each * count,)),
-                pltpu.SemaphoreType.DMA((2,)),
-            ],
+            scratch_shapes=[pltpu.VMEM((total, width), bf16), pltpu.SemaphoreType.DMA((each * count,))],
         ),
         out_shape=[jax.ShapeDtypeStruct((1, each * rows, width), bf16)] * count,
-        compiler_params=pltpu.CompilerParams(vmem_limit_bytes=10 * MIB),
-        name="split_pieces",
-    )(index, first, second)
+        cost_estimate=tiny,
+        compiler_params=pltpu.CompilerParams(vmem_limit_bytes=32 * MIB),
+        name="weight_grad",
+    )(index, grad, x, mine, other)
+
+
+def by_core(core_ref, group, whole):
+    if group is None:
+        return [whole]
+    picked = []
+    for c in range(2):
+        rows = []
+        for at in range(0, whole.shape[0], 2 * group):
+            first, second = whole[at : at + group], whole[at + group : at + 2 * group]
+            rows.append(jnp.where(core_ref[0] == c, first, second))
+        picked.append(jnp.concatenate(rows, axis=0))
+    return picked
+
+
+def middle_kernel(group, core_ref, *refs):
+    back_a, back_b, normed_ref, inverse_ref, grad_out, attn_out, pick, scale, gate, weight, context = refs[:11]
+    mid_ref, attn_ref, column_ref = refs[11:14]
+    normed = normed_ref[...]
+    back = (back_a[...] + back_b[...]) * (1.0 + dot(pick[...], scale[...], 1, 0))
+    grad_mid = grad_out[...].astype(f32) + norm_back(back, normed, inverse_ref[...])
+    mid_ref[...] = grad_mid
+    grad_attn = (dot(pick[...], gate[...], 1, 0) * grad_mid).astype(bf16)
+    attn_ref[...] = grad_attn
+    column_ref[...] = jnp.sum(grad_attn.astype(f32), axis=0, keepdims=True)
+    parts = by_core(core_ref, group, dot(weight[...], grad_attn, 0, 1))
+    parts += by_core(core_ref, group, dot(grad_attn, context[...], 0, 1))
+    for ref, value in zip(refs[14:], parts):
+        ref[...] = value.astype(bf16)
+
+
+def middle(core, group, *args):
+    tokens, width = args[0].shape
+    if group is None:
+        sizes = [(width, tokens), (width, width)]
+    else:
+        sizes = [(width // 2, tokens)] * 2 + [(width // 2, width)] * 2
+    return pl.pallas_call(
+        functools.partial(middle_kernel, group),
+        in_specs=[pl.BlockSpec(memory_space=pltpu.SMEM)] + [vmem_spec] * len(args),
+        out_specs=[vmem_spec] * (3 + len(sizes)),
+        out_shape=[
+            jax.ShapeDtypeStruct((tokens, width), f32),
+            jax.ShapeDtypeStruct((tokens, width), bf16),
+            jax.ShapeDtypeStruct((1, width), f32),
+        ]
+        + [jax.ShapeDtypeStruct(size, bf16) for size in sizes],
+        cost_estimate=tiny,
+        compiler_params=pltpu.CompilerParams(vmem_limit_bytes=40 * MIB),
+        name="middle",
+    )(core.reshape(1), *args)
+
+
+def slot_sums(pick, blocks, out_ref):
+    for n, block in enumerate(blocks):
+        high = block.astype(bf16)
+        low = (block - high.astype(f32)).astype(bf16)
+        total = dot(pick, high, 0, 0) + dot(pick, low, 0, 0)
+        out_ref[:, n * block.shape[1] : (n + 1) * block.shape[1]] = total.astype(bf16)
+
+
+def mlp_end_kernel(*refs):
+    back_a, back_b, out_a, out_b, bias, normed, grad_out, mid, pick, gate = refs[:10]
+    result_ref, pair_ref = refs[10:]
+    mlp_out = out_a[...] + out_b[...] + bias[...]
+    result_ref[...] = (mid[...] + dot(pick[...], gate[...], 1, 0) * mlp_out).astype(bf16)
+    back = back_a[...] + back_b[...]
+    slot_sums(pick[...], (back, back * normed[...], grad_out[...].astype(f32) * mlp_out), pair_ref)
+
+
+def attn_end_kernel(*refs):
+    back_a, back_b, normed_ref, inverse_ref, grad_mid, attn_out, pick, scale = refs[:8]
+    tokens_ref, pair_ref = refs[8:]
+    back, normed = back_a[...] + back_b[...], normed_ref[...]
+    slope = back * (1.0 + dot(pick[...], scale[...], 1, 0))
+    tokens_ref[...] = grad_mid[...] + norm_back(slope, normed, inverse_ref[...])
+    slot_sums(pick[...], (back, back * normed, grad_mid[...] * attn_out[...]), pair_ref)
+
+
+def end_call(kernel, dtype, slots, *args):
+    tokens, width = args[0].shape
+    return pl.pallas_call(
+        kernel,
+        in_specs=[vmem_spec] * len(args),
+        out_specs=[vmem_spec] * 2,
+        out_shape=[
+            jax.ShapeDtypeStruct((tokens, width), dtype),
+            jax.ShapeDtypeStruct((slots, 3 * width), bf16),
+        ],
+        cost_estimate=tiny,
+        compiler_params=pltpu.CompilerParams(vmem_limit_bytes=32 * MIB),
+        name=kernel.__name__,
+    )(*args)
+
+
+def rows_kernel(*refs):
+    at = 0
+    for ref in refs[:-1]:
+        refs[-1][at : at + ref.shape[0]] = ref[...]
+        at += ref.shape[0]
+
+
+def stack_rows(*args):
+    count = sum(a.shape[0] for a in args)
+    return pl.pallas_call(
+        rows_kernel,
+        in_specs=[vmem_spec] * len(args),
+        out_specs=vmem_spec,
+        out_shape=jax.ShapeDtypeStruct((count, args[0].shape[1]), f32),
+        cost_estimate=tiny,
+        name="stack_rows",
+    )(*args)
 
 
 def softmax_t(key, query, same, scale):
@@ -310,7 +419,6 @@
     _, groups, rows, tokens = qkv.shape
     scale = dim**-0.5
     ids_t = ids.T
-    flops = groups * rows * tokens * ids.shape[1] * 2
 
     def one(n):
         return pl.BlockSpec((1, 1, rows, tokens), lambda i: (n, i, 0, 0))
@@ -325,7 +433,7 @@
             in_specs=specs,
             out_specs=flat,
             out_shape=jax.ShapeDtypeStruct((groups, rows, tokens), bf16),
-            cost_estimate=pl.CostEstimate(flops=2 * flops, bytes_accessed=qkv.size * 3, transcendentals=0),
+            cost_estimate=tiny,
             compiler_params=pltpu.CompilerParams(vmem_limit_bytes=24 * MIB),
             name="attention",
         )(*args)
@@ -335,13 +443,13 @@
         in_specs=specs + [flat],
         out_specs=pl.BlockSpec((3, 1, rows, tokens), lambda i: (0, i, 0, 0)),
         out_shape=jax.ShapeDtypeStruct(qkv.shape, bf16),
-        cost_estimate=pl.CostEstimate(flops=5 * flops, bytes_accessed=qkv.size * 5, transcendentals=0),
+        cost_estimate=tiny,
         compiler_params=pltpu.CompilerParams(vmem_limit_bytes=24 * MIB),
         name="attention_back",
     )(*args, grad)
 
 
-def mlp_kernel(first, x_ref, g_ref, b_ref, *refs):
+def mlp_kernel(number, first, x_ref, g_ref, b_ref, *refs):
     if first:
         pieces, sums, before = refs[:2], refs[-4:], [None] * 4
     else:
@@ -353,7 +461,7 @@
     root = 0.7978845608028654
     for n, piece in enumerate(pieces):
         w_in, w_out = piece[0], piece[1]
-        hidden = dot(x, w_in, 1, 1) + b_ref[n : n + 1]
+        hidden = dot(x, w_in, 1, 1) + b_ref[2 * number + n : 2 * number + n + 1]
         square = hidden * hidden
         tanh = jnp.tanh(root * hidden * (1.0 + 0.044715 * square))
         act = (0.5 * hidden * (1.0 + tanh)).astype(bf16)
@@ -371,20 +479,18 @@
         ref[...] = value if prior is None else value + prior[...]
 
 
-def mlp_part(x, g, bias, own, other, before):
+def mlp_part(number, x, g, bias, own, other, before):
     tokens, width = x.shape
     units = own.shape[1]
     sums = [jax.ShapeDtypeStruct((tokens // 2, width), f32)] * 4
     outs = [jax.ShapeDtypeStruct(own.shape, bf16)] * 2 + [jax.ShapeDtypeStruct((2, units), f32)] + sums
     args = [x, g, bias, own, other, *before]
     return pl.pallas_call(
-        functools.partial(mlp_kernel, not before),
+        functools.partial(mlp_kernel, number, not before),
         in_specs=[vmem_spec] * len(args),
         out_specs=[vmem_spec] * len(outs),
         out_shape=outs,
-        cost_estimate=pl.CostEstimate(
-            flops=24 * tokens * width * units, bytes_accessed=units * width * 32, transcendentals=0
-        ),
+        cost_estimate=tiny,
         compiler_params=pltpu.CompilerParams(vmem_limit_bytes=48 * MIB),
         name="mlp_part",
     )(*args)
@@ -420,14 +526,15 @@
     for n in range(g_attn.count):
         g_attn.start().finish()
     g_attn.start()
+    first = g_attn.value
     for n in range(g_fc.count):
-        g_fc.start(*g_attn.value).finish()
+        g_fc.start(*first).finish()
     g_attn.finish().start()
     g_attn.finish().start()
     g_fc.start(*g_attn.got)
     attn_pieces = [(g_attn.value, g_attn.got)[side][n] for n, side in halves]
 
-    silu_cond = jax.nn.silu(cond.astype(f32)).astype(bf16)
+    silu_cond = jax.nn.silu(after(cond, *first).astype(f32)).astype(bf16)
     mod_part = times(silu_cond, ada_weight) + ada_bias.reshape(-1).astype(f32)
     mod_own = mod_part.astype(bf16)
     mod_other = net.swap(mod_own, "mod")
@@ -440,26 +547,28 @@
     token_slot = jnp.sum(jnp.where(crop_onehot, slots[None, :], 0), axis=1)
     slot_pick = token_slot[:, None] == jnp.arange(cond.shape[0], dtype=jnp.int32)[None, :]
     slot_pick = slot_pick.astype(bf16)
-    token_mod = times(slot_pick, modulation)
-    shift_a, scale_a, gate_a, shift_m, scale_m, gate_m = jnp.split(token_mod, 6, axis=1)
-
-    bias_all = lax.all_to_all(
-        jnp.broadcast_to(biases[None], (device_count, biases.shape[0])),
-        ("dp", "mod"),
-        split_axis=0,
-        concat_axis=0,
-        tiled=True,
-    ).reshape(-1)
-    bias_query, bias_value, bias_proj, bias_out = [
-        bias_all[n * width : (n + 1) * width].astype(f32) for n in range(4)
-    ]
-    bias_in = bias_all[4 * width :].reshape(device_count, shard)
-    bias_pieces, picks = [], []
+    mods = [modulation[:, n * width : (n + 1) * width] for n in range(6)]
+    shift_a, scale_a, gate_a, shift_m, scale_m, gate_m = [times(slot_pick, block) for block in mods]
+
+    slot_count, own_cols = cond.shape[0], width // net.dp
+    to_dp = jnp.moveaxis(silu_cond.reshape(slot_count, net.dp, own_cols), 1, 0).reshape(net.dp, 1, -1)
+    to_all = jnp.broadcast_to(to_dp, (net.dp, net.mod, slot_count * own_cols)).reshape(device_count, -1)
+    sent = jnp.concatenate([jnp.broadcast_to(biases[None], (device_count, biases.shape[0])), to_all], axis=1)
+    met = lax.all_to_all(sent, ("dp", "mod"), split_axis=0, concat_axis=0, tiled=True)
+    ada_order = list(range(1, net.bits)) + [0]
+    dp_order = net.ranks(ada_order, range(net.dp))[0]
+    dp_pick = (dp_order[:, None] == jnp.arange(net.dp)[None, :]).astype(bf16)
+    cond_cols = times(dp_pick, met.reshape(net.dp, net.mod, -1)[:, 0, biases.shape[0] :]).astype(bf16)
+    cond_cols = cond_cols.reshape(-1, own_cols)
+    bias_all = met[:, : biases.shape[0]].reshape(-1, width)
+    bias_query, bias_value, bias_proj, bias_out = [bias_all[n].astype(f32) for n in range(4)]
+    bias_in = bias_all[4:].reshape(device_count, 3, third)
+    picks = []
     for n, side in halves:
         devices = net.devices(net.orders[n], chunks_of[side])
-        pick = (devices[:, None] == jnp.arange(device_count)[None, :]).astype(bf16)
-        picks.append(pick)
-        bias_pieces.append(times(pick, bias_in[:, n * third : (n + 1) * third]).reshape(1, -1))
+        picks.append((devices[:, None] == jnp.arange(device_count)[None, :]).astype(bf16))
+    picks = jnp.stack(picks).reshape(3, 2, chips // 2, device_count)
+    bias_pieces = jnp.einsum("nsjd,dnr->nsjr", picks, bias_in, preferred_element_type=f32).reshape(6, -1)
 
     def join(own, other):
         own, other = [a.reshape(-1, 1, net.mod * shard, a.shape[-1]) for a in (own, other)]
@@ -491,8 +600,6 @@
         qkv = (times_rows(qkv_weight, attn_both) + qkv_bias).astype(bf16)
         qkv = qkv.reshape(3, -1, 2 * head_dim, 2 * tok_len)
         context_both = attention(qkv, ids, head_dim).reshape(-1, 2 * tok_len)
-        context_both = after(context_both, *g_fc.got)
-        g_fc.finish().start()
         context = join(context_both[:, :tok_len], net.swap(context_both[:, tok_len:], 0))
         attn_out = dot(context, proj_weight, 0, 1) + bias_proj
     else:
@@ -518,67 +625,60 @@
     mid = resid + gate_a * attn_out
     normed_m, inverse_m = layer_norm(mid)
     mlp_in = (normed_m * (1.0 + scale_m) + shift_m).astype(bf16)
-    grad_out = out_grad[0].astype(f32)
-    grad_mlp = (gate_m * grad_out).astype(bf16)
+    if aligned:
+        mlp_in = after(mlp_in, *g_fc.got)
+        g_fc.finish().start()
+    grad_mlp = (gate_m * out_grad[0].astype(f32)).astype(bf16)
 
     mlp_both = jnp.concatenate([mlp_in, net.swap(mlp_in, 0)], axis=0)
     grad_both = jnp.concatenate([grad_mlp, net.swap(grad_mlp, 0)], axis=0)
+    grad_bias_out = jnp.sum(grad_mlp.astype(f32), axis=0, keepdims=True)
     s_fc = Scatter(net)
     sums, columns = [], []
     for n in range(3):
-        bias = jnp.concatenate(bias_pieces[2 * n : 2 * n + 2], axis=0)
-        own, other, column, *sums = mlp_part(mlp_both, grad_both, bias, g_fc.value[n], g_fc.got[n], sums)
+        own, other, column, *sums = mlp_part(
+            n, mlp_both, grad_both, bias_pieces, g_fc.value[n], g_fc.got[n], sums
+        )
         s_fc.begin(n, own, other)
-        columns.extend([column[0], column[1]])
+        columns.append(column)
     out_own, out_other, back_own, back_other = sums
-    mlp_out = out_own + net.swap(out_other, 0) + bias_out
-    grad_mlp_in = back_own + net.swap(back_other, 0)
-    grad_bias_in = []
-    for n in range(3):
-        placed = 0.0
-        for side in range(2):
-            column = columns[2 * n + side].reshape(chips // 2, third)
-            placed = placed + jnp.dot(
-                picks[2 * n + side].astype(f32).T, column, precision=lax.Precision.HIGHEST
-            )
-        grad_bias_in.append(placed)
-    grad_bias_in = jnp.concatenate(grad_bias_in, axis=1)
-
-    ada_order = list(range(1, net.bits)) + [0]
-
-    def all_rows(value):
-        for dim in ada_order:
-            value = jnp.concatenate([value, net.swap(value, dim)], axis=0)
-        return value
-
-    cond_rows = all_rows(after(silu_cond, mlp_both))
-
-    result = (mid + gate_m * mlp_out).astype(bf16)
-    grad_gate_m = grad_out * mlp_out
-    grad_scale_m = grad_mlp_in * normed_m
-    grad_mid = grad_out + norm_back(grad_mlp_in * (1.0 + scale_m), normed_m, inverse_m)
-    grad_gate_a = grad_mid * attn_out
-    grad_attn = (gate_a * grad_mid).astype(bf16)
-    grad_proj = dot(grad_attn, context, 0, 1).astype(bf16)
-    grad_context = dot(proj_weight, grad_attn, 0, 1).astype(bf16)
+    mlp_back_met = net.swap(back_other, 0)
+    out_met = net.swap(after(out_other, mlp_back_met), 0)
+
+    grad_mid, grad_attn, grad_bias_proj, *parts = middle(
+        core,
+        net.mod * shard if aligned else None,
+        back_own,
+        mlp_back_met,
+        normed_m,
+        inverse_m,
+        out_grad[0],
+        attn_out,
+        slot_pick,
+        mods[4],
+        mods[2],
+        proj_weight,
+        context,
+    )
     s_attn = Scatter(net)
     if aligned:
-        proj_mine, proj_other = part(grad_proj)
-        proj_mine = summed(proj_mine, net.swap(proj_other, 0))
-        mine, other = part(grad_context)
+        mine, other, proj_mine, proj_other = parts
         context_grads = jnp.concatenate([mine, net.swap(other, 0)], axis=1)
+        proj_met = net.swap(after(proj_other, context_grads), 0)
         grad_qkv = attention(qkv, ids, head_dim, context_grads.reshape(-1, 2 * head_dim, 2 * tok_len))
         grad_qkv = grad_qkv.reshape(-1, 2 * tok_len)
-        grad_qkv = after(grad_qkv, *s_fc.arrived())
-        s_fc.advance()
-        grad_qkv_w = times(grad_qkv, attn_both).astype(bf16)
-        pieces = split_pieces(grad_qkv_w, proj_mine, index, third, 6)
+        grad_qkv = after(grad_qkv, *s_fc.arrived()[:2])
+        s_fc.advance((0, 1))
+        pieces = weight_grad(grad_qkv, attn_both, proj_mine, proj_met, index, third, 6)
+        pieces = lax.optimization_barrier((*pieces, *s_fc.arrived()[2:]))[:6]
+        s_fc.advance((2,))
         back_both = contract_rows(grad_qkv, qkv_weight)
-        grad_attn_in = back_both[:tok_len] + net.swap(back_both[tok_len:], 0)
+        back_own, back_met = back_both[:tok_len], net.swap(back_both[tok_len:], 0)
         column = jnp.sum(grad_qkv.astype(f32), axis=1, keepdims=True).reshape(3, -1, 1)
         none = jnp.zeros_like(column[0])
         grad_bias_query, grad_bias_value = join(column[0], none)[:, 0], join(column[2], none)[:, 0]
     else:
+        grad_context, grad_proj = parts
         grad_qkv = attention(
             qkv, seg_ids[None], head_dim, grad_context.reshape(-1, 2 * head_dim, tok_len)
         ).reshape(-1, tok_len)
@@ -592,37 +692,56 @@
         grads = lax.fori_loop(0, places.shape[0], take, jnp.zeros_like(attn_grad))
         grads = jnp.split(grads[None], 12, axis=1)
         pieces = [summed(a, net.swap(b, 0)) for a, b in zip(grads[:6], grads[6:])]
-        grad_attn_in = contract_rows(grad_qkv, qkv_weight)
+        back_own = contract_rows(grad_qkv, qkv_weight)
+        back_met = jnp.zeros_like(back_own)
         column = jnp.sum(grad_qkv.astype(f32), axis=1).reshape(3, -1)
         grad_bias_query, grad_bias_value = column[0], column[2]
     for n in range(3):
         s_attn.begin(n, pieces[2 * n], pieces[2 * n + 1])
-    grad_scale_a = grad_attn_in * normed_a
-    grad_tokens = grad_mid + norm_back(grad_attn_in * (1.0 + scale_a), normed_a, inverse_a)
-    grad_bias = jnp.concatenate(
-        [
-            grad_bias_query,
-            grad_bias_value,
-            jnp.sum(grad_attn.astype(f32), axis=0),
-            jnp.sum(grad_mlp.astype(f32), axis=0),
-            grad_bias_in.reshape(-1),
-        ]
+    result, pair_m = end_call(
+        mlp_end_kernel,
+        bf16,
+        slot_count,
+        sums[2],
+        mlp_back_met,
+        out_own,
+        out_met,
+        bias_out[None],
+        normed_m,
+        out_grad[0],
+        mid,
+        slot_pick,
+        mods[5],
+    )
+    grad_tokens, pair_a = end_call(
+        attn_end_kernel,
+        f32,
+        slot_count,
+        back_own,
+        back_met,
+        normed_a,
+        inverse_a,
+        grad_mid,
+        attn_out,
+        slot_pick,
+        mods[1],
+    )
+    columns = jnp.concatenate(columns, axis=0).reshape(3, 2, chips // 2, third)
+    grad_bias_in = jnp.einsum("nsjd,nsjr->dnr", picks.astype(f32), columns, precision=lax.Precision.HIGHEST)
+    grad_bias = stack_rows(
+        grad_bias_query[None],
+        grad_bias_value[None],
+        grad_bias_proj,
+        grad_bias_out,
+        grad_bias_in.reshape(-1, width),
     )
     bias_rows = lax.all_to_all(
         grad_bias.reshape(device_count, -1), ("dp", "mod"), split_axis=0, concat_axis=0, tiled=True
     )
     bias_sum = jnp.sum(bias_rows, axis=0)
 
-    grad_token_mod = jnp.concatenate(
-        [grad_attn_in, grad_scale_a, grad_gate_a, grad_mlp_in, grad_scale_m, grad_gate_m], axis=1
-    )
-    token_high = lax.reduce_precision(grad_token_mod, 8, 7)
-    token_low = (grad_token_mod - token_high).astype(bf16)
-    grad_pair = contract_rows(slot_pick, token_high.astype(bf16)) + contract_rows(slot_pick, token_low)
-    grad_pair = grad_pair.astype(bf16)
-    columns = grad_pair.shape[1] // 2
-    pair_own = jnp.where(mod_rank == 0, grad_pair[:, :columns], grad_pair[:, columns:])
-    pair_send = jnp.where(mod_rank == 0, grad_pair[:, columns:], grad_pair[:, :columns])
+    pair_own = jnp.where(mod_rank == 0, pair_a, pair_m)
+    pair_send = jnp.where(mod_rank == 0, pair_m, pair_a)
     grad_mod = summed(pair_own, net.swap(pair_send, "mod"))
     grad_silu = times_rows(grad_mod, ada_weight)
     silu_own = jnp.where(mod_rank == 0, grad_silu[:crop_count], grad_silu[crop_count:])
@@ -631,9 +750,9 @@
     own_cond = lax.dynamic_slice_in_dim(cond, mod_rank * crop_count, crop_count, 0).astype(f32)
     silu_back = jax.vjp(jax.nn.silu, own_cond)[1]
     grad_cond = silu_back(grad_silu)[0]
-    mod_rows = all_rows(grad_mod)
-    own_cols = width // net.dp
-    cond_cols = lax.dynamic_slice_in_dim(cond_rows, net.dp_rank * own_cols, own_cols, 1)
+    mod_rows = grad_mod
+    for dim in ada_order:
+        mod_rows = jnp.concatenate([mod_rows, net.swap(mod_rows, dim)], axis=0)
     ada_w_sum = contract_rows(cond_cols, mod_rows)
     ada_b_sum = jnp.sum(mod_rows.astype(f32), axis=0).reshape(ada_bias.shape[0], width)
     ada_b_sum = lax.dynamic_slice_in_dim(ada_b_sum, net.dp_rank * own_cols, own_cols, 1)

time: 502 us -> 469 us (0.934)
  waiting for transfers between devices: 215 us -> 162 us
  local copies, waits for them, and re-layouts: 55.9 us -> 74.4 us
  Pallas kernels: 66.7 us -> 84.6 us
  matrix products: 36.2 us -> 30.2 us
    ppermute x47 -> x43, waiting for transfers between devices: 180 us -> 115 us  [swap(): lax.ppermute(value, 'dp', [(i, i ^ 1 << dim) for i in range(self.dp)])]
    pallas_call x4 -> x8, Pallas kernels: 43.8 us -> 61.6 us  [the longest x3 34.8 us: mlp_part(): pl.pallas_call(functools.partial(mlp_kernel, number, not before), in_spec...]
    unnamed x209 -> x199, local copies, waits for them, and re-layouts: 28.3 us -> 41.7 us
    reduce_sum x4 -> x0, other arithmetic: 11.8 us -> none  [the longest x2 5.34 us: norm_back(): centered = grad_in - jnp.mean(grad_in, axis=-1, keepdims=True)]
    all_to_all x1, waiting for transfers between devices: 5.2 us -> 15.1 us  [on_device(): lax.all_to_all(sent, ('dp', 'mod'), split_axis=0, concat_axis=0, tiled=True)]
    dot_general x6 -> x2, matrix products: 8.37 us -> 1.7 us  [the longest x1 0.96 us: on_device(): jnp.einsum('nsjd,nsjr->dnr', picks.astype(f32), columns, precision=lax.Pr...]
    another operation x8 -> x2, local copies, waits for them, and re-layouts: 8.98 us -> 2.74 us  [the longest x1 1.37 us: on_device(): grad_bias_value[None]]
    reshape x8 -> x9, local copies, waits for them, and re-layouts: 2.02 us -> 7.8 us  [the longest x1 1.57 us: on_device(): met.reshape(net.dp, net.mod, -1)[:, 0, biases.shape[0]:]]
  transfers between devices with their start and end apart: 64 -> 60, of which waited for: 31 -> 21; matrix products, arithmetic and copies ran while one was open for 20% -> 24% of each run, Pallas kernels for 11% -> 16%
where the time goes in v4:
time: 469 us; the launch traced here: 464 us
  waiting for transfers between devices  162 us (35%)
  Pallas kernels  84.6 us (18%)
  local copies, waits for them, and re-layouts  74.4 us (16%)
  starting transfers between devices  65.3 us (14%)
  other arithmetic  44.4 us (9%)
  matrix products  30.2 us (6%)
    ppermute x43, waiting for transfers between devices, swap(): lax.ppermute(value, 'dp', [(i, i ^ 1 << dim) for i in range(self.dp)])  115 us
    unnamed x199, local copies, waits for them, and re-layouts  41.7 us
    ppermute x43, starting transfers between devices, swap(): lax.ppermute(value, 'dp', [(i, i ^ 1 << dim) for i in range(self.dp)])  40.9 us
    pallas_call x3, Pallas kernels, mlp_part(): pl.pallas_call(functools.partial(mlp_kernel, number, not before), in_spec...  34.8 us
    ppermute x15, waiting for transfers between devices, swap(): return lax.ppermute(value, 'mod', [(i, i ^ 1) for i in range(self.mod)])  32.2 us
    dot_general x13, matrix products, dot(): lax.dot_general(left, right, (((left_dim,), (right_dim,)), ((), ())), pre...  28.5 us
    ppermute x15, starting transfers between devices, swap(): return lax.ppermute(value, 'mod', [(i, i ^ 1) for i in range(self.mod)])  16.6 us
    convert_element_type x18, other arithmetic, summed(): return (left.astype(f32) + right.astype(f32)).astype(bf16)  15.8 us
  transfers between devices with their start and end apart: 60, of which 21 were waited for; matrix products, arithmetic and copies ran while one was open for 24% of the time, Pallas kernels for 16%

profile of v4, /device:TPU:0, one launch (start us, length us, event | category | flops | bytes accessed | tf_op | source)
XLA Modules:
  0.0 463.5 jit_solution(9442005328844633898)
XLA Ops:
  0.7 4.1 collective-permute-start
  9.9 2.4 fusion.16.refs_2_
  13.6 6.3 %collective-permute-done = bf16[1,144,1152]{2,1,0:T(8,128)(2,1)S(1)} collective-permute-done((bf16[1,144,1152]{2,1,0:T(8,128)(2,1)}, bf16[1,144,1152]{2,1,0:T(8,128)(2,1)S(1)}, u32[]{:S(2)}, u32[]{:S(2)}) %collective-permute-start) | collective-permute-done | bytes 331808 | tf_op jit(solution)/shard_map/ppermute | solution.py:70
  20.9 1.5 collective-permute-start.3
  22.4 1.5 collective-permute-start.6
  23.9 3.3 collective-permute-start.13
  27.2 4.4 fusion
  34.7 2.8 all-to-all-start
  40.9 1.8 convert_reduce_fusion.3
  42.7 15.1 %all-to-all-done = bf16[32,2,720]{2,1,0:T(2,128)(2,1)S(1)} async-done(((bf16[32,2,720]{2,1,0:T(2,128)(2,1)}), bf16[32,2,720]{2,1,0:T(2,128)(2,1)S(1)}, u32[]{:S(2)}, u32[]{:S(2)}) %all-to-all-start) | async-done | bytes 92192 | tf_op jit(solution)/shard_map/all_to_all | solution.py:557
  63.2 1.6 collective-permute-start.4
  64.9 8.6 %collective-permute-done.10 = bf16[1,192,1152]{2,1,0:T(8,128)(2,1)S(1)} collective-permute-done((bf16[1,192,1152]{2,1,0:T(8,128)(2,1)S(1)}, bf16[1,192,1152]{2,1,0:T(8,128)(2,1)S(1)}, u32[]{:S(2)}, u32[]{:S(2)}) %collective-permute-start.10) | collective-permute-done | bytes 442400 | tf_op jit(solution)/shard_map/ppermute | solution.py:69
  75.6 1.5 collective-permute-start.11
  78.1 7.1 %collective-permute-done.7 = bf16[1,192,1152]{2,1,0:T(8,128)(2,1)S(1)} collective-permute-done((bf16[1,192,1152]{2,1,0:T(8,128)(2,1)S(1)}, bf16[1,192,1152]{2,1,0:T(8,128)(2,1)S(1)}, u32[]{:S(2)}, u32[]{:S(2)}) %collective-permute-start.7) | collective-permute-done | bytes 442400 | tf_op jit(solution)/shard_map/ppermute | solution.py:70
  85.6 1.8 collective-permute-start.8
  89.9 6.7 %collective-permute-done.11.refs_5_ = bf16[1,384,1152]{2,1,0:T(8,128)(2,1)S(1)} collective-permute-done((bf16[1,384,1152]{2,1,0:T(8,128)(2,1)S(1)}, bf16[1,384,1152]{2,1,0:T(8,128)(2,1)S(1)}, u32[]{:S(2)}, u32[]{:S(2)}) %collective-permute-start.11) | collective-permute-done | bytes 884768 | tf_op jit(solution)/shard_map/ppermute | solution.py:70
  96.5 9.1 %collective-permute-done.5.refs_1_ = bf16[1,384,1152]{2,1,0:T(8,128)(2,1)S(1)} collective-permute-done((bf16[1,384,1152]{2,1,0:T(8,128)(2,1)S(1)}, bf16[1,384,1152]{2,1,0:T(8,128)(2,1)S(1)}, u32[]{:S(2)}, u32[]{:S(2)}) %collective-permute-start.5) | collective-permute-done | bytes 884768 | tf_op jit(solution)/shard_map/ppermute | solution.py:70
  105.8 1.7 collective-permute-start.14
  108.9 1.5 collective-permute-start.16
  110.4 9.7 %assemble.1 = bf16[2304,1152]{1,0:T(8,128)(2,1)S(1)} custom-call(s32[48]{0:T(128)S(1)} %concatenate.118.index_ref, bf16[1,384,1152]{2,1,0:T(8,128)(2,1)S(1)} %pad_maximum_fusion.4.refs_0_, bf16[1,384,1152]{2,1,0:T(8,128)(2,1)S(1)} %collective-permute-done.5.refs_1_, bf16[1,384,1152]{2,1,0:T(8,128)(2,1)S(1)} %pad_maximum_fusion.5.refs_2_, ...), custom_call_target="tpu_custom_call" | custom-call | tf_op jit(solution)/shard_map/assemble/pallas_call | solution.py:206
  124.3 2.5 add_convert_fusion
  126.8 5.8 %attention.1 = bf16[4,144,512]{2,1,0:T(8,128)(2,1)S(1)} custom-call(s32[2,256]{1,0:T(2,128)S(1)} %pad_add_fusion.row_ref, s32[256,2]{1,0:T(8,128)S(1)} %bitcast.132, bf16[3,4,144,512]{3,2,1,0:T(8,128)(2,1)S(1)} %bitcast.115, bf16[3,4,144,512]{3,2,1,0:T(8,128)(2,1)S(1)} %bitcast.116, bf16[3,4,144,512]{3,2,1,0:T(8,128)(2,1)S(1)} %bitcast.117), custom_call_target="tpu_custom_call" | custom-call | flops 1024 | bytes 1024 | tf_op jit(solution)/shard_map/attention/pallas_call | solution.py:430
  135.8 8.6 %collective-permute-done.19 = bf16[2,192,1152]{2,1,0:T(8,128)(2,1)S(1)} collective-permute-done((bf16[2,192,1152]{2,1,0:T(8,128)(2,1)S(1)}, bf16[2,192,1152]{2,1,0:T(8,128)(2,1)S(1)}, u32[]{:S(2)}, u32[]{:S(2)}) %collective-permute-start.19) | collective-permute-done | bytes 884768 | tf_op jit(solution)/shard_map/ppermute | solution.py:70
  151.3 6.5 %collective-permute-done.21 = bf16[2,192,1152]{2,1,0:T(8,128)(2,1)S(1)} collective-permute-done((bf16[2,192,1152]{2,1,0:T(8,128)(2,1)S(1)}, bf16[2,192,1152]{2,1,0:T(8,128)(2,1)S(1)}, u32[]{:S(2)}, u32[]{:S(2)}) %collective-permute-start.21) | collective-permute-done | bytes 884768 | tf_op jit(solution)/shard_map/ppermute | solution.py:69
  160.4 2.0 fusion.14
  164.9 2.3 pad_maximum_fusion.3.g_ref
  169.6 15.5 %collective-permute-done.26.refs_1_ = bf16[2,384,1152]{2,1,0:T(8,128)(2,1)} collective-permute-done((bf16[2,384,1152]{2,1,0:T(8,128)(2,1)}, bf16[2,384,1152]{2,1,0:T(8,128)(2,1)}, u32[]{:S(2)}, u32[]{:S(2)}) %collective-permute-start.26) | collective-permute-done | bytes 1769504 | tf_op jit(solution)/shard_map/ppermute | solution.py:70
  185.1 10.3 %mlp_part.3 = (bf16[2,384,1152]{2,1,0:T(8,128)(2,1)}, bf16[2,384,1152]{2,1,0:T(8,128)(2,1)}, f32[2,384]{1,0:T(2,128)S(1)}, f32[256,1152]{1,0:T(8,128)S(1)}, f32[...) custom-call(bf16[512,1152]{1,0:T(8,128)(2,1)S(1)} %constant_dynamic-update-slice_fusion.x_ref, ...), custom_call_target="tpu_custom_call" | custom-call | flops 1024 | bytes 1024 | tf_op jit(solution)/shard_map/mlp_part/pallas_call | solution.py:488
  200.1 11.8 %mlp_part.4 = (bf16[2,384,1152]{2,1,0:T(8,128)(2,1)}, bf16[2,384,1152]{2,1,0:T(8,128)(2,1)}, f32[2,384]{1,0:T(2,128)S(1)}, f32[256,1152]{1,0:T(8,128)S(1)}, f32[...) custom-call(bf16[512,1152]{1,0:T(8,128)(2,1)S(1)} %constant_dynamic-update-slice_fusion.x_ref, ...), custom_call_target="tpu_custom_call" | custom-call | flops 1024 | bytes 1024 | tf_op jit(solution)/shard_map/mlp_part/pallas_call | solution.py:488
  216.7 12.7 %mlp_part.5 = (bf16[2,384,1152]{2,1,0:T(8,128)(2,1)}, bf16[2,384,1152]{2,1,0:T(8,128)(2,1)}, f32[2,384]{1,0:T(2,128)S(1)}, f32[256,1152]{1,0:T(8,128)S(1)}, f32[...) custom-call(bf16[512,1152]{1,0:T(8,128)(2,1)S(1)} %constant_dynamic-update-slice_fusion.x_ref, ...), custom_call_target="tpu_custom_call" | custom-call | flops 1024 | bytes 1024 | tf_op jit(solution)/shard_map/mlp_part/pallas_call | solution.py:488
  238.9 2.1 reduce.5
  241.8 1.6 reshape.539
  245.4 1.6 reshape.540
  251.0 1.7 copy-done.12
  258.4 5.1 %middle.1 = (f32[256,1152]{1,0:T(8,128)S(1)}, bf16[256,1152]{1,0:T(8,128)(2,1)}, f32[1,1152]{1,0:T(1,128)S(1)}, bf16[576,256]{1,0:T(8,128)(2,1)S(1)}, bf16[576,2...) custom-call(s32[1]{0:T(128)} %bitcast.34.core_ref, f32[256,1152]{1,0:T(8,128)S(1)} %copy-done.16, ...), custom_call_target="tpu_custom_call" | custom-call | flops 1024 | bytes 1024 | tf_op jit(solution)/shard_map/middle/pallas_call | solution.py:299
  270.7 1.6 reshape.551.refs_4_
  275.9 7.5 %attention_back.1 = bf16[3,4,144,512]{3,2,1,0:T(8,128)(2,1)S(1)} custom-call(s32[2,256]{1,0:T(2,128)S(1)} %copy-done.50, s32[256,2]{1,0:T(8,128)S(1)} %bitcast.133, bf16[3,4,144,512]{3,2,1,0:T(8,128)(2,1)S(1)} %bitcast.118, bf16[3,4,144,512]{3,2,1,0:T(8,128)(2,1)S(1)} %bitcast.119, bf16[3,4,144,512]{3,2,1,0:T(8,128)(2,1)S(1)} %bitcast.120, ...), custom_call_target="tpu_custom_call" | custom-call | flops 1024 | bytes 1024 | tf_op jit(solution)/shard_map/attention_back/pallas_call | solution.py:440
  291.8 1.5 all_to_all.19
  293.3 5.0 %all-to-all-start.1 = ((f32[32,1,288]{2,1,0:T(1,128)}), f32[32,1,288]{2,1,0:T(1,128)}, u32[]{:S(2)}, u32[]{:S(2)}) async-start(f32[32,1,288]{2,1,0:T(1,128)} %all_to_all.19), calls=%async_computation.1 | async-start | bytes 98304 | tf_op jit(solution)/shard_map/all_to_all | solution.py:738
  298.3 3.4 add_convert_fusion.6
  301.7 1.7 collective-permute-start.51
  303.4 4.8 %fusion.1 = f32[512,1152]{1,0:T(8,128)S(1)} fusion(bf16[1728,512]{1,0:T(8,128)(2,1)S(1)} %bitcast.122, bf16[2304,1152]{1,0:T(8,128)(2,1)} %copy-done.13), kind=kOutput, calls=%fused_computation.5 | convolution fusion | flops 2038431744 | bytes 8110080 | tf_op jit(solution)/shard_map/dot_general | solution.py:30
  308.2 1.5 fusion.65
  310.5 3.2 add_convert_fusion.4
  315.8 3.2 add_convert_fusion.2
  320.5 1.7 collective-permute-start.55
  324.8 3.3 mlp_end_kernel.1
  328.1 5.0 %collective-permute-done.51 = bf16[2,192,1152]{2,1,0:T(8,128)(2,1)} collective-permute-done((bf16[2,192,1152]{2,1,0:T(8,128)(2,1)}, bf16[2,192,1152]{2,1,0:T(8,128)(2,1)}, u32[]{:S(2)}, u32[]{:S(2)}) %collective-permute-start.51) | collective-permute-done | bytes 884768 | tf_op jit(solution)/shard_map/ppermute | solution.py:70
  334.2 1.6 collective-permute-start.52
  335.9 3.4 attn_end_kernel.1
  341.6 11.5 %collective-permute-done.33 = bf16[16,3456]{1,0:T(8,128)(2,1)S(1)} collective-permute-done((bf16[16,3456]{1,0:T(8,128)(2,1)S(1)}, bf16[16,3456]{1,0:T(8,128)(2,1)S(1)}, u32[]{:S(2)}, u32[]{:S(2)}) %collective-permute-start.33) | collective-permute-done | bytes 110624 | tf_op jit(solution)/shard_map/ppermute | solution.py:69
  353.2 5.6 %fusion.73 = f32[16,1152]{1,0:T(8,128)S(1)} fusion(bf16[16,3456]{1,0:T(8,128)(2,1)S(1)} %get-tuple-element.116, bf16[1152,3456]{1,0:T(8,128)(2,1)} %param.40), kind=kOutput, calls=%fused_computation.225 | convolution fusion | flops 127401984 | bytes 8146944 | tf_op jit(solution)/shard_map/dot_general | solution.py:30
  358.8 1.8 collective-permute-start.34
  361.3 13.5 %weight_grad.1 = (bf16[1,384,1152]{2,1,0:T(8,128)(2,1)S(1)}, bf16[1,384,1152]{2,1,0:T(8,128)(2,1)S(1)}, bf16[1,384,1152]{2,1,0:T(8,128)(2,1)S(1)}, bf16[1,384,11...) custom-call(s32[48]{0:T(128)S(1)} %copy-done.52, ...), custom_call_target="tpu_custom_call" | custom-call | flops 1024 | bytes 1024 | tf_op jit(solution)/shard_map/weight_grad/pallas_call | solution.py:248
  374.8 1.6 collective-permute-start.41
  382.3 2.5 collective-permute-start.57
  384.8 13.6 %collective-permute-done.35 = bf16[16,3456]{1,0:T(8,128)(2,1)S(1)} collective-permute-done((bf16[16,3456]{1,0:T(8,128)(2,1)S(1)}, bf16[16,3456]{1,0:T(8,128)(2,1)S(1)}, u32[]{:S(2)}, u32[]{:S(2)}) %collective-permute-start.35) | collective-permute-done | bytes 110624 | tf_op jit(solution)/shard_map/ppermute | solution.py:70
  399.6 13.3 %collective-permute-done.36 = bf16[32,3456]{1,0:T(8,128)(2,1)S(1)} collective-permute-done((bf16[32,3456]{1,0:T(8,128)(2,1)S(1)}, bf16[32,3456]{1,0:T(8,128)(2,1)S(1)}, u32[]{:S(2)}, u32[]{:S(2)}) %collective-permute-start.36) | collective-permute-done | bytes 221216 | tf_op jit(solution)/shard_map/ppermute | solution.py:70
  413.0 2.9 collective-permute-start.37
  420.8 11.5 %collective-permute-done.37 = bf16[64,3456]{1,0:T(8,128)(2,1)S(1)} collective-permute-done((bf16[64,3456]{1,0:T(8,128)(2,1)S(1)}, bf16[64,3456]{1,0:T(8,128)(2,1)S(1)}, u32[]{:S(2)}, u32[]{:S(2)}) %collective-permute-start.37) | collective-permute-done | bytes 442400 | tf_op jit(solution)/shard_map/ppermute | solution.py:70
  432.5 1.7 collective-permute-start.43
  434.9 5.4 %collective-permute-done.43 = bf16[1,96,1152]{2,1,0:T(8,128)(2,1)S(1)} collective-permute-done((bf16[1,96,1152]{2,1,0:T(8,128)(2,1)S(1)}, bf16[1,96,1152]{2,1,0:T(8,128)(2,1)S(1)}, u32[]{:S(2)}, u32[]{:S(2)}) %collective-permute-start.43) | collective-permute-done | bytes 221216 | tf_op jit(solution)/shard_map/ppermute | solution.py:69
  442.4 1.6 collective-permute-start.50
  444.0 15.2 %collective-permute-done.50 = bf16[1,144,1152]{2,1,0:T(8,128)(2,1)S(1)} collective-permute-done((bf16[1,144,1152]{2,1,0:T(8,128)(2,1)S(1)}, bf16[1,144,1152]{2,1,0:T(8,128)(2,1)S(1)}, u32[]{:S(2)}, u32[]{:S(2)}) %collective-permute-start.50) | collective-permute-done | bytes 331808 | tf_op jit(solution)/shard_map/ppermute | solution.py:70
  (416 shorter events, 128.3 us)
Async XLA Ops:
  0.7 19.2 %collective-permute-start = (bf16[1,144,1152]{2,1,0:T(8,128)(2,1)}, bf16[1,144,1152]{2,1,0:T(8,128)(2,1)S(1)}, u32[]{:S(2)}, u32[]{:S(2)}) collective-permute-start(bf16[1,144,1152]{2,1,0:T(8,128)(2,1)} %bitcast.169), channel_id=1, source_target_pairs={{0,16},{2,18},{4,20},{6,22},{8,24},{10,26},{12,28},{14,30},{16,0},... | collective-permute-start | bytes 995336 | tf_op jit(solution)/shard_map/ppermute | solution.py:70
  4.8 8.2 %collective-permute-start.2 = (s32[256]{0:T(256)}, s32[256]{0:T(256)S(1)}, u32[]{:S(2)}, u32[]{:S(2)}) collective-permute-start(s32[256]{0:T(256)} %bitcast.180), channel_id=1, source_target_pairs={{0,2},{2,0},{4,6},{6,4},{8,10},{10,8},{12,14},{14,12},{16,18},{18,... | collective-permute-start | bytes 3080 | tf_op jit(solution)/shard_map/ppermute | solution.py:70
  12.9 97.5 %copy-start.51 = (s32[48]{0:T(128)}, s32[48]{0:T(128)S(1)}, u32[]{:S(2)}) copy-start(s32[48]{0:T(128)S(1)} %concatenate.118.index_ref) | copy-start | bytes 580
  13.4 113.4 %copy-start.49 = (s32[2,256]{1,0:T(2,128)}, s32[2,256]{1,0:T(2,128)S(1)}, u32[]{:S(2)}) copy-start(s32[2,256]{1,0:T(2,128)S(1)} %pad_add_fusion.row_ref) | copy-start | bytes 6148
  13.5 113.3 %copy-start.26 = (s32[2,256]{0,1:T(8,128)}, s32[2,256]{0,1:T(8,128)S(1)}, u32[]{:S(2)}) copy-start(s32[2,256]{0,1:T(8,128)S(1)} %copy.135) | copy-start | bytes 6148
  20.0 39.7 %collective-permute-start.9 = (bf16[1,96,1152]{2,1,0:T(8,128)(2,1)S(1)}, bf16[1,96,1152]{2,1,0:T(8,128)(2,1)}, u32[]{:S(2)}, u32[]{:S(2)}) collective-permute-start(bf16[1,96,1152]{2,1,0:T(8,128)(2,1)S(1)} %bitcast.156), channel_id=1, source_target_pairs={{0,8},{2,10},{4,12},{6,14},{8,0},{10,2},{12,4},{14,6},{16,24},{18,... | collective-permute-start | bytes 663560 | tf_op jit(solution)/shard_map/ppermute | solution.py:70
  20.9 39.9 %collective-permute-start.3 = (bf16[1,96,1152]{2,1,0:T(8,128)(2,1)S(1)}, bf16[1,96,1152]{2,1,0:T(8,128)(2,1)}, u32[]{:S(2)}, u32[]{:S(2)}) collective-permute-start(bf16[1,96,1152]{2,1,0:T(8,128)(2,1)S(1)} %bitcast.153), channel_id=1, source_target_pairs={{0,1},{1,0},{2,3},{3,2},{4,5},{5,4},{6,7},{7,6},{8,9},{9,8},{10,11... | collective-permute-start | bytes 663560 | tf_op jit(solution)/shard_map/ppermute | solution.py:69
  22.4 40.8 %collective-permute-start.6 = (bf16[1,96,1152]{2,1,0:T(8,128)(2,1)S(1)}, bf16[1,96,1152]{2,1,0:T(8,128)(2,1)S(1)}, u32[]{:S(2)}, u32[]{:S(2)}) collective-permute-start(bf16[1,96,1152]{2,1,0:T(8,128)(2,1)S(1)} %bitcast.150), channel_id=1, source_target_pairs={{0,4},{2,6},{4,0},{6,2},{8,12},{10,14},{12,8},{14,10},{16,20},{18,... | collective-permute-start | bytes 663560 | tf_op jit(solution)/shard_map/ppermute | solution.py:70
  23.9 61.7 %collective-permute-start.13 = (bf16[2,144,1152]{2,1,0:T(8,128)(2,1)S(1)}, bf16[2,144,1152]{2,1,0:T(8,128)(2,1)}, u32[]{:S(2)}, u32[]{:S(2)}) collective-permute-start(bf16[2,144,1152]{2,1,0:T(8,128)(2,1)S(1)} %pad_maximum_fusion.12), channel_id=1, source_target_pairs={{0,16},{2,18},{4,20},{6,22},{8,24},{10,26},{12,28},{14,30},{16,0},... | collective-permute-start | bytes 1990664 | tf_op jit(solution)/shard_map/ppermute | solution.py:70
  31.7 5.9 %collective-permute-start.1 = (bf16[16,3456]{1,0:T(8,128)(2,1)S(1)}, bf16[16,3456]{1,0:T(8,128)(2,1)S(1)}, u32[]{:S(2)}, u32[]{:S(2)}) collective-permute-start(bf16[16,3456]{1,0:T(8,128)(2,1)S(1)} %fusion), channel_id=1, source_target_pairs={{0,1},{1,0},{2,3},{3,2},{4,5},{5,4},{6,7},{7,6},{8,9},{9,8},{10,11... | collective-permute-start | bytes 331784 | tf_op jit(solution)/shard_map/ppermute | solution.py:69
  34.7 23.0 %all-to-all-start = ((bf16[32,2,720]{2,1,0:T(2,128)(2,1)}), bf16[32,2,720]{2,1,0:T(2,128)(2,1)S(1)}, u32[]{:S(2)}, u32[]{:S(2)}) async-start(bf16[32,2,720]{2,1,0:T(2,128)(2,1)} %reshape.564), calls=%async_computation | async-start | bytes 196608 | tf_op jit(solution)/shard_map/all_to_all | solution.py:557
  39.2 49.5 %collective-permute-start.12 = (bf16[256,1152]{1,0:T(8,128)(2,1)S(1)}, bf16[256,1152]{1,0:T(8,128)(2,1)}, u32[]{:S(2)}, u32[]{:S(2)}) collective-permute-start(bf16[256,1152]{1,0:T(8,128)(2,1)S(1)} %fusion.13), channel_id=1, source_target_pairs={{0,2},{2,0},{4,6},{6,4},{8,10},{10,8},{12,14},{14,12},{16,18},{18,... | collective-permute-start | bytes 1769480 | tf_op jit(solution)/shard_map/ppermute | solution.py:70
  59.8 105.2 %collective-permute-start.23 = (bf16[256,1152]{1,0:T(8,128)(2,1)}, bf16[256,1152]{1,0:T(8,128)(2,1)}, u32[]{:S(2)}, u32[]{:S(2)}) collective-permute-start(bf16[256,1152]{1,0:T(8,128)(2,1)} %get-tuple-element.172), channel_id=1, source_target_pairs={{0,2},{2,0},{4,6},{6,4},{8,10},{10,8},{12,14},{14,12},{16,18},{18,... | collective-permute-start | bytes 1769480 | tf_op jit(solution)/shard_map/ppermute | solution.py:70
  60.8 12.6 %collective-permute-start.10 = (bf16[1,192,1152]{2,1,0:T(8,128)(2,1)S(1)}, bf16[1,192,1152]{2,1,0:T(8,128)(2,1)S(1)}, u32[]{:S(2)}, u32[]{:S(2)}) collective-permute-start(bf16[1,192,1152]{2,1,0:T(8,128)(2,1)S(1)} %pad_maximum_fusion.16), channel_id=1, source_target_pairs={{0,1},{1,0},{2,3},{3,2},{4,5},{5,4},{6,7},{7,6},{8,9},{9,8},{10,11... | collective-permute-start | bytes 1327112 | tf_op jit(solution)/shard_map/ppermute | solution.py:69
  63.2 12.4 %collective-permute-start.4 = (bf16[1,192,1152]{2,1,0:T(8,128)(2,1)S(1)}, bf16[1,192,1152]{2,1,0:T(8,128)(2,1)S(1)}, u32[]{:S(2)}, u32[]{:S(2)}) collective-permute-start(bf16[1,192,1152]{2,1,0:T(8,128)(2,1)S(1)} %pad_maximum_fusion.14), channel_id=1, source_target_pairs={{0,4},{2,6},{4,0},{6,2},{8,12},{10,14},{12,8},{14,10},{16,20},{18,... | collective-permute-start | bytes 1327112 | tf_op jit(solution)/shard_map/ppermute | solution.py:70
  73.5 11.8 %collective-permute-start.7 = (bf16[1,192,1152]{2,1,0:T(8,128)(2,1)S(1)}, bf16[1,192,1152]{2,1,0:T(8,128)(2,1)S(1)}, u32[]{:S(2)}, u32[]{:S(2)}) collective-permute-start(bf16[1,192,1152]{2,1,0:T(8,128)(2,1)S(1)} %pad_maximum_fusion.15), channel_id=1, source_target_pairs={{0,8},{2,10},{4,12},{6,14},{8,0},{10,2},{12,4},{14,6},{16,24},{18,... | collective-permute-start | bytes 1327112 | tf_op jit(solution)/shard_map/ppermute | solution.py:70
  75.6 20.9 %collective-permute-start.11 = (bf16[1,384,1152]{2,1,0:T(8,128)(2,1)S(1)}, bf16[1,384,1152]{2,1,0:T(8,128)(2,1)S(1)}, u32[]{:S(2)}, u32[]{:S(2)}) collective-permute-start(bf16[1,384,1152]{2,1,0:T(8,128)(2,1)S(1)} %pad_maximum_fusion.6.refs_4_), channel_id=1, source_target_pairs={{0,4},{2,6},{4,0},{6,2},{8,12},{10,14},{12,8},{14,10},{16,20},{18,... | collective-permute-start | bytes 2654216 | tf_op jit(solution)/shard_map/ppermute | solution.py:70
  85.3 20.4 %collective-permute-start.5 = (bf16[1,384,1152]{2,1,0:T(8,128)(2,1)S(1)}, bf16[1,384,1152]{2,1,0:T(8,128)(2,1)S(1)}, u32[]{:S(2)}, u32[]{:S(2)}) collective-permute-start(bf16[1,384,1152]{2,1,0:T(8,128)(2,1)S(1)} %pad_maximum_fusion.4.refs_0_), channel_id=1, source_target_pairs={{0,8},{2,10},{4,12},{6,14},{8,0},{10,2},{12,4},{14,6},{16,24},{18,... | collective-permute-start | bytes 2654216 | tf_op jit(solution)/shard_map/ppermute | solution.py:70
  85.6 20.2 %collective-permute-start.8 = (bf16[1,384,1152]{2,1,0:T(8,128)(2,1)S(1)}, bf16[1,384,1152]{2,1,0:T(8,128)(2,1)S(1)}, u32[]{:S(2)}, u32[]{:S(2)}) collective-permute-start(bf16[1,384,1152]{2,1,0:T(8,128)(2,1)S(1)} %pad_maximum_fusion.5.refs_2_), channel_id=1, source_target_pairs={{0,1},{1,0},{2,3},{3,2},{4,5},{5,4},{6,7},{7,6},{8,9},{9,8},{10,11... | collective-permute-start | bytes 2654216 | tf_op jit(solution)/shard_map/ppermute | solution.py:69
  89.9 34.4 %copy-start.19 = (bf16[512,1152]{1,0:T(8,128)(2,1)}, bf16[512,1152]{1,0:T(8,128)(2,1)S(1)}, u32[]{:S(2)}) copy-start(bf16[512,1152]{1,0:T(8,128)(2,1)S(1)} %pad_maximum_fusion.2.x_ref) | copy-start | bytes 3538948
  105.8 17.1 %collective-permute-start.14 = (bf16[2,96,1152]{2,1,0:T(8,128)(2,1)S(1)}, bf16[2,96,1152]{2,1,0:T(8,128)(2,1)S(1)}, u32[]{:S(2)}, u32[]{:S(2)}) collective-permute-start(bf16[2,96,1152]{2,1,0:T(8,128)(2,1)S(1)} %bitcast.144), channel_id=1, source_target_pairs={{0,1},{1,0},{2,3},{3,2},{4,5},{5,4},{6,7},{7,6},{8,9},{9,8},{10,11... | collective-permute-start | bytes 1327112 | tf_op jit(solution)/shard_map/ppermute | solution.py:69
  107.5 16.0 %collective-permute-start.15 = (bf16[2,96,1152]{2,1,0:T(8,128)(2,1)S(1)}, bf16[2,96,1152]{2,1,0:T(8,128)(2,1)S(1)}, u32[]{:S(2)}, u32[]{:S(2)}) collective-permute-start(bf16[2,96,1152]{2,1,0:T(8,128)(2,1)S(1)} %bitcast.141), channel_id=1, source_target_pairs={{0,4},{2,6},{4,0},{6,2},{8,12},{10,14},{12,8},{14,10},{16,20},{18,... | collective-permute-start | bytes 1327112 | tf_op jit(solution)/shard_map/ppermute | solution.py:70
  108.9 15.4 %collective-permute-start.16 = (bf16[2,96,1152]{2,1,0:T(8,128)(2,1)S(1)}, bf16[2,96,1152]{2,1,0:T(8,128)(2,1)S(1)}, u32[]{:S(2)}, u32[]{:S(2)}) collective-permute-start(bf16[2,96,1152]{2,1,0:T(8,128)(2,1)S(1)} %bitcast.138), channel_id=1, source_target_pairs={{0,8},{2,10},{4,12},{6,14},{8,0},{10,2},{12,4},{14,6},{16,24},{18,... | collective-permute-start | bytes 1327112 | tf_op jit(solution)/shard_map/ppermute | solution.py:70
  120.2 27.1 %collective-permute-start.18 = (bf16[576,1152]{1,0:T(8,128)(2,1)S(1)}, bf16[576,1152]{1,0:T(8,128)(2,1)S(1)}, u32[]{:S(2)}, u32[]{:S(2)}) collective-permute-start(bf16[576,1152]{1,0:T(8,128)(2,1)S(1)} %slice.393), channel_id=1, source_target_pairs={{0,2},{2,0},{4,6},{6,4},{8,10},{10,8},{12,14},{14,12},{16,18},{18,... | collective-permute-start | bytes 3981320 | tf_op jit(solution)/shard_map/ppermute | solution.py:70
  122.9 21.4 %collective-permute-start.19 = (bf16[2,192,1152]{2,1,0:T(8,128)(2,1)S(1)}, bf16[2,192,1152]{2,1,0:T(8,128)(2,1)S(1)}, u32[]{:S(2)}, u32[]{:S(2)}) collective-permute-start(bf16[2,192,1152]{2,1,0:T(8,128)(2,1)S(1)} %pad_maximum_fusion.7), channel_id=1, source_target_pairs={{0,4},{2,6},{4,0},{6,2},{8,12},{10,14},{12,8},{14,10},{16,20},{18,... | collective-permute-start | bytes 2654216 | tf_op jit(solution)/shard_map/ppermute | solution.py:70
  123.6 22.3 %collective-permute-start.20 = (bf16[2,192,1152]{2,1,0:T(8,128)(2,1)S(1)}, bf16[2,192,1152]{2,1,0:T(8,128)(2,1)S(1)}, u32[]{:S(2)}, u32[]{:S(2)}) collective-permute-start(bf16[2,192,1152]{2,1,0:T(8,128)(2,1)S(1)} %pad_maximum_fusion.8), channel_id=1, source_target_pairs={{0,8},{2,10},{4,12},{6,14},{8,0},{10,2},{12,4},{14,6},{16,24},{18,... | collective-permute-start | bytes 2654216 | tf_op jit(solution)/shard_map/ppermute | solution.py:70
  132.7 2.6 collective-permute-start.17
  135.3 22.5 %collective-permute-start.21 = (bf16[2,192,1152]{2,1,0:T(8,128)(2,1)S(1)}, bf16[2,192,1152]{2,1,0:T(8,128)(2,1)S(1)}, u32[]{:S(2)}, u32[]{:S(2)}) collective-permute-start(bf16[2,192,1152]{2,1,0:T(8,128)(2,1)S(1)} %pad_maximum_fusion.9), channel_id=1, source_target_pairs={{0,1},{1,0},{2,3},{3,2},{4,5},{5,4},{6,7},{7,6},{8,9},{9,8},{10,11... | collective-permute-start | bytes 2654216 | tf_op jit(solution)/shard_map/ppermute | solution.py:69
  145.3 39.8 %collective-permute-start.26 = (bf16[2,384,1152]{2,1,0:T(8,128)(2,1)}, bf16[2,384,1152]{2,1,0:T(8,128)(2,1)}, u32[]{:S(2)}, u32[]{:S(2)}) collective-permute-start(bf16[2,384,1152]{2,1,0:T(8,128)(2,1)} %constant_dynamic-update-slice_fusion.14.refs_0_), channel_id=1, source_target_pairs={{0,8},{2,10},{4,12},{6,14},{8,0},{10,2},{12,4},{14,6},{16,24},{18,... | collective-permute-start | bytes 5308424 | tf_op jit(solution)/shard_map/ppermute | solution.py:70
  146.8 52.7 %collective-permute-start.25 = (bf16[2,384,1152]{2,1,0:T(8,128)(2,1)}, bf16[2,384,1152]{2,1,0:T(8,128)(2,1)}, u32[]{:S(2)}, u32[]{:S(2)}) collective-permute-start(bf16[2,384,1152]{2,1,0:T(8,128)(2,1)} %constant_dynamic-update-slice_fusion.11.refs_0_), channel_id=1, source_target_pairs={{0,1},{1,0},{2,3},{3,2},{4,5},{5,4},{6,7},{7,6},{8,9},{9,8},{10,11... | collective-permute-start | bytes 5308424 | tf_op jit(solution)/shard_map/ppermute | solution.py:69
  158.8 57.3 %collective-permute-start.24 = (bf16[2,384,1152]{2,1,0:T(8,128)(2,1)}, bf16[2,384,1152]{2,1,0:T(8,128)(2,1)}, u32[]{:S(2)}, u32[]{:S(2)}) collective-permute-start(bf16[2,384,1152]{2,1,0:T(8,128)(2,1)} %constant_dynamic-update-slice_fusion.8.refs_0_), channel_id=1, source_target_pairs={{0,4},{2,6},{4,0},{6,2},{8,12},{10,14},{12,8},{14,10},{16,20},{18,... | collective-permute-start | bytes 5308424 | tf_op jit(solution)/shard_map/ppermute | solution.py:70
  163.4 5.0 %collective-permute-start.22 = (bf16[256,1152]{1,0:T(8,128)(2,1)}, bf16[256,1152]{1,0:T(8,128)(2,1)}, u32[]{:S(2)}, u32[]{:S(2)}) collective-permute-start(bf16[256,1152]{1,0:T(8,128)(2,1)} %fusion.14), channel_id=1, source_target_pairs={{0,2},{2,0},{4,6},{6,4},{8,10},{10,8},{12,14},{14,12},{16,18},{18,... | collective-permute-start | bytes 1769480 | tf_op jit(solution)/shard_map/ppermute | solution.py:70
  232.4 16.1 %collective-permute-start.27 = (f32[256,1152]{1,0:T(8,128)}, f32[256,1152]{1,0:T(8,128)}, u32[]{:S(2)}, u32[]{:S(2)}) collective-permute-start(f32[256,1152]{1,0:T(8,128)} %get-tuple-element.78), channel_id=1, source_target_pairs={{0,2},{2,0},{4,6},{6,4},{8,10},{10,8},{12,14},{14,12},{16,18},{18,... | collective-permute-start | bytes 3538952 | tf_op jit(solution)/shard_map/ppermute | solution.py:70
  232.4 51.3 %collective-permute-start.31 = (bf16[2,384,1152]{2,1,0:T(8,128)(2,1)}, bf16[2,384,1152]{2,1,0:T(8,128)(2,1)}, u32[]{:S(2)}, u32[]{:S(2)}) collective-permute-start(bf16[2,384,1152]{2,1,0:T(8,128)(2,1)} %get-tuple-element.86), channel_id=1, source_target_pairs={{0,1},{1,0},{2,3},{3,2},{4,5},{5,4},{6,7},{7,6},{8,9},{9,8},{10,11... | collective-permute-start | bytes 5308424 | tf_op jit(solution)/shard_map/ppermute | solution.py:69
  232.7 51.0 %collective-permute-start.30 = (bf16[2,384,1152]{2,1,0:T(8,128)(2,1)}, bf16[2,384,1152]{2,1,0:T(8,128)(2,1)}, u32[]{:S(2)}, u32[]{:S(2)}) collective-permute-start(bf16[2,384,1152]{2,1,0:T(8,128)(2,1)} %get-tuple-element.85), channel_id=1, source_target_pairs={{0,8},{2,10},{4,12},{6,14},{8,0},{10,2},{12,4},{14,6},{16,24},{18,... | collective-permute-start | bytes 5308424 | tf_op jit(solution)/shard_map/ppermute | solution.py:70
  267.0 6.9 %collective-permute-start.29 = (bf16[576,256]{1,0:T(8,128)(2,1)}, bf16[576,256]{1,0:T(8,128)(2,1)}, u32[]{:S(2)}, u32[]{:S(2)}) collective-permute-start(bf16[576,256]{1,0:T(8,128)(2,1)} %get-tuple-element.84), channel_id=1, source_target_pairs={{0,2},{2,0},{4,6},{6,4},{8,10},{10,8},{12,14},{14,12},{16,18},{18,... | collective-permute-start | bytes 884744 | tf_op jit(solution)/shard_map/ppermute | solution.py:70
  272.3 42.2 %collective-permute-start.40 = (bf16[2,384,1152]{2,1,0:T(8,128)(2,1)}, bf16[2,384,1152]{2,1,0:T(8,128)(2,1)}, u32[]{:S(2)}, u32[]{:S(2)}) collective-permute-start(bf16[2,384,1152]{2,1,0:T(8,128)(2,1)} %get-tuple-element.101), channel_id=1, source_target_pairs={{0,4},{2,6},{4,0},{6,2},{8,12},{10,14},{12,8},{14,10},{16,20},{18,... | collective-permute-start | bytes 5308424 | tf_op jit(solution)/shard_map/ppermute | solution.py:70
  272.7 47.7 %collective-permute-start.28 = (f32[256,1152]{1,0:T(8,128)}, f32[256,1152]{1,0:T(8,128)}, u32[]{:S(2)}, u32[]{:S(2)}) collective-permute-start(f32[256,1152]{1,0:T(8,128)} %copy-done.60), channel_id=1, source_target_pairs={{0,2},{2,0},{4,6},{6,4},{8,10},{10,8},{12,14},{14,12},{16,18},{18,... | collective-permute-start | bytes 3538952 | tf_op jit(solution)/shard_map/ppermute | solution.py:70
  283.4 77.9 %collective-permute-start.39 = (bf16[576,1152]{1,0:T(8,128)(2,1)}, bf16[576,1152]{1,0:T(8,128)(2,1)}, u32[]{:S(2)}, u32[]{:S(2)}) collective-permute-start(bf16[576,1152]{1,0:T(8,128)(2,1)} %get-tuple-element.94), channel_id=1, source_target_pairs={{0,2},{2,0},{4,6},{6,4},{8,10},{10,8},{12,14},{14,12},{16,18},{18,... | collective-permute-start | bytes 3981320 | tf_op jit(solution)/shard_map/ppermute | solution.py:70
  293.3 25.7 %all-to-all-start.1 = ((f32[32,1,288]{2,1,0:T(1,128)}), f32[32,1,288]{2,1,0:T(1,128)}, u32[]{:S(2)}, u32[]{:S(2)}) async-start(f32[32,1,288]{2,1,0:T(1,128)} %all_to_all.19), calls=%async_computation.1 | async-start | bytes 98304 | tf_op jit(solution)/shard_map/all_to_all | solution.py:738
  301.7 31.4 %collective-permute-start.51 = (bf16[2,192,1152]{2,1,0:T(8,128)(2,1)}, bf16[2,192,1152]{2,1,0:T(8,128)(2,1)}, u32[]{:S(2)}, u32[]{:S(2)}) collective-permute-start(bf16[2,192,1152]{2,1,0:T(8,128)(2,1)} %get-tuple-element.118), channel_id=1, source_target_pairs={{0,4},{2,6},{4,0},{6,2},{8,12},{10,14},{12,8},{14,10},{16,20},{18,... | collective-permute-start | bytes 2654216 | tf_op jit(solution)/shard_map/ppermute | solution.py:70
  309.7 26.1 %collective-permute-start.32 = (f32[256,1152]{1,0:T(8,128)}, f32[256,1152]{1,0:T(8,128)}, u32[]{:S(2)}, u32[]{:S(2)}) collective-permute-start(f32[256,1152]{1,0:T(8,128)} %get-tuple-element.123), channel_id=1, source_target_pairs={{0,2},{2,0},{4,6},{6,4},{8,10},{10,8},{12,14},{14,12},{16,18},{18,... | collective-permute-start | bytes 3538952 | tf_op jit(solution)/shard_map/ppermute | solution.py:70
  314.4 25.4 %collective-permute-start.53 = (bf16[2,192,1152]{2,1,0:T(8,128)(2,1)}, bf16[2,192,1152]{2,1,0:T(8,128)(2,1)}, u32[]{:S(2)}, u32[]{:S(2)}) collective-permute-start(bf16[2,192,1152]{2,1,0:T(8,128)(2,1)} %get-tuple-element.120), channel_id=1, source_target_pairs={{0,8},{2,10},{4,12},{6,14},{8,0},{10,2},{12,4},{14,6},{16,24},{18,... | collective-permute-start | bytes 2654216 | tf_op jit(solution)/shard_map/ppermute | solution.py:70
  320.5 40.1 %collective-permute-start.55 = (bf16[2,192,1152]{2,1,0:T(8,128)(2,1)}, bf16[2,192,1152]{2,1,0:T(8,128)(2,1)S(1)}, u32[]{:S(2)}, u32[]{:S(2)}) collective-permute-start(bf16[2,192,1152]{2,1,0:T(8,128)(2,1)} %get-tuple-element.122), channel_id=1, source_target_pairs={{0,1},{1,0},{2,3},{3,2},{4,5},{5,4},{6,7},{7,6},{8,9},{9,8},{10,11... | collective-permute-start | bytes 2654216 | tf_op jit(solution)/shard_map/ppermute | solution.py:69
  334.2 43.2 %collective-permute-start.52 = (bf16[2,96,1152]{2,1,0:T(8,128)(2,1)S(1)}, bf16[2,96,1152]{2,1,0:T(8,128)(2,1)S(1)}, u32[]{:S(2)}, u32[]{:S(2)}) collective-permute-start(bf16[2,96,1152]{2,1,0:T(8,128)(2,1)S(1)} %add_convert_fusion.14), channel_id=1, source_target_pairs={{0,1},{1,0},{2,3},{3,2},{4,5},{5,4},{6,7},{7,6},{8,9},{9,8},{10,11... | collective-permute-start | bytes 1327112 | tf_op jit(solution)/shard_map/ppermute | solution.py:69
  339.4 13.8 %collective-permute-start.33 = (bf16[16,3456]{1,0:T(8,128)(2,1)S(1)}, bf16[16,3456]{1,0:T(8,128)(2,1)S(1)}, u32[]{:S(2)}, u32[]{:S(2)}) collective-permute-start(bf16[16,3456]{1,0:T(8,128)(2,1)S(1)} %broadcast_select_fusion), channel_id=1, source_target_pairs={{0,1},{1,0},{2,3},{3,2},{4,5},{5,4},{6,7},{7,6},{8,9},{9,8},{10,11... | collective-permute-start | bytes 331784 | tf_op jit(solution)/shard_map/ppermute | solution.py:69
  341.0 38.4 %collective-permute-start.54 = (bf16[2,96,1152]{2,1,0:T(8,128)(2,1)S(1)}, bf16[2,96,1152]{2,1,0:T(8,128)(2,1)S(1)}, u32[]{:S(2)}, u32[]{:S(2)}) collective-permute-start(bf16[2,96,1152]{2,1,0:T(8,128)(2,1)S(1)} %add_convert_fusion.11), channel_id=1, source_target_pairs={{0,4},{2,6},{4,0},{6,2},{8,12},{10,14},{12,8},{14,10},{16,20},{18,... | collective-permute-start | bytes 1327112 | tf_op jit(solution)/shard_map/ppermute | solution.py:70
  358.8 17.6 %collective-permute-start.34 = (bf16[8,1152]{1,0:T(8,128)(2,1)S(1)}, bf16[8,1152]{1,0:T(8,128)(2,1)S(1)}, u32[]{:S(2)}, u32[]{:S(2)}) collective-permute-start(bf16[8,1152]{1,0:T(8,128)(2,1)S(1)} %select_convert_fusion), channel_id=1, source_target_pairs={{0,1},{1,0},{2,3},{3,2},{4,5},{5,4},{6,7},{7,6},{8,9},{9,8},{10,11... | collective-permute-start | bytes 55304 | tf_op jit(solution)/shard_map/ppermute | solution.py:69
  360.7 21.2 %collective-permute-start.56 = (bf16[2,96,1152]{2,1,0:T(8,128)(2,1)S(1)}, bf16[2,96,1152]{2,1,0:T(8,128)(2,1)S(1)}, u32[]{:S(2)}, u32[]{:S(2)}) collective-permute-start(bf16[2,96,1152]{2,1,0:T(8,128)(2,1)S(1)} %add_convert_fusion.8), channel_id=1, source_target_pairs={{0,8},{2,10},{4,12},{6,14},{8,0},{10,2},{12,4},{14,6},{16,24},{18,... | collective-permute-start | bytes 1327112 | tf_op jit(solution)/shard_map/ppermute | solution.py:70
  374.8 41.1 %collective-permute-start.41 = (bf16[1,384,1152]{2,1,0:T(8,128)(2,1)S(1)}, bf16[1,384,1152]{2,1,0:T(8,128)(2,1)S(1)}, u32[]{:S(2)}, u32[]{:S(2)}) collective-permute-start(bf16[1,384,1152]{2,1,0:T(8,128)(2,1)S(1)} %get-tuple-element.103), channel_id=1, source_target_pairs={{0,8},{2,10},{4,12},{6,14},{8,0},{10,2},{12,4},{14,6},{16,24},{18,... | collective-permute-start | bytes 2654216 | tf_op jit(solution)/shard_map/ppermute | solution.py:70
  376.4 40.4 %collective-permute-start.44 = (bf16[1,384,1152]{2,1,0:T(8,128)(2,1)S(1)}, bf16[1,384,1152]{2,1,0:T(8,128)(2,1)S(1)}, u32[]{:S(2)}, u32[]{:S(2)}) collective-permute-start(bf16[1,384,1152]{2,1,0:T(8,128)(2,1)S(1)} %get-tuple-element.105), channel_id=1, source_target_pairs={{0,1},{1,0},{2,3},{3,2},{4,5},{5,4},{6,7},{7,6},{8,9},{9,8},{10,11... | collective-permute-start | bytes 2654216 | tf_op jit(solution)/shard_map/ppermute | solution.py:69
  377.4 41.1 %collective-permute-start.47 = (bf16[1,384,1152]{2,1,0:T(8,128)(2,1)S(1)}, bf16[1,384,1152]{2,1,0:T(8,128)(2,1)S(1)}, u32[]{:S(2)}, u32[]{:S(2)}) collective-permute-start(bf16[1,384,1152]{2,1,0:T(8,128)(2,1)S(1)} %get-tuple-element.107), channel_id=1, source_target_pairs={{0,4},{2,6},{4,0},{6,2},{8,12},{10,14},{12,8},{14,10},{16,20},{18,... | collective-permute-start | bytes 2654216 | tf_op jit(solution)/shard_map/ppermute | solution.py:70
  379.5 18.9 %collective-permute-start.35 = (bf16[16,3456]{1,0:T(8,128)(2,1)S(1)}, bf16[16,3456]{1,0:T(8,128)(2,1)S(1)}, u32[]{:S(2)}, u32[]{:S(2)}) collective-permute-start(bf16[16,3456]{1,0:T(8,128)(2,1)S(1)} %get-tuple-element.116), channel_id=1, source_target_pairs={{0,4},{2,6},{4,0},{6,2},{8,12},{10,14},{12,8},{14,10},{16,20},{18,... | collective-permute-start | bytes 331784 | tf_op jit(solution)/shard_map/ppermute | solution.py:70
  382.3 37.2 %collective-permute-start.57 = (bf16[2,144,1152]{2,1,0:T(8,128)(2,1)S(1)}, bf16[2,144,1152]{2,1,0:T(8,128)(2,1)S(1)}, u32[]{:S(2)}, u32[]{:S(2)}) collective-permute-start(bf16[2,144,1152]{2,1,0:T(8,128)(2,1)S(1)} %slice.444), channel_id=1, source_target_pairs={{0,16},{2,18},{4,20},{6,22},{8,24},{10,26},{12,28},{14,30},{16,0},... | collective-permute-start | bytes 1990664 | tf_op jit(solution)/shard_map/ppermute | solution.py:70
  398.4 14.6 %collective-permute-start.36 = (bf16[32,3456]{1,0:T(8,128)(2,1)S(1)}, bf16[32,3456]{1,0:T(8,128)(2,1)S(1)}, u32[]{:S(2)}, u32[]{:S(2)}) collective-permute-start(bf16[32,3456]{1,0:T(8,128)(2,1)S(1)} %pad_maximum_fusion.18), channel_id=1, source_target_pairs={{0,8},{2,10},{4,12},{6,14},{8,0},{10,2},{12,4},{14,6},{16,24},{18,... | collective-permute-start | bytes 663560 | tf_op jit(solution)/shard_map/ppermute | solution.py:70
  413.0 19.3 %collective-permute-start.37 = (bf16[64,3456]{1,0:T(8,128)(2,1)S(1)}, bf16[64,3456]{1,0:T(8,128)(2,1)S(1)}, u32[]{:S(2)}, u32[]{:S(2)}) collective-permute-start(bf16[64,3456]{1,0:T(8,128)(2,1)S(1)} %pad_maximum_fusion.17), channel_id=1, source_target_pairs={{0,16},{2,18},{4,20},{6,22},{8,24},{10,26},{12,28},{14,30},{16,0},... | collective-permute-start | bytes 1327112 | tf_op jit(solution)/shard_map/ppermute | solution.py:70
  416.2 16.2 %collective-permute-start.42 = (bf16[1,192,1152]{2,1,0:T(8,128)(2,1)S(1)}, bf16[1,192,1152]{2,1,0:T(8,128)(2,1)S(1)}, u32[]{:S(2)}, u32[]{:S(2)}) collective-permute-start(bf16[1,192,1152]{2,1,0:T(8,128)(2,1)S(1)} %get-tuple-element.126), channel_id=1, source_target_pairs={{0,4},{2,6},{4,0},{6,2},{8,12},{10,14},{12,8},{14,10},{16,20},{18,... | collective-permute-start | bytes 1327112 | tf_op jit(solution)/shard_map/ppermute | solution.py:70
  417.1 17.2 %collective-permute-start.45 = (bf16[1,192,1152]{2,1,0:T(8,128)(2,1)S(1)}, bf16[1,192,1152]{2,1,0:T(8,128)(2,1)S(1)}, u32[]{:S(2)}, u32[]{:S(2)}) collective-permute-start(bf16[1,192,1152]{2,1,0:T(8,128)(2,1)S(1)} %get-tuple-element.128), channel_id=1, source_target_pairs={{0,8},{2,10},{4,12},{6,14},{8,0},{10,2},{12,4},{14,6},{16,24},{18,... | collective-permute-start | bytes 1327112 | tf_op jit(solution)/shard_map/ppermute | solution.py:70
  418.7 16.1 %collective-permute-start.48 = (bf16[1,192,1152]{2,1,0:T(8,128)(2,1)S(1)}, bf16[1,192,1152]{2,1,0:T(8,128)(2,1)S(1)}, u32[]{:S(2)}, u32[]{:S(2)}) collective-permute-start(bf16[1,192,1152]{2,1,0:T(8,128)(2,1)S(1)} %get-tuple-element.130), channel_id=1, source_target_pairs={{0,1},{1,0},{2,3},{3,2},{4,5},{5,4},{6,7},{7,6},{8,9},{9,8},{10,11... | collective-permute-start | bytes 1327112 | tf_op jit(solution)/shard_map/ppermute | solution.py:69
  432.3 27.8 %collective-permute-start.38 = (bf16[128,3456]{1,0:T(8,128)(2,1)S(1)}, bf16[128,3456]{1,0:T(8,128)(2,1)S(1)}, u32[]{:S(2)}, u32[]{:S(2)}) collective-permute-start(bf16[128,3456]{1,0:T(8,128)(2,1)S(1)} %pad_maximum_fusion.10), channel_id=1, source_target_pairs={{0,2},{2,0},{4,6},{6,4},{8,10},{10,8},{12,14},{14,12},{16,18},{18,... | collective-permute-start | bytes 2654216 | tf_op jit(solution)/shard_map/ppermute | solution.py:70
  432.5 7.9 %collective-permute-start.43 = (bf16[1,96,1152]{2,1,0:T(8,128)(2,1)S(1)}, bf16[1,96,1152]{2,1,0:T(8,128)(2,1)S(1)}, u32[]{:S(2)}, u32[]{:S(2)}) collective-permute-start(bf16[1,96,1152]{2,1,0:T(8,128)(2,1)S(1)} %add_convert_fusion.29), channel_id=1, source_target_pairs={{0,1},{1,0},{2,3},{3,2},{4,5},{5,4},{6,7},{7,6},{8,9},{9,8},{10,11... | collective-permute-start | bytes 663560 | tf_op jit(solution)/shard_map/ppermute | solution.py:69
  434.3 7.6 %collective-permute-start.46 = (bf16[1,96,1152]{2,1,0:T(8,128)(2,1)S(1)}, bf16[1,96,1152]{2,1,0:T(8,128)(2,1)S(1)}, u32[]{:S(2)}, u32[]{:S(2)}) collective-permute-start(bf16[1,96,1152]{2,1,0:T(8,128)(2,1)S(1)} %add_convert_fusion.26), channel_id=1, source_target_pairs={{0,4},{2,6},{4,0},{6,2},{8,12},{10,14},{12,8},{14,10},{16,20},{18,... | collective-permute-start | bytes 663560 | tf_op jit(solution)/shard_map/ppermute | solution.py:70
  434.9 7.3 %collective-permute-start.49 = (bf16[1,96,1152]{2,1,0:T(8,128)(2,1)S(1)}, bf16[1,96,1152]{2,1,0:T(8,128)(2,1)S(1)}, u32[]{:S(2)}, u32[]{:S(2)}) collective-permute-start(bf16[1,96,1152]{2,1,0:T(8,128)(2,1)S(1)} %add_convert_fusion.23), channel_id=1, source_target_pairs={{0,8},{2,10},{4,12},{6,14},{8,0},{10,2},{12,4},{14,6},{16,24},{18,... | collective-permute-start | bytes 663560 | tf_op jit(solution)/shard_map/ppermute | solution.py:70
  442.4 16.9 %collective-permute-start.50 = (bf16[1,144,1152]{2,1,0:T(8,128)(2,1)S(1)}, bf16[1,144,1152]{2,1,0:T(8,128)(2,1)S(1)}, u32[]{:S(2)}, u32[]{:S(2)}) collective-permute-start(bf16[1,144,1152]{2,1,0:T(8,128)(2,1)S(1)} %slice.424), channel_id=1, source_target_pairs={{0,16},{2,18},{4,20},{6,22},{8,24},{10,26},{12,28},{14,30},{16,0},... | collective-permute-start | bytes 995336 | tf_op jit(solution)/shard_map/ppermute | solution.py:70
  (89 other events, 481.2 us)
